TPU v7x, 512 devices: a whole 4x8x8 slice. The times are simulated.
512 devices in a mesh: span: 16 (over y, core), cross: 32 (over x, z).
Axes of the slice: x: 4, y: 8, z: 8, core: 2. Of those that a mesh axis runs over, the one named last changes fastest.
Arguments:
- right_side: float32 [512, 1024, 128], P('span', 'cross')
- shift: float32 [512, 1024, 128], P('span', 'cross'), may hold values from 0.05 to 2
- tile_mask: int32 [16, 32], P('span', 'cross'), may hold values from 0 to 1, as said below
- owner_lists: int32 [16, 32, 12], P('span', 'cross'), may hold values from 0 to 32, as said below
- owner_ids: int32 [16, 32], P('span', 'cross'), may hold values from 0 to 31, as said below
Outputs:
- pressure: float32 [512, 1024, 128], P('span', 'cross')
- residual: float32 [512, 1024, 128], P('span', 'cross')
Inputs may be any that keep to these rules, and one draw needn't show every extreme that they name: `tile_mask`: 24 tiles of each span row are 1. `owner_lists`: each span row has 4 owners, themselves masked tiles; every masked tile stands in exactly one list, that of owner_ids, in increasing order of a drawn rank; lists of non-owners are all 32, lists are padded at the end with 32; in every span row one owner's list is full. `owner_ids`: on unmasked tiles the tile's own cross index.
All inputs are finite; a program needn't handle non-finite values.
Results may differ from a plain program's by a relative error of at most 0.000051.
Values sent between devices are 32-bit elements; how exact they have to be, the bound alone decides.
No kernel may reach another device: no remote copies, remote signals or barrier semaphores. Data moves between devices by JAX's collectives and lax.ppermute only.
A program may use at most 64 MiB of HBM per device.

v0:
```python
import jax
import jax.numpy as jnp
from jax import lax
from jax.sharding import PartitionSpec as P

LEVELS = 4
SWEEPS = 4
COARSE_SWEEPS = 4


DAMPING = 0.8


def padded_2(block, sides, width):
    for axis, dim in sides:
        count = lax.axis_size(axis)
        forward = [(i, i + 1) for i in range(count - 1)]
        backward = [(target, source) for source, target in forward]
        low = lax.ppermute(
            lax.slice_in_dim(block, block.shape[dim] - width, None, axis=dim), axis, forward
        )
        high = lax.ppermute(lax.slice_in_dim(block, 0, width, axis=dim), axis, backward)
        block = jnp.concatenate([low, block, high], axis=dim)
    return block


def strip_sweeps(strip):
    solution = jnp.zeros_like(strip)
    for sweep_index in range(COARSE_SWEEPS):
        padded = jnp.pad(solution, ((1, 1), (1, 1), (1, 1)))
        beside = padded[2:, 1:-1, 1:-1] + padded[:-2, 1:-1, 1:-1]
        beside = beside + padded[1:-1, 2:, 1:-1] + padded[1:-1, :-2, 1:-1]
        beside = beside + padded[1:-1, 1:-1, 2:] + padded[1:-1, 1:-1, :-2]
        solution = solution + DAMPING * (strip - (6.0 * solution - beside)) / 6.0
    return solution


def on_device(right_side, shift, tile_mask, owner_lists, owner_ids):
    span_cells, cross_cells, column_cells = right_side.shape
    factor = 2**LEVELS
    scales = 6.0 + shift

    def apply_operator(values):
        padded = padded_2(values, (("span", 0), ("cross", 1)), 1)
        column = jnp.pad(values, ((0, 0), (0, 0), (1, 1)))
        beside = padded[2:, 1:-1] + padded[:-2, 1:-1]
        beside = beside + padded[1:-1, 2:] + padded[1:-1, :-2]
        beside = beside + column[:, :, 2:] + column[:, :, :-2]
        return scales * values - beside

    def smooth_all(pressure):
        for sweep_index in range(SWEEPS):
            pressure = pressure + DAMPING * (right_side - apply_operator(pressure)) / scales
        return pressure

    pressure = smooth_all(jnp.zeros_like(right_side))
    fine_residual = right_side - apply_operator(pressure)
    coarse_span = span_cells // factor
    coarse_cross = cross_cells // factor
    coarse_column = column_cells // factor
    shaped = fine_residual.reshape(coarse_span, factor, coarse_cross, factor, coarse_column, factor)
    coarse = jnp.sum(shaped, axis=(1, 3, 5)) / float(factor)
    gathered = lax.all_gather(coarse.reshape(1, -1), "cross", axis=0, tiled=True)
    tiles = lax.axis_size("cross")
    positions = jnp.arange(tiles, dtype=jnp.int32)
    mine = (positions == lax.axis_index("cross")).astype(jnp.float32)
    chosen_mask = jnp.sum(
        (owner_lists[0, 0][:, None] == positions[None, :]).astype(jnp.float32), axis=0
    )
    strip = (chosen_mask[:, None] * gathered).reshape(
        tiles, coarse_span, coarse_cross, coarse_column
    )
    strip = jnp.transpose(strip, (1, 0, 2, 3)).reshape(
        coarse_span, tiles * coarse_cross, coarse_column
    )
    solution = strip_sweeps(strip).reshape(coarse_span, tiles, coarse_cross, coarse_column)
    own_solution = jnp.transpose(solution, (1, 0, 2, 3)).reshape(tiles, -1)
    every_solution = lax.all_gather(own_solution[None], "cross", axis=0, tiled=True)
    select = (owner_ids[0, 0] == positions).astype(jnp.float32)
    owner_row = jnp.sum(select[:, None, None] * every_solution, axis=0)
    tile_block = jnp.sum(mine[:, None] * owner_row, axis=0)
    correction = tile_block.reshape(coarse_span, coarse_cross, coarse_column) * tile_mask[
        0, 0
    ].astype(jnp.float32)
    expanded = jnp.broadcast_to(correction[:, None, :, None, :, None], shaped.shape)
    pressure = pressure + expanded.reshape(right_side.shape)
    pressure = smooth_all(pressure)
    residual = right_side - apply_operator(pressure)
    return (pressure, residual)


def solution(mesh):
    return jax.shard_map(
        on_device,
        mesh=mesh,
        in_specs=(
            P("span", "cross", None),
            P("span", "cross", None),
            P("span", "cross"),
            P("span", "cross", None),
            P("span", "cross"),
        ),
        out_specs=(P("span", "cross", None), P("span", "cross", None)),
        check_vma=False,
    )
```

profile of v0, /device:TPU:34, one launch (start us, length us, event | category | flops | bytes accessed | tf_op | source)
XLA Modules:
  0.0 294.5 jit_solution(18228920963747837235)
XLA Ops:
  5.1 3.8 %collective-permute-done.1 = f32[1,32,128]{2,1,0:T(8,128)S(1)} collective-permute-done((f32[1,32,128]{2,1,0:T(8,128)S(1)}, f32[1,32,128]{2,1,0:T(8,128)S(1)}, u32[]{:S(2)}, u32[]{:S(2)}) %collective-permute-start.1) | collective-permute-done | bytes 16416 | tf_op jit(solution)/shard_map/ppermute | solution.py:19
  9.1 10.9 %collective-permute-start.2 = (f32[34,1,128]{2,1,0:T(1,128)S(1)}, f32[34,1,128]{2,1,0:T(1,128)S(1)}, u32[]{:S(2)}, u32[]{:S(2)}) collective-permute-start(f32[34,1,128]{2,1,0:T(1,128)S(1)} %get-tuple-element.20), channel_id=1, source_target_pairs={{1,0},{2,1},{3,2},{4,3},{5,4},{6,5},{7,6},{8,7},{9,8},{10,9},{11,1... | collective-permute-start | bytes 52232 | tf_op jit(solution)/shard_map/ppermute | solution.py:22
  22.0 5.8 %collective-permute-done.3 = f32[34,1,128]{2,1,0:T(1,128)S(1)} collective-permute-done((f32[34,1,128]{2,1,0:T(1,128)S(1)}, f32[34,1,128]{2,1,0:T(1,128)S(1)}, u32[]{:S(2)}, u32[]{:S(2)}) %collective-permute-start.3) | collective-permute-done | bytes 17440 | tf_op jit(solution)/shard_map/ppermute | solution.py:19
  33.7 3.8 %collective-permute-done.5 = f32[1,32,128]{2,1,0:T(8,128)S(1)} collective-permute-done((f32[1,32,128]{2,1,0:T(8,128)S(1)}, f32[1,32,128]{2,1,0:T(8,128)S(1)}, u32[]{:S(2)}, u32[]{:S(2)}) %collective-permute-start.5) | collective-permute-done | bytes 16416 | tf_op jit(solution)/shard_map/ppermute | solution.py:19
  39.5 3.9 %collective-permute-start.7 = (f32[34,1,128]{2,1,0:T(1,128)S(1)}, f32[34,1,128]{2,1,0:T(1,128)S(1)}, u32[]{:S(2)}, u32[]{:S(2)}) collective-permute-start(f32[34,1,128]{2,1,0:T(1,128)S(1)} %get-tuple-element.19), channel_id=1, source_target_pairs={{0,1},{1,2},{2,3},{3,4},{4,5},{5,6},{6,7},{7,8},{8,9},{9,10},{10,1... | collective-permute-start | bytes 52232 | tf_op jit(solution)/shard_map/ppermute | solution.py:19
  43.5 3.8 %collective-permute-done.7 = f32[34,1,128]{2,1,0:T(1,128)S(1)} collective-permute-done((f32[34,1,128]{2,1,0:T(1,128)S(1)}, f32[34,1,128]{2,1,0:T(1,128)S(1)}, u32[]{:S(2)}, u32[]{:S(2)}) %collective-permute-start.7) | collective-permute-done | bytes 17440 | tf_op jit(solution)/shard_map/ppermute | solution.py:19
  52.1 3.8 %collective-permute-done.9 = f32[1,32,128]{2,1,0:T(8,128)S(1)} collective-permute-done((f32[1,32,128]{2,1,0:T(8,128)S(1)}, f32[1,32,128]{2,1,0:T(8,128)S(1)}, u32[]{:S(2)}, u32[]{:S(2)}) %collective-permute-start.9) | collective-permute-done | bytes 16416 | tf_op jit(solution)/shard_map/ppermute | solution.py:19
  57.9 3.9 %collective-permute-start.11 = (f32[34,1,128]{2,1,0:T(1,128)S(1)}, f32[34,1,128]{2,1,0:T(1,128)S(1)}, u32[]{:S(2)}, u32[]{:S(2)}) collective-permute-start(f32[34,1,128]{2,1,0:T(1,128)S(1)} %get-tuple-element.17), channel_id=1, source_target_pairs={{0,1},{1,2},{2,3},{3,4},{4,5},{5,6},{6,7},{7,8},{8,9},{9,10},{10,1... | collective-permute-start | bytes 52232 | tf_op jit(solution)/shard_map/ppermute | solution.py:19
  61.8 3.8 %collective-permute-done.11 = f32[34,1,128]{2,1,0:T(1,128)S(1)} collective-permute-done((f32[34,1,128]{2,1,0:T(1,128)S(1)}, f32[34,1,128]{2,1,0:T(1,128)S(1)}, u32[]{:S(2)}, u32[]{:S(2)}) %collective-permute-start.11) | collective-permute-done | bytes 17440 | tf_op jit(solution)/shard_map/ppermute | solution.py:19
  70.5 3.8 %collective-permute-done.13 = f32[1,32,128]{2,1,0:T(8,128)S(1)} collective-permute-done((f32[1,32,128]{2,1,0:T(8,128)S(1)}, f32[1,32,128]{2,1,0:T(8,128)S(1)}, u32[]{:S(2)}, u32[]{:S(2)}) %collective-permute-start.13) | collective-permute-done | bytes 16416 | tf_op jit(solution)/shard_map/ppermute | solution.py:19
  76.3 3.9 %collective-permute-start.15 = (f32[34,1,128]{2,1,0:T(1,128)S(1)}, f32[34,1,128]{2,1,0:T(1,128)S(1)}, u32[]{:S(2)}, u32[]{:S(2)}) collective-permute-start(f32[34,1,128]{2,1,0:T(1,128)S(1)} %get-tuple-element.15), channel_id=1, source_target_pairs={{0,1},{1,2},{2,3},{3,4},{4,5},{5,6},{6,7},{7,8},{8,9},{9,10},{10,1... | collective-permute-start | bytes 52232 | tf_op jit(solution)/shard_map/ppermute | solution.py:19
  88.8 3.8 %collective-permute-done.17 = f32[1,32,128]{2,1,0:T(8,128)S(1)} collective-permute-done((f32[1,32,128]{2,1,0:T(8,128)S(1)}, f32[1,32,128]{2,1,0:T(8,128)S(1)}, u32[]{:S(2)}, u32[]{:S(2)}) %collective-permute-start.17) | collective-permute-done | bytes 16416 | tf_op jit(solution)/shard_map/ppermute | solution.py:19
  94.6 3.9 %collective-permute-start.19 = (f32[34,1,128]{2,1,0:T(1,128)S(1)}, f32[34,1,128]{2,1,0:T(1,128)S(1)}, u32[]{:S(2)}, u32[]{:S(2)}) collective-permute-start(f32[34,1,128]{2,1,0:T(1,128)S(1)} %get-tuple-element.13), channel_id=1, source_target_pairs={{0,1},{1,2},{2,3},{3,4},{4,5},{5,6},{6,7},{7,8},{8,9},{9,10},{10,1... | collective-permute-start | bytes 52232 | tf_op jit(solution)/shard_map/ppermute | solution.py:19
  99.2 3.2 %collective-permute-done.19 = f32[34,1,128]{2,1,0:T(1,128)S(1)} collective-permute-done((f32[34,1,128]{2,1,0:T(1,128)S(1)}, f32[34,1,128]{2,1,0:T(1,128)S(1)}, u32[]{:S(2)}, u32[]{:S(2)}) %collective-permute-start.19) | collective-permute-done | bytes 17440 | tf_op jit(solution)/shard_map/ppermute | solution.py:19
  108.1 36.9 %all-gather = f32[32,1,32]{2,1,0:T(1,128)S(1)} all-gather(f32[1,1,32]{2,1,0:T(1,128)S(1)} %reshape.58), channel_id=1, replica_groups=mesh['span'=16,'cross'=32] {'cross'}, dimensions={0}, use_global_device_ids=true | all-gather | bytes 4224 | tf_op jit(solution)/shard_map/all_gather | solution.py:63
  145.8 47.6 %all_gather.7 = f32[32,32,32]{2,1,0:T(8,128)S(1)} all-gather(f32[1,32,32]{2,1,0:T(8,128)S(1)} %copy.18), channel_id=1, replica_groups=mesh['span'=16,'cross'=32] {'cross'}, dimensions={0}, use_global_device_ids=true | all-gather | bytes 135168 | tf_op jit(solution)/shard_map/all_gather | solution.py:78
  196.2 3.2 %reshape.57 = f32[32,32,128]{2,1,0:T(8,128)S(1)} reshape(f32[2,16,2,16,8,16]{5,4,3,2,1,0:T(8,128)} %broadcast_in_dim.5) | data formatting | bytes 1048576 | tf_op jit(solution)/shard_map/reshape | solution.py:86
  203.9 3.8 %collective-permute-done.21 = f32[1,32,128]{2,1,0:T(8,128)S(1)} collective-permute-done((f32[1,32,128]{2,1,0:T(8,128)S(1)}, f32[1,32,128]{2,1,0:T(8,128)S(1)}, u32[]{:S(2)}, u32[]{:S(2)}) %collective-permute-start.21) | collective-permute-done | bytes 16416 | tf_op jit(solution)/shard_map/ppermute | solution.py:19
  207.8 4.3 %collective-permute-start.22 = (f32[34,1,128]{2,1,0:T(1,128)S(1)}, f32[34,1,128]{2,1,0:T(1,128)S(1)}, u32[]{:S(2)}, u32[]{:S(2)}) collective-permute-start(f32[34,1,128]{2,1,0:T(1,128)S(1)} %get-tuple-element.10), channel_id=1, source_target_pairs={{1,0},{2,1},{3,2},{4,3},{5,4},{6,5},{7,6},{8,7},{9,8},{10,9},{11,1... | collective-permute-start | bytes 52232 | tf_op jit(solution)/shard_map/ppermute | solution.py:22
  214.1 5.8 %collective-permute-done.23 = f32[34,1,128]{2,1,0:T(1,128)S(1)} collective-permute-done((f32[34,1,128]{2,1,0:T(1,128)S(1)}, f32[34,1,128]{2,1,0:T(1,128)S(1)}, u32[]{:S(2)}, u32[]{:S(2)}) %collective-permute-start.23) | collective-permute-done | bytes 17440 | tf_op jit(solution)/shard_map/ppermute | solution.py:19
  224.7 3.8 %collective-permute-done.25 = f32[1,32,128]{2,1,0:T(8,128)S(1)} collective-permute-done((f32[1,32,128]{2,1,0:T(8,128)S(1)}, f32[1,32,128]{2,1,0:T(8,128)S(1)}, u32[]{:S(2)}, u32[]{:S(2)}) %collective-permute-start.25) | collective-permute-done | bytes 16416 | tf_op jit(solution)/shard_map/ppermute | solution.py:19
  230.5 3.9 %collective-permute-start.27 = (f32[34,1,128]{2,1,0:T(1,128)S(1)}, f32[34,1,128]{2,1,0:T(1,128)S(1)}, u32[]{:S(2)}, u32[]{:S(2)}) collective-permute-start(f32[34,1,128]{2,1,0:T(1,128)S(1)} %get-tuple-element.9), channel_id=1, source_target_pairs={{0,1},{1,2},{2,3},{3,4},{4,5},{5,6},{6,7},{7,8},{8,9},{9,10},{10,1... | collective-permute-start | bytes 52232 | tf_op jit(solution)/shard_map/ppermute | solution.py:19
  234.4 3.8 %collective-permute-done.27 = f32[34,1,128]{2,1,0:T(1,128)S(1)} collective-permute-done((f32[34,1,128]{2,1,0:T(1,128)S(1)}, f32[34,1,128]{2,1,0:T(1,128)S(1)}, u32[]{:S(2)}, u32[]{:S(2)}) %collective-permute-start.27) | collective-permute-done | bytes 17440 | tf_op jit(solution)/shard_map/ppermute | solution.py:19
  243.1 3.8 %collective-permute-done.29 = f32[1,32,128]{2,1,0:T(8,128)S(1)} collective-permute-done((f32[1,32,128]{2,1,0:T(8,128)S(1)}, f32[1,32,128]{2,1,0:T(8,128)S(1)}, u32[]{:S(2)}, u32[]{:S(2)}) %collective-permute-start.29) | collective-permute-done | bytes 16416 | tf_op jit(solution)/shard_map/ppermute | solution.py:19
  248.9 3.9 %collective-permute-start.31 = (f32[34,1,128]{2,1,0:T(1,128)S(1)}, f32[34,1,128]{2,1,0:T(1,128)S(1)}, u32[]{:S(2)}, u32[]{:S(2)}) collective-permute-start(f32[34,1,128]{2,1,0:T(1,128)S(1)} %get-tuple-element.7), channel_id=1, source_target_pairs={{0,1},{1,2},{2,3},{3,4},{4,5},{5,6},{6,7},{7,8},{8,9},{9,10},{10,1... | collective-permute-start | bytes 52232 | tf_op jit(solution)/shard_map/ppermute | solution.py:19
  252.8 3.8 %collective-permute-done.31 = f32[34,1,128]{2,1,0:T(1,128)S(1)} collective-permute-done((f32[34,1,128]{2,1,0:T(1,128)S(1)}, f32[34,1,128]{2,1,0:T(1,128)S(1)}, u32[]{:S(2)}, u32[]{:S(2)}) %collective-permute-start.31) | collective-permute-done | bytes 17440 | tf_op jit(solution)/shard_map/ppermute | solution.py:19
  261.4 3.8 %collective-permute-done.33 = f32[1,32,128]{2,1,0:T(8,128)S(1)} collective-permute-done((f32[1,32,128]{2,1,0:T(8,128)S(1)}, f32[1,32,128]{2,1,0:T(8,128)S(1)}, u32[]{:S(2)}, u32[]{:S(2)}) %collective-permute-start.33) | collective-permute-done | bytes 16416 | tf_op jit(solution)/shard_map/ppermute | solution.py:19
  267.2 3.9 %collective-permute-start.35 = (f32[34,1,128]{2,1,0:T(1,128)S(1)}, f32[34,1,128]{2,1,0:T(1,128)S(1)}, u32[]{:S(2)}, u32[]{:S(2)}) collective-permute-start(f32[34,1,128]{2,1,0:T(1,128)S(1)} %get-tuple-element.5), channel_id=1, source_target_pairs={{0,1},{1,2},{2,3},{3,4},{4,5},{5,6},{6,7},{7,8},{8,9},{9,10},{10,1... | collective-permute-start | bytes 52232 | tf_op jit(solution)/shard_map/ppermute | solution.py:19
  271.2 3.8 %collective-permute-done.35 = f32[34,1,128]{2,1,0:T(1,128)S(1)} collective-permute-done((f32[34,1,128]{2,1,0:T(1,128)S(1)}, f32[34,1,128]{2,1,0:T(1,128)S(1)}, u32[]{:S(2)}, u32[]{:S(2)}) %collective-permute-start.35) | collective-permute-done | bytes 17440 | tf_op jit(solution)/shard_map/ppermute | solution.py:19
  279.8 3.8 %collective-permute-done.37 = f32[1,32,128]{2,1,0:T(8,128)S(1)} collective-permute-done((f32[1,32,128]{2,1,0:T(8,128)S(1)}, f32[1,32,128]{2,1,0:T(8,128)S(1)}, u32[]{:S(2)}, u32[]{:S(2)}) %collective-permute-start.37) | collective-permute-done | bytes 16416 | tf_op jit(solution)/shard_map/ppermute | solution.py:19
  285.6 3.9 %collective-permute-start.39 = (f32[34,1,128]{2,1,0:T(1,128)S(1)}, f32[34,1,128]{2,1,0:T(1,128)S(1)}, u32[]{:S(2)}, u32[]{:S(2)}) collective-permute-start(f32[34,1,128]{2,1,0:T(1,128)S(1)} %get-tuple-element.3), channel_id=1, source_target_pairs={{0,1},{1,2},{2,3},{3,4},{4,5},{5,6},{6,7},{7,8},{8,9},{9,10},{10,1... | collective-permute-start | bytes 52232 | tf_op jit(solution)/shard_map/ppermute | solution.py:19
  289.5 3.8 %collective-permute-done.39 = f32[34,1,128]{2,1,0:T(1,128)S(1)} collective-permute-done((f32[34,1,128]{2,1,0:T(1,128)S(1)}, f32[34,1,128]{2,1,0:T(1,128)S(1)}, u32[]{:S(2)}, u32[]{:S(2)}) %collective-permute-start.39) | collective-permute-done | bytes 17440 | tf_op jit(solution)/shard_map/ppermute | solution.py:19
  (114 shorter events, 81.4 us)
Async XLA Ops:
  0.7 4.5 %collective-permute-start = (f32[1,32,128]{2,1,0:T(8,128)S(1)}, f32[1,32,128]{2,1,0:T(8,128)S(1)}, u32[]{:S(2)}, u32[]{:S(2)}) collective-permute-start(f32[1,32,128]{2,1,0:T(8,128)S(1)} %broadcast.79), channel_id=1, source_target_pairs={{32,0},{64,32},{96,64},{128,96},{160,128},{192,160},{224,192},{256... | collective-permute-start | bytes 49160 | tf_op jit(solution)/shard_map/ppermute | solution.py:22
  2.7 6.3 %collective-permute-start.1 = (f32[1,32,128]{2,1,0:T(8,128)S(1)}, f32[1,32,128]{2,1,0:T(8,128)S(1)}, u32[]{:S(2)}, u32[]{:S(2)}) collective-permute-start(f32[1,32,128]{2,1,0:T(8,128)S(1)} %broadcast.79), channel_id=1, source_target_pairs={{0,32},{32,64},{64,96},{96,128},{128,160},{160,192},{192,224},{224... | collective-permute-start | bytes 49160 | tf_op jit(solution)/shard_map/ppermute | solution.py:19
  9.1 12.9 %collective-permute-start.2 = (f32[34,1,128]{2,1,0:T(1,128)S(1)}, f32[34,1,128]{2,1,0:T(1,128)S(1)}, u32[]{:S(2)}, u32[]{:S(2)}) collective-permute-start(f32[34,1,128]{2,1,0:T(1,128)S(1)} %get-tuple-element.20), channel_id=1, source_target_pairs={{1,0},{2,1},{3,2},{4,3},{5,4},{6,5},{7,6},{8,7},{9,8},{10,9},{11,1... | collective-permute-start | bytes 52232 | tf_op jit(solution)/shard_map/ppermute | solution.py:22
  20.0 7.8 %collective-permute-start.3 = (f32[34,1,128]{2,1,0:T(1,128)S(1)}, f32[34,1,128]{2,1,0:T(1,128)S(1)}, u32[]{:S(2)}, u32[]{:S(2)}) collective-permute-start(f32[34,1,128]{2,1,0:T(1,128)S(1)} %get-tuple-element.21), channel_id=1, source_target_pairs={{0,1},{1,2},{2,3},{3,4},{4,5},{5,6},{6,7},{7,8},{8,9},{9,10},{10,1... | collective-permute-start | bytes 52232 | tf_op jit(solution)/shard_map/ppermute | solution.py:19
  31.3 6.3 %collective-permute-start.5 = (f32[1,32,128]{2,1,0:T(8,128)S(1)}, f32[1,32,128]{2,1,0:T(8,128)S(1)}, u32[]{:S(2)}, u32[]{:S(2)}) collective-permute-start(f32[1,32,128]{2,1,0:T(8,128)S(1)} %get-tuple-element.38), channel_id=1, source_target_pairs={{0,32},{32,64},{64,96},{96,128},{128,160},{160,192},{192,224},{224... | collective-permute-start | bytes 49160 | tf_op jit(solution)/shard_map/ppermute | solution.py:19
  37.6 5.9 %collective-permute-start.6 = (f32[34,1,128]{2,1,0:T(1,128)S(1)}, f32[34,1,128]{2,1,0:T(1,128)S(1)}, u32[]{:S(2)}, u32[]{:S(2)}) collective-permute-start(f32[34,1,128]{2,1,0:T(1,128)S(1)} %get-tuple-element.18), channel_id=1, source_target_pairs={{1,0},{2,1},{3,2},{4,3},{5,4},{6,5},{7,6},{8,7},{9,8},{10,9},{11,1... | collective-permute-start | bytes 52232 | tf_op jit(solution)/shard_map/ppermute | solution.py:22
  39.5 7.8 %collective-permute-start.7 = (f32[34,1,128]{2,1,0:T(1,128)S(1)}, f32[34,1,128]{2,1,0:T(1,128)S(1)}, u32[]{:S(2)}, u32[]{:S(2)}) collective-permute-start(f32[34,1,128]{2,1,0:T(1,128)S(1)} %get-tuple-element.19), channel_id=1, source_target_pairs={{0,1},{1,2},{2,3},{3,4},{4,5},{5,6},{6,7},{7,8},{8,9},{9,10},{10,1... | collective-permute-start | bytes 52232 | tf_op jit(solution)/shard_map/ppermute | solution.py:19
  49.7 6.3 %collective-permute-start.9 = (f32[1,32,128]{2,1,0:T(8,128)S(1)}, f32[1,32,128]{2,1,0:T(8,128)S(1)}, u32[]{:S(2)}, u32[]{:S(2)}) collective-permute-start(f32[1,32,128]{2,1,0:T(8,128)S(1)} %get-tuple-element.36), channel_id=1, source_target_pairs={{0,32},{32,64},{64,96},{96,128},{128,160},{160,192},{192,224},{224... | collective-permute-start | bytes 49160 | tf_op jit(solution)/shard_map/ppermute | solution.py:19
  56.0 5.9 %collective-permute-start.10 = (f32[34,1,128]{2,1,0:T(1,128)S(1)}, f32[34,1,128]{2,1,0:T(1,128)S(1)}, u32[]{:S(2)}, u32[]{:S(2)}) collective-permute-start(f32[34,1,128]{2,1,0:T(1,128)S(1)} %get-tuple-element.16), channel_id=1, source_target_pairs={{1,0},{2,1},{3,2},{4,3},{5,4},{6,5},{7,6},{8,7},{9,8},{10,9},{11,1... | collective-permute-start | bytes 52232 | tf_op jit(solution)/shard_map/ppermute | solution.py:22
  57.9 7.8 %collective-permute-start.11 = (f32[34,1,128]{2,1,0:T(1,128)S(1)}, f32[34,1,128]{2,1,0:T(1,128)S(1)}, u32[]{:S(2)}, u32[]{:S(2)}) collective-permute-start(f32[34,1,128]{2,1,0:T(1,128)S(1)} %get-tuple-element.17), channel_id=1, source_target_pairs={{0,1},{1,2},{2,3},{3,4},{4,5},{5,6},{6,7},{7,8},{8,9},{9,10},{10,1... | collective-permute-start | bytes 52232 | tf_op jit(solution)/shard_map/ppermute | solution.py:19
  68.0 6.3 %collective-permute-start.13 = (f32[1,32,128]{2,1,0:T(8,128)S(1)}, f32[1,32,128]{2,1,0:T(8,128)S(1)}, u32[]{:S(2)}, u32[]{:S(2)}) collective-permute-start(f32[1,32,128]{2,1,0:T(8,128)S(1)} %get-tuple-element.34), channel_id=1, source_target_pairs={{0,32},{32,64},{64,96},{96,128},{128,160},{160,192},{192,224},{224... | collective-permute-start | bytes 49160 | tf_op jit(solution)/shard_map/ppermute | solution.py:19
  74.3 6.6 %collective-permute-start.14 = (f32[34,1,128]{2,1,0:T(1,128)S(1)}, f32[34,1,128]{2,1,0:T(1,128)S(1)}, u32[]{:S(2)}, u32[]{:S(2)}) collective-permute-start(f32[34,1,128]{2,1,0:T(1,128)S(1)} %get-tuple-element.14), channel_id=1, source_target_pairs={{1,0},{2,1},{3,2},{4,3},{5,4},{6,5},{7,6},{8,7},{9,8},{10,9},{11,1... | collective-permute-start | bytes 52232 | tf_op jit(solution)/shard_map/ppermute | solution.py:22
  76.3 7.8 %collective-permute-start.15 = (f32[34,1,128]{2,1,0:T(1,128)S(1)}, f32[34,1,128]{2,1,0:T(1,128)S(1)}, u32[]{:S(2)}, u32[]{:S(2)}) collective-permute-start(f32[34,1,128]{2,1,0:T(1,128)S(1)} %get-tuple-element.15), channel_id=1, source_target_pairs={{0,1},{1,2},{2,3},{3,4},{4,5},{5,6},{6,7},{7,8},{8,9},{9,10},{10,1... | collective-permute-start | bytes 52232 | tf_op jit(solution)/shard_map/ppermute | solution.py:19
  84.5 4.4 %collective-permute-start.16 = (f32[1,32,128]{2,1,0:T(8,128)S(1)}, f32[1,32,128]{2,1,0:T(8,128)S(1)}, u32[]{:S(2)}, u32[]{:S(2)}) collective-permute-start(f32[1,32,128]{2,1,0:T(8,128)S(1)} %get-tuple-element.33), channel_id=1, source_target_pairs={{32,0},{64,32},{96,64},{128,96},{160,128},{192,160},{224,192},{256... | collective-permute-start | bytes 49160 | tf_op jit(solution)/shard_map/ppermute | solution.py:22
  86.4 6.3 %collective-permute-start.17 = (f32[1,32,128]{2,1,0:T(8,128)S(1)}, f32[1,32,128]{2,1,0:T(8,128)S(1)}, u32[]{:S(2)}, u32[]{:S(2)}) collective-permute-start(f32[1,32,128]{2,1,0:T(8,128)S(1)} %get-tuple-element.32), channel_id=1, source_target_pairs={{0,32},{32,64},{64,96},{96,128},{128,160},{160,192},{192,224},{224... | collective-permute-start | bytes 49160 | tf_op jit(solution)/shard_map/ppermute | solution.py:19
  92.7 6.5 %collective-permute-start.18 = (f32[34,1,128]{2,1,0:T(1,128)S(1)}, f32[34,1,128]{2,1,0:T(1,128)S(1)}, u32[]{:S(2)}, u32[]{:S(2)}) collective-permute-start(f32[34,1,128]{2,1,0:T(1,128)S(1)} %get-tuple-element.12), channel_id=1, source_target_pairs={{1,0},{2,1},{3,2},{4,3},{5,4},{6,5},{7,6},{8,7},{9,8},{10,9},{11,1... | collective-permute-start | bytes 52232 | tf_op jit(solution)/shard_map/ppermute | solution.py:22
  94.6 7.8 %collective-permute-start.19 = (f32[34,1,128]{2,1,0:T(1,128)S(1)}, f32[34,1,128]{2,1,0:T(1,128)S(1)}, u32[]{:S(2)}, u32[]{:S(2)}) collective-permute-start(f32[34,1,128]{2,1,0:T(1,128)S(1)} %get-tuple-element.13), channel_id=1, source_target_pairs={{0,1},{1,2},{2,3},{3,4},{4,5},{5,6},{6,7},{7,8},{8,9},{9,10},{10,1... | collective-permute-start | bytes 52232 | tf_op jit(solution)/shard_map/ppermute | solution.py:19
  201.5 6.3 %collective-permute-start.21 = (f32[1,32,128]{2,1,0:T(8,128)S(1)}, f32[1,32,128]{2,1,0:T(8,128)S(1)}, u32[]{:S(2)}, u32[]{:S(2)}) collective-permute-start(f32[1,32,128]{2,1,0:T(8,128)S(1)} %get-tuple-element.30), channel_id=1, source_target_pairs={{0,32},{32,64},{64,96},{96,128},{128,160},{160,192},{192,224},{224... | collective-permute-start | bytes 49160 | tf_op jit(solution)/shard_map/ppermute | solution.py:19
  207.8 6.3 %collective-permute-start.22 = (f32[34,1,128]{2,1,0:T(1,128)S(1)}, f32[34,1,128]{2,1,0:T(1,128)S(1)}, u32[]{:S(2)}, u32[]{:S(2)}) collective-permute-start(f32[34,1,128]{2,1,0:T(1,128)S(1)} %get-tuple-element.10), channel_id=1, source_target_pairs={{1,0},{2,1},{3,2},{4,3},{5,4},{6,5},{7,6},{8,7},{9,8},{10,9},{11,1... | collective-permute-start | bytes 52232 | tf_op jit(solution)/shard_map/ppermute | solution.py:22
  212.1 7.8 %collective-permute-start.23 = (f32[34,1,128]{2,1,0:T(1,128)S(1)}, f32[34,1,128]{2,1,0:T(1,128)S(1)}, u32[]{:S(2)}, u32[]{:S(2)}) collective-permute-start(f32[34,1,128]{2,1,0:T(1,128)S(1)} %get-tuple-element.11), channel_id=1, source_target_pairs={{0,1},{1,2},{2,3},{3,4},{4,5},{5,6},{6,7},{7,8},{8,9},{9,10},{10,1... | collective-permute-start | bytes 52232 | tf_op jit(solution)/shard_map/ppermute | solution.py:19
  222.3 6.3 %collective-permute-start.25 = (f32[1,32,128]{2,1,0:T(8,128)S(1)}, f32[1,32,128]{2,1,0:T(8,128)S(1)}, u32[]{:S(2)}, u32[]{:S(2)}) collective-permute-start(f32[1,32,128]{2,1,0:T(8,128)S(1)} %get-tuple-element.28), channel_id=1, source_target_pairs={{0,32},{32,64},{64,96},{96,128},{128,160},{160,192},{192,224},{224... | collective-permute-start | bytes 49160 | tf_op jit(solution)/shard_map/ppermute | solution.py:19
  228.6 5.9 %collective-permute-start.26 = (f32[34,1,128]{2,1,0:T(1,128)S(1)}, f32[34,1,128]{2,1,0:T(1,128)S(1)}, u32[]{:S(2)}, u32[]{:S(2)}) collective-permute-start(f32[34,1,128]{2,1,0:T(1,128)S(1)} %get-tuple-element.8), channel_id=1, source_target_pairs={{1,0},{2,1},{3,2},{4,3},{5,4},{6,5},{7,6},{8,7},{9,8},{10,9},{11,1... | collective-permute-start | bytes 52232 | tf_op jit(solution)/shard_map/ppermute | solution.py:22
  230.5 7.8 %collective-permute-start.27 = (f32[34,1,128]{2,1,0:T(1,128)S(1)}, f32[34,1,128]{2,1,0:T(1,128)S(1)}, u32[]{:S(2)}, u32[]{:S(2)}) collective-permute-start(f32[34,1,128]{2,1,0:T(1,128)S(1)} %get-tuple-element.9), channel_id=1, source_target_pairs={{0,1},{1,2},{2,3},{3,4},{4,5},{5,6},{6,7},{7,8},{8,9},{9,10},{10,1... | collective-permute-start | bytes 52232 | tf_op jit(solution)/shard_map/ppermute | solution.py:19
  240.6 6.3 %collective-permute-start.29 = (f32[1,32,128]{2,1,0:T(8,128)S(1)}, f32[1,32,128]{2,1,0:T(8,128)S(1)}, u32[]{:S(2)}, u32[]{:S(2)}) collective-permute-start(f32[1,32,128]{2,1,0:T(8,128)S(1)} %get-tuple-element.26), channel_id=1, source_target_pairs={{0,32},{32,64},{64,96},{96,128},{128,160},{160,192},{192,224},{224... | collective-permute-start | bytes 49160 | tf_op jit(solution)/shard_map/ppermute | solution.py:19
  246.9 5.9 %collective-permute-start.30 = (f32[34,1,128]{2,1,0:T(1,128)S(1)}, f32[34,1,128]{2,1,0:T(1,128)S(1)}, u32[]{:S(2)}, u32[]{:S(2)}) collective-permute-start(f32[34,1,128]{2,1,0:T(1,128)S(1)} %get-tuple-element.6), channel_id=1, source_target_pairs={{1,0},{2,1},{3,2},{4,3},{5,4},{6,5},{7,6},{8,7},{9,8},{10,9},{11,1... | collective-permute-start | bytes 52232 | tf_op jit(solution)/shard_map/ppermute | solution.py:22
  248.9 7.8 %collective-permute-start.31 = (f32[34,1,128]{2,1,0:T(1,128)S(1)}, f32[34,1,128]{2,1,0:T(1,128)S(1)}, u32[]{:S(2)}, u32[]{:S(2)}) collective-permute-start(f32[34,1,128]{2,1,0:T(1,128)S(1)} %get-tuple-element.7), channel_id=1, source_target_pairs={{0,1},{1,2},{2,3},{3,4},{4,5},{5,6},{6,7},{7,8},{8,9},{9,10},{10,1... | collective-permute-start | bytes 52232 | tf_op jit(solution)/shard_map/ppermute | solution.py:19
  259.0 6.3 %collective-permute-start.33 = (f32[1,32,128]{2,1,0:T(8,128)S(1)}, f32[1,32,128]{2,1,0:T(8,128)S(1)}, u32[]{:S(2)}, u32[]{:S(2)}) collective-permute-start(f32[1,32,128]{2,1,0:T(8,128)S(1)} %get-tuple-element.24), channel_id=1, source_target_pairs={{0,32},{32,64},{64,96},{96,128},{128,160},{160,192},{192,224},{224... | collective-permute-start | bytes 49160 | tf_op jit(solution)/shard_map/ppermute | solution.py:19
  265.3 5.9 %collective-permute-start.34 = (f32[34,1,128]{2,1,0:T(1,128)S(1)}, f32[34,1,128]{2,1,0:T(1,128)S(1)}, u32[]{:S(2)}, u32[]{:S(2)}) collective-permute-start(f32[34,1,128]{2,1,0:T(1,128)S(1)} %get-tuple-element.4), channel_id=1, source_target_pairs={{1,0},{2,1},{3,2},{4,3},{5,4},{6,5},{7,6},{8,7},{9,8},{10,9},{11,1... | collective-permute-start | bytes 52232 | tf_op jit(solution)/shard_map/ppermute | solution.py:22
  267.2 7.8 %collective-permute-start.35 = (f32[34,1,128]{2,1,0:T(1,128)S(1)}, f32[34,1,128]{2,1,0:T(1,128)S(1)}, u32[]{:S(2)}, u32[]{:S(2)}) collective-permute-start(f32[34,1,128]{2,1,0:T(1,128)S(1)} %get-tuple-element.5), channel_id=1, source_target_pairs={{0,1},{1,2},{2,3},{3,4},{4,5},{5,6},{6,7},{7,8},{8,9},{9,10},{10,1... | collective-permute-start | bytes 52232 | tf_op jit(solution)/shard_map/ppermute | solution.py:19
  277.4 6.3 %collective-permute-start.37 = (f32[1,32,128]{2,1,0:T(8,128)S(1)}, f32[1,32,128]{2,1,0:T(8,128)S(1)}, u32[]{:S(2)}, u32[]{:S(2)}) collective-permute-start(f32[1,32,128]{2,1,0:T(8,128)S(1)} %get-tuple-element.22), channel_id=1, source_target_pairs={{0,32},{32,64},{64,96},{96,128},{128,160},{160,192},{192,224},{224... | collective-permute-start | bytes 49160 | tf_op jit(solution)/shard_map/ppermute | solution.py:19
  283.7 5.9 %collective-permute-start.38 = (f32[34,1,128]{2,1,0:T(1,128)S(1)}, f32[34,1,128]{2,1,0:T(1,128)S(1)}, u32[]{:S(2)}, u32[]{:S(2)}) collective-permute-start(f32[34,1,128]{2,1,0:T(1,128)S(1)} %get-tuple-element.2), channel_id=1, source_target_pairs={{1,0},{2,1},{3,2},{4,3},{5,4},{6,5},{7,6},{8,7},{9,8},{10,9},{11,1... | collective-permute-start | bytes 52232 | tf_op jit(solution)/shard_map/ppermute | solution.py:22
  285.6 7.8 %collective-permute-start.39 = (f32[34,1,128]{2,1,0:T(1,128)S(1)}, f32[34,1,128]{2,1,0:T(1,128)S(1)}, u32[]{:S(2)}, u32[]{:S(2)}) collective-permute-start(f32[34,1,128]{2,1,0:T(1,128)S(1)} %get-tuple-element.3), channel_id=1, source_target_pairs={{0,1},{1,2},{2,3},{3,4},{4,5},{5,6},{6,7},{7,8},{8,9},{9,10},{10,1... | collective-permute-start | bytes 52232 | tf_op jit(solution)/shard_map/ppermute | solution.py:19
  (12 other events, 207.3 us)
where the time goes:
time: 296 us; the launch traced here: 295 us
  starting transfers between devices  109 us (37%)
  blocking collectives  84.5 us (29%)
  waiting for transfers between devices  79.2 us (27%)
  other arithmetic  9.96 us (3%)
  local copies, waits for them, and re-layouts  8.94 us (3%)
    ppermute x20, waiting for transfers between devices, padded_2(): lax.ppermute(lax.slice_in_dim(block, block.shape[dim] - width, None, axis...  79.1 us
    ppermute x20, starting transfers between devices, padded_2(): lax.ppermute(lax.slice_in_dim(block, block.shape[dim] - width, None, axis...  59.3 us
    ppermute x20, starting transfers between devices, padded_2(): lax.ppermute(lax.slice_in_dim(block, 0, width, axis=dim), axis, backward)  50 us
    all_gather x1, blocking collectives, on_device(): lax.all_gather(own_solution[None], 'cross', axis=0, tiled=True)  47.6 us
    all_gather x1, blocking collectives, on_device(): lax.all_gather(coarse.reshape(1, -1), 'cross', axis=0, tiled=True)  36.9 us
  transfers between devices with their start and end apart: 40, of which 20 were waited for; matrix products, arithmetic and copies ran while one was open for 0% of the time, Pallas kernels for 0%

commit v1 on v0

v1 whole, which is shorter than its diff:
```python
import functools

import jax
import jax.numpy as jnp
from jax import lax
from jax.experimental import pallas as pl
from jax.experimental.pallas import tpu as pltpu
from jax.sharding import PartitionSpec as P

DAMPING = 0.8
N = 32
LANES = 128
WIDE = N + 16
HALO = 4
REACH = 5
ROWS_W = N + 2 * HALO
ROWS_V = N + 2 * REACH
CUBE = 16
F32 = jnp.float32


def iota(shape, axis):
    return lax.broadcasted_iota(jnp.int32, shape, axis)


def neighbours(prev, cur, nxt):
    cells = cur.shape[0]
    lane = iota(cur.shape, 1)
    low = jnp.where(lane == 0, 0.0, pltpu.roll(cur, 1, 1))
    high = jnp.where(lane == LANES - 1, 0.0, pltpu.roll(cur, LANES - 1, 1))
    beside = pltpu.roll(cur, 1, 0) + pltpu.roll(cur, cells - 1, 0)
    return (prev + nxt) + beside + (low + high)


def sweep_rows(v_ref, w_ref, wb_ref, low, high):
    def body(r, carry):
        prev, cur = carry
        nxt = v_ref[r + 1]
        beside = neighbours(prev, cur, nxt)
        v_ref[r] = (1.0 - DAMPING) * cur + (wb_ref[r - 1] + w_ref[r - 1] * beside)
        return cur, nxt

    lax.fori_loop(low, high, body, (v_ref[low - 1], v_ref[low]), unroll=2)


def prepare_kernel(b_ref, s_ref, w_ref, wb_ref, down_ref, up_ref):
    for r in range(N):
        w = DAMPING / (6.0 + s_ref[r])
        wb = w * b_ref[r]
        w_ref[r] = w
        wb_ref[r] = wb
        if r < HALO:
            up_ref[0, r] = w
            up_ref[1, r] = wb
        if r >= N - HALO:
            down_ref[0, r - (N - HALO)] = w
            down_ref[1, r - (N - HALO)] = wb


def edges_kernel(w_ref, wb_ref, above_ref, below_ref, right_ref, left_ref):
    sub = iota((8, LANES), 0)
    for r in range(ROWS_W):
        if r < HALO:
            w, wb = above_ref.at[0, r], above_ref.at[1, r]
        elif r < HALO + N:
            w, wb = w_ref.at[r - HALO], wb_ref.at[r - HALO]
        else:
            w, wb = below_ref.at[0, r - HALO - N], below_ref.at[1, r - HALO - N]
        right_ref[r] = jnp.where(sub < 4, pltpu.roll(w[N - 8 : N], 4, 0), wb[N - 8 : N])
        left_ref[r] = jnp.where(sub < 4, w[0:8], pltpu.roll(wb[0:8], 4, 0))


def first_kernel(
    b_ref, s_ref, w_ref, wb_ref, above_ref, below_ref, from_left_ref, from_right_ref, mask_ref, id_ref,
    v_ref, ww_ref, wwb_ref, down_ref, up_ref, coarse_ref,
):
    span, cross = lax.axis_index("span"), lax.axis_index("cross")
    has_up, has_down = span > 0, span < lax.axis_size("span") - 1
    has_left, has_right = cross > 0, cross < lax.axis_size("cross") - 1
    sub = iota((8, LANES), 0)
    for r in range(ROWS_W):
        if r < HALO:
            w, wb = above_ref[0, r], above_ref[1, r]
        elif r < HALO + N:
            w, wb = w_ref[r - HALO], wb_ref[r - HALO]
        else:
            w, wb = below_ref[0, r - HALO - N], below_ref[1, r - HALO - N]
        in_left = (sub >= 4) & has_left
        in_right = (sub < 4) & has_right
        if r < HALO or r >= HALO + N:
            inside = has_up if r < HALO else has_down
            w, wb = jnp.where(inside, w, 0.0), jnp.where(inside, wb, 0.0)
            in_left, in_right = in_left & inside, in_right & inside
        left, right = from_left_ref[r], from_right_ref[r]
        wb_left = jnp.where(in_left, left, 0.0)
        wb_right = jnp.where(in_right, pltpu.roll(right, 4, 0), 0.0)
        ww_ref[r, 0:8] = jnp.where(in_left, pltpu.roll(left, 4, 0), 0.0)
        ww_ref[r, 8 : 8 + N] = w
        ww_ref[r, 8 + N :] = jnp.where(in_right, right, 0.0)
        wwb_ref[r, 0:8] = wb_left
        wwb_ref[r, 8 : 8 + N] = wb
        wwb_ref[r, 8 + N :] = wb_right
        v_ref[r + 1, 0:8] = wb_left
        v_ref[r + 1, 8 : 8 + N] = wb
        v_ref[r + 1, 8 + N :] = wb_right
    for step in range(1, 4):
        sweep_rows(v_ref, ww_ref, wwb_ref, 1 + step, ROWS_V - 1 - step)

    rows = []
    for part in range(2):
        start = REACH + part * CUBE

        def body(r, carry):
            prev, cur, total = carry
            nxt = v_ref[r + 1]
            beside = neighbours(prev, cur, nxt)[8 : 8 + N]
            own = cur[8 : 8 + N]
            fine = b_ref[r - REACH] - ((6.0 + s_ref[r - REACH]) * own - beside)
            return cur, nxt, total + fine

        zero = jnp.zeros((N, LANES), F32)
        _, _, total = lax.fori_loop(start, start + CUBE, body, (v_ref[start - 1], v_ref[start], zero), unroll=2)
        for half in range(2):
            rows.append(jnp.sum(total[half * CUBE : (half + 1) * CUBE], axis=0, keepdims=True))
    tile = jnp.zeros((8, LANES), F32)
    for i, row in enumerate(rows):
        tile = jnp.where(sub == i, row, tile)
    lane = iota((8, LANES), 1)
    for step in (1, 2, 4, 8):
        tile = tile + jnp.where((lane & step) == 0, pltpu.roll(tile, LANES - step, 1), pltpu.roll(tile, step, 1))
    tile = tile / float(CUBE)
    tile = jnp.where(sub == 4, id_ref[0, 0].astype(F32), tile)
    tile = jnp.where(sub == 5, mask_ref[0, 0].astype(F32), tile)
    coarse_ref[...] = tile
    for k in range(4):
        for q in range(4):
            down_ref[4 * k + q] = v_ref[REACH + N - 5 + k, 8 + 8 * q : 16 + 8 * q]
            up_ref[4 * k + q] = v_ref[REACH + 1 + k, 8 + 8 * q : 16 + 8 * q]
    down_ref[16] = tile
    up_ref[16] = tile


def second_edges_kernel(v_ref, above_ref, below_ref, coarse_ref, right_ref, left_ref, far_ref):
    sub = iota((8, LANES), 0)
    for k in range(17):
        a, c = REACH - 1 + k, REACH - 1 + 17 + k
        right_ref[k] = jnp.where((sub >= 3) & (sub < 7), v_ref[a, N : N + 8], pltpu.roll(v_ref[c, N : N + 8], 4, 0))
        left_ref[k] = jnp.where((sub >= 1) & (sub < 5), v_ref[a, 8:16], pltpu.roll(v_ref[c, 8:16], 4, 0))
    for k in range(3):
        right_ref[17 + k] = above_ref[4 * (k + 1) + 3]
        left_ref[17 + k] = above_ref[4 * (k + 1)]
        right_ref[20 + k] = below_ref[4 * k + 3]
        left_ref[20 + k] = below_ref[4 * k]
    for k, source in enumerate((above_ref.at[16], coarse_ref, below_ref.at[16])):
        right_ref[23 + k] = source[...]
        left_ref[23 + k] = source[...]
        far_ref[k] = source[...]


def second_kernel(
    b_ref, s_ref, v_in_ref, ww_ref, wwb_ref, above_ref, below_ref, coarse_ref, from_left_ref, from_right_ref,
    far_left_ref, far_right_ref, pressure_ref, residual_ref, v_ref, e_ref,
):
    span, cross = lax.axis_index("span"), lax.axis_index("cross")
    n_cross = lax.axis_size("cross")
    has_up, has_down = span > 0, span < lax.axis_size("span") - 1
    has_left, has_right = cross > 0, cross < n_cross - 1
    sub = iota((8, LANES), 0)
    lane = iota((8, LANES), 1)
    even = (sub & 1) == 0

    def wide(row):
        return jnp.broadcast_to(row, (8, LANES))

    scale = [
        jnp.where((cross + d >= 0) & (cross + d < n_cross), F32(DAMPING / 6.0), F32(0.0)) for d in range(-2, 3)
    ]
    middle = (above_ref.at[16], coarse_ref, below_ref.at[16])
    for rho in range(3):
        tiles = (
            far_left_ref.at[rho], from_left_ref.at[23 + rho], middle[rho], from_right_ref.at[23 + rho],
            far_right_ref.at[rho],
        )
        ids = [wide(t[4:5]) for t in tiles]
        masks = [wide(t[5:6]) for t in tiles]
        owner = jnp.where(sub < 2, ids[1], jnp.where(sub < 4, ids[2], ids[3]))
        strip = []
        for d in range(5):
            chosen = (ids[d] == owner) & (masks[d] > 0.5)
            for j in range(2):
                cells = jnp.where(even, wide(tiles[d][j : j + 1]), wide(tiles[d][2 + j : 3 + j]))
                strip.append(jnp.where(chosen, cells, 0.0))
        e = [scale[j // 2] * strip[j] for j in range(10)]
        for step in range(1, 4):
            new = list(e)
            for j in range(step, 10 - step):
                beside = e[j - 1] + e[j + 1]
                beside = beside + jnp.where(even, pltpu.roll(e[j], 7, 0), pltpu.roll(e[j], 1, 0))
                beside = beside + jnp.where(lane < CUBE, 0.0, pltpu.roll(e[j], CUBE, 1))
                beside = beside + jnp.where(lane >= LANES - CUBE, 0.0, pltpu.roll(e[j], LANES - CUBE, 1))
                new[j] = (1.0 - DAMPING) * e[j] + scale[j // 2] * (strip[j] + beside)
            e = new
        mask = jnp.where(
            sub < 2, jnp.where(has_left, masks[1], 0.0), jnp.where(sub < 4, masks[2], jnp.where(has_right, masks[3], 0.0))
        )
        if rho != 1:
            mask = jnp.where(has_up if rho == 0 else has_down, mask, 0.0)
        for j in range(3, 7):
            e_ref[rho, j - 3] = e[j] * mask

    def correction(rho, j, side, i):
        k = 2 * side + i
        return wide(e_ref[rho, j - 3, k : k + 1])

    def own(rho, i):
        first, second = correction(rho, 4, 1, i), correction(rho, 5, 1, i)
        return jnp.concatenate([first, first, second, second], axis=0)

    zero = jnp.zeros((8, LANES), F32)
    for r in range(ROWS_V):
        cell = r - REACH
        rho = 0 if cell < 0 else (1 if cell < N else 2)
        i = 1 if cell < 0 else (cell // CUBE if cell < N else 0)
        inside = (has_up, None, has_down)[rho]
        if cell < -1 or cell > N:
            source, k = (above_ref, cell + 5) if cell < 0 else (below_ref, cell - N - 1)
            for q in range(4):
                v_ref[r, 8 + 8 * q : 16 + 8 * q] = jnp.where(inside, source[4 * k + q], 0.0) + correction(
                    rho, 4 + q // 2, 1, i
                )
            if cell == -REACH or cell == N + REACH - 1:
                left, right = zero, zero
            else:
                k = 17 + cell + 4 if cell < 0 else 20 + cell - N - 1
                left = jnp.where(inside & has_left, from_left_ref[k], 0.0)
                right = jnp.where(inside & has_right, from_right_ref[k], 0.0)
        else:
            v_ref[r, 8 : 8 + N] = v_in_ref[r, 8 : 8 + N] + own(rho, i)
            k = cell + 1
            left, right = from_left_ref[k % 17], from_right_ref[k % 17]
            if k >= 17:
                left, right = pltpu.roll(left, 4, 0), pltpu.roll(right, 4, 0)
            in_left, in_right = has_left, has_right
            if rho != 1:
                in_left, in_right = in_left & inside, in_right & inside
            left = jnp.where((sub >= 3) & (sub < 7) & in_left, left, jnp.where(sub == 7, v_in_ref[r, 0:8], 0.0))
            right = jnp.where((sub >= 1) & (sub < 5) & in_right, right, jnp.where(sub == 0, v_in_ref[r, 8 + N :], 0.0))
        v_ref[r, 0:8] = left + correction(rho, 3, 0, i)
        v_ref[r, 8 + N :] = right + correction(rho, 6, 2, i)

    for step in range(4):
        sweep_rows(v_ref, ww_ref, wwb_ref, 1 + step, ROWS_V - 1 - step)

    def body(r, carry):
        prev, cur = carry
        nxt = v_ref[r + 1]
        beside = neighbours(prev, cur, nxt)[8 : 8 + N]
        mine = cur[8 : 8 + N]
        pressure_ref[r - REACH] = mine
        residual_ref[r - REACH] = b_ref[r - REACH] - ((6.0 + s_ref[r - REACH]) * mine - beside)
        return cur, nxt

    lax.fori_loop(REACH, REACH + N, body, (v_ref[REACH - 1], v_ref[REACH]), unroll=2)


def call(kernel, outs, args, scalars=0, scratch=()):
    vmem = pl.BlockSpec(memory_space=pltpu.VMEM)
    smem = pl.BlockSpec(memory_space=pltpu.SMEM)
    return pl.pallas_call(
        kernel,
        out_shape=[jax.ShapeDtypeStruct(s, F32) for s in outs],
        in_specs=[vmem] * (len(args) - scalars) + [smem] * scalars,
        out_specs=[vmem] * len(outs),
        scratch_shapes=[pltpu.VMEM(s, F32) for s in scratch],
        compiler_params=pltpu.CompilerParams(vmem_limit_bytes=32 * 1024 * 1024),
    )(*args)


def shifted(block, axis, step):
    count = lax.axis_size(axis)
    return lax.ppermute(block, axis, [(i, (i + step) % count) for i in range(count)])


def on_device(right_side, shift, tile_mask, owner_lists, owner_ids):
    block = (N, N, LANES)
    w, wb, down, up = call(
        prepare_kernel, [block, block, (2, HALO, N, LANES), (2, HALO, N, LANES)], [right_side, shift]
    )
    above = shifted(down, "span", 1)
    below = shifted(up, "span", -1)
    right, left = call(edges_kernel, [(ROWS_W, 8, LANES)] * 2, [w, wb, above, below])
    from_left = shifted(right, "cross", 1)
    from_right = shifted(left, "cross", -1)
    v, ww, wwb, down, up, coarse = call(
        first_kernel,
        [
            (ROWS_V, WIDE, LANES), (ROWS_W, WIDE, LANES), (ROWS_W, WIDE, LANES), (17, 8, LANES), (17, 8, LANES),
            (8, LANES),
        ],
        [right_side, shift, w, wb, above, below, from_left, from_right, tile_mask, owner_ids],
        scalars=2,
    )
    above = shifted(down, "span", 1)
    below = shifted(up, "span", -1)
    right, left, far = call(
        second_edges_kernel, [(26, 8, LANES), (26, 8, LANES), (3, 8, LANES)], [v, above, below, coarse]
    )
    from_left = shifted(right, "cross", 1)
    from_right = shifted(left, "cross", -1)
    far_left = shifted(far, "cross", 2)
    far_right = shifted(far, "cross", -2)
    pressure, residual = call(
        second_kernel,
        [block, block],
        [right_side, shift, v, ww, wwb, above, below, coarse, from_left, from_right, far_left, far_right],
        scratch=[(ROWS_V, WIDE, LANES), (3, 4, 8, LANES)],
    )
    return (pressure, residual)


def solution(mesh):
    return jax.shard_map(
        on_device,
        mesh=mesh,
        in_specs=(
            P("span", "cross", None),
            P("span", "cross", None),
            P("span", "cross"),
            P("span", "cross", None),
            P("span", "cross"),
        ),
        out_specs=(P("span", "cross", None), P("span", "cross", None)),
        check_vma=False,
    )
```

time: 296 us -> 73.9 us (0.25)
  the two profiles are of different devices: /device:TPU:34 before, /device:TPU:25 now
where the time goes in v1:
time: 73.9 us; the launch traced here: 73.6 us
  starting transfers between devices  35.1 us (47%)
  Pallas kernels  17.4 us (24%)
  waiting for transfers between devices  17 us (23%)
  local copies, waits for them, and re-layouts  2.09 us (3%)
  between operations  2.01 us (3%)
    ppermute x10, starting transfers between devices, shifted(): lax.ppermute(block, axis, [(i, (i + step) % count) for i in range(count)])  35.1 us
    pallas_call x5, Pallas kernels, call(): pl.pallas_call(kernel, out_shape=[jax.ShapeDtypeStruct(s, F32) for s in o...  17.4 us
    ppermute x10, waiting for transfers between devices, shifted(): lax.ppermute(block, axis, [(i, (i + step) % count) for i in range(count)])  17 us
    unnamed x8, local copies, waits for them, and re-layouts  2.09 us
  transfers between devices with their start and end apart: 10, of which 6 were waited for; matrix products, arithmetic and copies ran while one was open for 0% of the time, Pallas kernels for 0%

profile of v1, /device:TPU:25, one launch (start us, length us, event | category | flops | bytes accessed | tf_op | source)
XLA Modules:
  0.0 73.6 jit_solution(10567001885617104201)
XLA Ops:
  0.6 0.0 copy-start
  0.6 1.0 %copy-done = f32[32,32,128]{2,1,0:T(8,128)S(1)} copy-done((f32[32,32,128]{2,1,0:T(8,128)S(1)}, f32[32,32,128]{2,1,0:T(8,128)}, u32[]{:S(2)}) %copy-start) | copy-done | bytes 524312
  1.7 0.0 copy-start.2
  1.7 1.0 %copy-done.2 = f32[32,32,128]{2,1,0:T(8,128)S(1)} copy-done((f32[32,32,128]{2,1,0:T(8,128)S(1)}, f32[32,32,128]{2,1,0:T(8,128)}, u32[]{:S(2)}) %copy-start.2) | copy-done | bytes 524312
  2.7 0.1 shard_map.59
  2.8 3.1 %collective-permute-start = (f32[2,4,32,128]{3,2,1,0:T(8,128)S(1)}, f32[2,4,32,128]{3,2,1,0:T(8,128)S(1)}, u32[]{:S(2)}, u32[]{:S(2)}) collective-permute-start(f32[2,4,32,128]{3,2,1,0:T(8,128)S(1)} %get-tuple-element.19), channel_id=1, source_target_pairs={{0,32},{32,64},{64,96},{96,128},{128,160},{160,192},{192,224},{224... | collective-permute-start | bytes 393224 | tf_op jit(solution)/shard_map/ppermute | solution.py:281
  5.9 0.0 collective-permute-start.1
  5.9 1.9 %collective-permute-done.above_ref = f32[2,4,32,128]{3,2,1,0:T(8,128)S(1)} collective-permute-done((f32[2,4,32,128]{3,2,1,0:T(8,128)S(1)}, f32[2,4,32,128]{3,2,1,0:T(8,128)S(1)}, u32[]{:S(2)}, u32[]{:S(2)}) %collective-permute-start) | collective-permute-done | bytes 131104 | tf_op jit(solution)/shard_map/ppermute | solution.py:281
  7.8 3.7 %collective-permute-done.1.below_ref = f32[2,4,32,128]{3,2,1,0:T(8,128)S(1)} collective-permute-done((f32[2,4,32,128]{3,2,1,0:T(8,128)S(1)}, f32[2,4,32,128]{3,2,1,0:T(8,128)S(1)}, u32[]{:S(2)}, u32[]{:S(2)}) %collective-permute-start.1) | collective-permute-done | bytes 131104 | tf_op jit(solution)/shard_map/ppermute | solution.py:281
  11.5 0.0 copy-start.1
  11.5 0.0 copy-start.3
  11.6 4.1 %collective-permute-start.2 = (f32[40,8,128]{2,1,0:T(8,128)S(1)}, f32[40,8,128]{2,1,0:T(8,128)S(1)}, u32[]{:S(2)}, u32[]{:S(2)}) collective-permute-start(f32[40,8,128]{2,1,0:T(8,128)S(1)} %get-tuple-element.21), channel_id=1, source_target_pairs={{0,1},{1,2},{2,3},{3,4},{4,5},{5,6},{6,7},{7,8},{8,9},{9,10},{10,1... | collective-permute-start | bytes 491528 | tf_op jit(solution)/shard_map/ppermute | solution.py:281
  15.7 10.8 %collective-permute-start.3 = (f32[40,8,128]{2,1,0:T(8,128)S(1)}, f32[40,8,128]{2,1,0:T(8,128)S(1)}, u32[]{:S(2)}, u32[]{:S(2)}) collective-permute-start(f32[40,8,128]{2,1,0:T(8,128)S(1)} %get-tuple-element.22), channel_id=1, source_target_pairs={{0,31},{1,0},{2,1},{3,2},{4,3},{5,4},{6,5},{7,6},{8,7},{9,8},{10,9... | collective-permute-start | bytes 491528 | tf_op jit(solution)/shard_map/ppermute | solution.py:281
  27.8 0.0 collective-permute-done.2.from_left_ref
  27.8 0.9 %collective-permute-done.3.from_right_ref = f32[40,8,128]{2,1,0:T(8,128)S(1)} collective-permute-done((f32[40,8,128]{2,1,0:T(8,128)S(1)}, f32[40,8,128]{2,1,0:T(8,128)S(1)}, u32[]{:S(2)}, u32[]{:S(2)}) %collective-permute-start.3) | collective-permute-done | bytes 163872 | tf_op jit(solution)/shard_map/ppermute | solution.py:281
  28.7 0.0 copy-done.1
  28.7 0.0 copy-done.3
  28.7 7.2 %shard_map.61 = (f32[42,48,128]{2,1,0:T(8,128)S(1)}, f32[40,48,128]{2,1,0:T(8,128)S(1)}, f32[40,48,128]{2,1,0:T(8,128)S(1)}, f32[17,8,128]{2,1,0:T(8,128)S(1)}, ...) custom-call(f32[32,32,128]{2,1,0:T(8,128)S(1)} %copy-done.1, f32[32,32,128]{2,1,0:T(8,128)S(1)} %copy-done.3, ...), custom_call_target="tpu_custom_call" | custom-call | tf_op jit(solution)/shard_map/pallas_call | solution.py:269
  36.0 1.5 %collective-permute-start.4 = (f32[17,8,128]{2,1,0:T(8,128)S(1)}, f32[17,8,128]{2,1,0:T(8,128)S(1)}, u32[]{:S(2)}, u32[]{:S(2)}) collective-permute-start(f32[17,8,128]{2,1,0:T(8,128)S(1)} %get-tuple-element.26), channel_id=1, source_target_pairs={{0,32},{32,64},{64,96},{96,128},{128,160},{160,192},{192,224},{224... | collective-permute-start | bytes 208904 | tf_op jit(solution)/shard_map/ppermute | solution.py:281
  37.5 0.0 collective-permute-start.5
  37.5 1.4 %collective-permute-done.4.above_ref = f32[17,8,128]{2,1,0:T(8,128)S(1)} collective-permute-done((f32[17,8,128]{2,1,0:T(8,128)S(1)}, f32[17,8,128]{2,1,0:T(8,128)S(1)}, u32[]{:S(2)}, u32[]{:S(2)}) %collective-permute-start.4) | collective-permute-done | bytes 69664 | tf_op jit(solution)/shard_map/ppermute | solution.py:281
  38.9 3.6 %collective-permute-done.5.below_ref = f32[17,8,128]{2,1,0:T(8,128)S(1)} collective-permute-done((f32[17,8,128]{2,1,0:T(8,128)S(1)}, f32[17,8,128]{2,1,0:T(8,128)S(1)}, u32[]{:S(2)}, u32[]{:S(2)}) %collective-permute-start.5) | collective-permute-done | bytes 69664 | tf_op jit(solution)/shard_map/ppermute | solution.py:281
  42.5 1.9 %collective-permute-start.6 = (f32[26,8,128]{2,1,0:T(8,128)S(1)}, f32[26,8,128]{2,1,0:T(8,128)S(1)}, u32[]{:S(2)}, u32[]{:S(2)}) collective-permute-start(f32[26,8,128]{2,1,0:T(8,128)S(1)} %get-tuple-element.29), channel_id=1, source_target_pairs={{0,1},{1,2},{2,3},{3,4},{4,5},{5,6},{6,7},{7,8},{8,9},{9,10},{10,1... | collective-permute-start | bytes 319496 | tf_op jit(solution)/shard_map/ppermute | solution.py:281
  44.4 7.4 %collective-permute-start.7 = (f32[26,8,128]{2,1,0:T(8,128)S(1)}, f32[26,8,128]{2,1,0:T(8,128)S(1)}, u32[]{:S(2)}, u32[]{:S(2)}) collective-permute-start(f32[26,8,128]{2,1,0:T(8,128)S(1)} %get-tuple-element.30), channel_id=1, source_target_pairs={{0,31},{1,0},{2,1},{3,2},{4,3},{5,4},{6,5},{7,6},{8,7},{9,8},{10,9... | collective-permute-start | bytes 319496 | tf_op jit(solution)/shard_map/ppermute | solution.py:281
  51.8 3.1 %collective-permute-start.9 = (f32[3,8,128]{2,1,0:T(8,128)S(1)}, f32[3,8,128]{2,1,0:T(8,128)S(1)}, u32[]{:S(2)}, u32[]{:S(2)}) collective-permute-start(f32[3,8,128]{2,1,0:T(8,128)S(1)} %get-tuple-element.31), channel_id=1, source_target_pairs={{0,30},{1,31},{2,0},{3,1},{4,2},{5,3},{6,4},{7,5},{8,6},{9,7},{10,... | collective-permute-start | bytes 36872 | tf_op jit(solution)/shard_map/ppermute | solution.py:281
  54.9 3.1 %collective-permute-start.8 = (f32[3,8,128]{2,1,0:T(8,128)S(1)}, f32[3,8,128]{2,1,0:T(8,128)S(1)}, u32[]{:S(2)}, u32[]{:S(2)}) collective-permute-start(f32[3,8,128]{2,1,0:T(8,128)S(1)} %get-tuple-element.31), channel_id=1, source_target_pairs={{0,2},{1,3},{2,4},{3,5},{4,6},{5,7},{6,8},{7,9},{8,10},{9,11},{10,... | collective-permute-start | bytes 36872 | tf_op jit(solution)/shard_map/ppermute | solution.py:281
  58.0 0.0 collective-permute-done.9.far_right_ref
  58.0 5.5 %collective-permute-done.8.far_left_ref = f32[3,8,128]{2,1,0:T(8,128)S(1)} collective-permute-done((f32[3,8,128]{2,1,0:T(8,128)S(1)}, f32[3,8,128]{2,1,0:T(8,128)S(1)}, u32[]{:S(2)}, u32[]{:S(2)}) %collective-permute-start.8) | collective-permute-done | bytes 12320 | tf_op jit(solution)/shard_map/ppermute | solution.py:281
  63.6 0.0 collective-permute-done.6.from_left_ref
  63.6 0.0 collective-permute-done.7.from_right_ref
  63.6 10.0 %shard_map.63 = (f32[32,32,128]{2,1,0:T(8,128)}, f32[32,32,128]{2,1,0:T(8,128)}) custom-call(f32[32,32,128]{2,1,0:T(8,128)S(1)} %copy-done.1, f32[32,32,128]{2,1,0:T(8,128)S(1)} %copy-done.3, f32[42,48,128]{2,1,0:T(8,128)S(1)} %get-tuple-element.23.v_ref.v_in_ref, f32[40,48,128]{2,1,0:T(8,128)S(1)} %get-tuple-element.24.ww_ref, ...), custom_call_target="tpu_custom_call" | custom-call | tf_op jit(solution)/shard_map/pallas_call | solution.py:269
  (2 shorter events, 0.1 us)
Async XLA Ops:
  0.6 1.0 %copy-start = (f32[32,32,128]{2,1,0:T(8,128)S(1)}, f32[32,32,128]{2,1,0:T(8,128)}, u32[]{:S(2)}) copy-start(f32[32,32,128]{2,1,0:T(8,128)} %b_ref.5) | copy-start | bytes 1572868
  1.7 1.0 %copy-start.2 = (f32[32,32,128]{2,1,0:T(8,128)S(1)}, f32[32,32,128]{2,1,0:T(8,128)}, u32[]{:S(2)}) copy-start(f32[32,32,128]{2,1,0:T(8,128)} %s_ref.5) | copy-start | bytes 1572868
  2.8 5.0 %collective-permute-start = (f32[2,4,32,128]{3,2,1,0:T(8,128)S(1)}, f32[2,4,32,128]{3,2,1,0:T(8,128)S(1)}, u32[]{:S(2)}, u32[]{:S(2)}) collective-permute-start(f32[2,4,32,128]{3,2,1,0:T(8,128)S(1)} %get-tuple-element.19), channel_id=1, source_target_pairs={{0,32},{32,64},{64,96},{96,128},{128,160},{160,192},{192,224},{224... | collective-permute-start | bytes 393224 | tf_op jit(solution)/shard_map/ppermute | solution.py:281
  5.9 5.6 %collective-permute-start.1 = (f32[2,4,32,128]{3,2,1,0:T(8,128)S(1)}, f32[2,4,32,128]{3,2,1,0:T(8,128)S(1)}, u32[]{:S(2)}, u32[]{:S(2)}) collective-permute-start(f32[2,4,32,128]{3,2,1,0:T(8,128)S(1)} %get-tuple-element.20), channel_id=1, source_target_pairs={{0,480},{32,0},{64,32},{96,64},{128,96},{160,128},{192,160},{224,1... | collective-permute-start | bytes 393224 | tf_op jit(solution)/shard_map/ppermute | solution.py:281
  11.5 17.2 %copy-start.1 = (f32[32,32,128]{2,1,0:T(8,128)S(1)}, f32[32,32,128]{2,1,0:T(8,128)}, u32[]{:S(2)}) copy-start(f32[32,32,128]{2,1,0:T(8,128)} %b_ref.5) | copy-start | bytes 1572868
  11.5 17.2 %copy-start.3 = (f32[32,32,128]{2,1,0:T(8,128)S(1)}, f32[32,32,128]{2,1,0:T(8,128)}, u32[]{:S(2)}) copy-start(f32[32,32,128]{2,1,0:T(8,128)} %s_ref.5) | copy-start | bytes 1572868
  11.6 16.2 %collective-permute-start.2 = (f32[40,8,128]{2,1,0:T(8,128)S(1)}, f32[40,8,128]{2,1,0:T(8,128)S(1)}, u32[]{:S(2)}, u32[]{:S(2)}) collective-permute-start(f32[40,8,128]{2,1,0:T(8,128)S(1)} %get-tuple-element.21), channel_id=1, source_target_pairs={{0,1},{1,2},{2,3},{3,4},{4,5},{5,6},{6,7},{7,8},{8,9},{9,10},{10,1... | collective-permute-start | bytes 491528 | tf_op jit(solution)/shard_map/ppermute | solution.py:281
  15.7 13.0 %collective-permute-start.3 = (f32[40,8,128]{2,1,0:T(8,128)S(1)}, f32[40,8,128]{2,1,0:T(8,128)S(1)}, u32[]{:S(2)}, u32[]{:S(2)}) collective-permute-start(f32[40,8,128]{2,1,0:T(8,128)S(1)} %get-tuple-element.22), channel_id=1, source_target_pairs={{0,31},{1,0},{2,1},{3,2},{4,3},{5,4},{6,5},{7,6},{8,7},{9,8},{10,9... | collective-permute-start | bytes 491528 | tf_op jit(solution)/shard_map/ppermute | solution.py:281
  36.0 2.9 %collective-permute-start.4 = (f32[17,8,128]{2,1,0:T(8,128)S(1)}, f32[17,8,128]{2,1,0:T(8,128)S(1)}, u32[]{:S(2)}, u32[]{:S(2)}) collective-permute-start(f32[17,8,128]{2,1,0:T(8,128)S(1)} %get-tuple-element.26), channel_id=1, source_target_pairs={{0,32},{32,64},{64,96},{96,128},{128,160},{160,192},{192,224},{224... | collective-permute-start | bytes 208904 | tf_op jit(solution)/shard_map/ppermute | solution.py:281
  37.5 4.9 %collective-permute-start.5 = (f32[17,8,128]{2,1,0:T(8,128)S(1)}, f32[17,8,128]{2,1,0:T(8,128)S(1)}, u32[]{:S(2)}, u32[]{:S(2)}) collective-permute-start(f32[17,8,128]{2,1,0:T(8,128)S(1)} %get-tuple-element.27), channel_id=1, source_target_pairs={{0,480},{32,0},{64,32},{96,64},{128,96},{160,128},{192,160},{224,1... | collective-permute-start | bytes 208904 | tf_op jit(solution)/shard_map/ppermute | solution.py:281
  42.5 21.1 %collective-permute-start.6 = (f32[26,8,128]{2,1,0:T(8,128)S(1)}, f32[26,8,128]{2,1,0:T(8,128)S(1)}, u32[]{:S(2)}, u32[]{:S(2)}) collective-permute-start(f32[26,8,128]{2,1,0:T(8,128)S(1)} %get-tuple-element.29), channel_id=1, source_target_pairs={{0,1},{1,2},{2,3},{3,4},{4,5},{5,6},{6,7},{7,8},{8,9},{9,10},{10,1... | collective-permute-start | bytes 319496 | tf_op jit(solution)/shard_map/ppermute | solution.py:281
  44.4 19.2 %collective-permute-start.7 = (f32[26,8,128]{2,1,0:T(8,128)S(1)}, f32[26,8,128]{2,1,0:T(8,128)S(1)}, u32[]{:S(2)}, u32[]{:S(2)}) collective-permute-start(f32[26,8,128]{2,1,0:T(8,128)S(1)} %get-tuple-element.30), channel_id=1, source_target_pairs={{0,31},{1,0},{2,1},{3,2},{4,3},{5,4},{6,5},{7,6},{8,7},{9,8},{10,9... | collective-permute-start | bytes 319496 | tf_op jit(solution)/shard_map/ppermute | solution.py:281
  51.8 6.2 %collective-permute-start.9 = (f32[3,8,128]{2,1,0:T(8,128)S(1)}, f32[3,8,128]{2,1,0:T(8,128)S(1)}, u32[]{:S(2)}, u32[]{:S(2)}) collective-permute-start(f32[3,8,128]{2,1,0:T(8,128)S(1)} %get-tuple-element.31), channel_id=1, source_target_pairs={{0,30},{1,31},{2,0},{3,1},{4,2},{5,3},{6,4},{7,5},{8,6},{9,7},{10,... | collective-permute-start | bytes 36872 | tf_op jit(solution)/shard_map/ppermute | solution.py:281
  54.9 8.7 %collective-permute-start.8 = (f32[3,8,128]{2,1,0:T(8,128)S(1)}, f32[3,8,128]{2,1,0:T(8,128)S(1)}, u32[]{:S(2)}, u32[]{:S(2)}) collective-permute-start(f32[3,8,128]{2,1,0:T(8,128)S(1)} %get-tuple-element.31), channel_id=1, source_target_pairs={{0,2},{1,3},{2,4},{3,5},{4,6},{5,7},{6,8},{7,9},{8,10},{9,11},{10,... | collective-permute-start | bytes 36872 | tf_op jit(solution)/shard_map/ppermute | solution.py:281

commit v2 on v0

v2 whole, which is shorter than its diff:
```python
import math

import jax
import jax.numpy as jnp
from jax import lax
from jax.experimental import pallas as pl
from jax.experimental.pallas import tpu as pltpu
from jax.sharding import PartitionSpec as P

DAMPING = 0.8
N = 32
LANES = 128
WIDE = N + 16
HALO = 4
REACH = 5
ROWS_W = N + 2 * HALO
ROWS_V = N + 2 * REACH
CUBE = 16
F32 = jnp.float32


def iota(shape, axis):
    return lax.broadcasted_iota(jnp.int32, shape, axis)


def neighbours(prev, cur, nxt):
    cells = cur.shape[0]
    lane = iota(cur.shape, 1)
    low = jnp.where(lane == 0, 0.0, pltpu.roll(cur, 1, 1))
    high = jnp.where(lane == LANES - 1, 0.0, pltpu.roll(cur, LANES - 1, 1))
    beside = pltpu.roll(cur, 1, 0) + pltpu.roll(cur, cells - 1, 0)
    return (prev + nxt) + beside + (low + high)


def sweeps(v_ref, w_ref, wb_ref, low, high, count):
    def one(step, carry):
        prev, cur = v_ref[low - 1], v_ref[low]
        for r in range(low, high):
            nxt = v_ref[r + 1]
            beside = neighbours(prev, cur, nxt)
            v_ref[r] = (1.0 - DAMPING) * cur + (wb_ref[r - 1] + w_ref[r - 1] * beside)
            prev, cur = cur, nxt
        return carry

    lax.fori_loop(0, count, one, 0)


def edges_kernel(b_ref, s_ref, right_ref, left_ref, b_left, b_right, s_left, s_right, sems):
    copies = [
        pltpu.make_async_copy(source.at[:, pl.ds(start, 8), :], target, sems.at[n])
        for n, (source, start, target) in enumerate(
            ((s_ref, N - 8, s_right), (b_ref, N - 8, b_right), (s_ref, 0, s_left), (b_ref, 0, b_left))
        )
    ]
    for copy in copies:
        copy.start()
    sub = iota((8, LANES), 0)
    copies[0].wait()
    copies[1].wait()
    for r in range(N):
        w = DAMPING / (6.0 + s_right[r])
        right_ref[r] = jnp.where(sub < 4, pltpu.roll(w, 4, 0), w * b_right[r])
    copies[2].wait()
    copies[3].wait()
    for r in range(N):
        w = DAMPING / (6.0 + s_left[r])
        left_ref[r] = jnp.where(sub < 4, w, pltpu.roll(w * b_left[r], 4, 0))


def coefficients_kernel(b_ref, s_ref, mask_ref, id_ref, w_ref, wb_ref, info_ref):
    for r in range(N):
        w = DAMPING / (6.0 + s_ref[r])
        w_ref[r] = w
        wb_ref[r] = w * b_ref[r]
    sub = iota((8, LANES), 0)
    number = jnp.broadcast_to(id_ref[...].astype(F32), (8, LANES))
    mask = jnp.broadcast_to(mask_ref[...].astype(F32), (8, LANES))
    info_ref[...] = jnp.where(sub == 4, number, jnp.where(sub == 5, mask, 0.0))


def beside_of(left_msg, right_msg):
    sub = iota((8, LANES), 0)
    w = jnp.where(sub < 4, right_msg, pltpu.roll(left_msg, 4, 0))
    wb = jnp.where(sub < 4, pltpu.roll(right_msg, 4, 0), left_msg)
    return w, wb


def rows_kernel(w_ref, wb_ref, from_left_ref, from_right_ref, down_ref, up_ref):
    for target, start in ((up_ref, 0), (down_ref, N - HALO)):
        for k in range(HALO):
            r = start + k
            sides = beside_of(from_left_ref[r], from_right_ref[r])
            for a, ref in enumerate((w_ref, wb_ref)):
                target[a, k, 0:N] = ref[r]
                target[a, k, N:] = sides[a]


def first_kernel(
    b_ref, s_ref, w_ref, wb_ref, from_left_ref, from_right_ref, above_ref, below_ref, info_ref,
    v_ref, ww_ref, wwb_ref, right_ref, left_ref, coarse_ref,
):
    span, cross = lax.axis_index("span"), lax.axis_index("cross")
    has_up, has_down = span > 0, span < lax.axis_size("span") - 1
    has_left, has_right = cross > 0, cross < lax.axis_size("cross") - 1
    sub = iota((8, LANES), 0)
    for r in range(ROWS_W):
        in_left, in_right = (sub >= 4) & has_left, (sub < 4) & has_right
        if HALO <= r < HALO + N:
            w, wb = w_ref[r - HALO], wb_ref[r - HALO]
            w_side, wb_side = beside_of(from_left_ref[r - HALO], from_right_ref[r - HALO])
        else:
            source, k, inside = (above_ref, r, has_up) if r < HALO else (below_ref, r - HALO - N, has_down)
            w, wb = jnp.where(inside, source[0, k, 0:N], 0.0), jnp.where(inside, source[1, k, 0:N], 0.0)
            w_side, wb_side = source[0, k, N:], source[1, k, N:]
            in_left, in_right = in_left & inside, in_right & inside
        wb_left, wb_right = jnp.where(in_left, wb_side, 0.0), jnp.where(in_right, wb_side, 0.0)
        ww_ref[r, 0:8] = jnp.where(in_left, w_side, 0.0)
        ww_ref[r, 8 : 8 + N] = w
        ww_ref[r, 8 + N :] = jnp.where(in_right, w_side, 0.0)
        wwb_ref[r, 0:8] = wb_left
        wwb_ref[r, 8 : 8 + N] = wb
        wwb_ref[r, 8 + N :] = wb_right
        v_ref[r + 1, 0:8] = wb_left
        v_ref[r + 1, 8 : 8 + N] = wb
        v_ref[r + 1, 8 + N :] = wb_right
    sweeps(v_ref, ww_ref, wwb_ref, 2, ROWS_V - 2, 3)

    tile = info_ref[...]
    prev, cur = v_ref[REACH - 1], v_ref[REACH]
    for part in range(2):
        total = None
        for r in range(part * CUBE, (part + 1) * CUBE):
            nxt = v_ref[r + REACH + 1]
            beside = neighbours(prev, cur, nxt)[8 : 8 + N]
            fine = b_ref[r] - ((6.0 + s_ref[r]) * cur[8 : 8 + N] - beside)
            total = fine if total is None else total + fine
            prev, cur = cur, nxt
        for half in range(2):
            row = jnp.sum(total[half * CUBE : (half + 1) * CUBE], axis=0, keepdims=True)
            tile = jnp.where(sub == 2 * part + half, row, tile)
    lane = iota((8, LANES), 1)
    cells = tile
    for step in (1, 2, 4, 8):
        cells = cells + jnp.where((lane & step) == 0, pltpu.roll(cells, LANES - step, 1), pltpu.roll(cells, step, 1))
    tile = jnp.where(sub < 4, cells / float(CUBE), tile)
    coarse_ref[...] = tile
    right_ref[16] = tile
    left_ref[16] = tile
    for k in range(16):
        a, c = REACH + k, REACH + 16 + k
        right_ref[k] = jnp.where((sub >= 3) & (sub < 7), v_ref[a, N : N + 8], pltpu.roll(v_ref[c, N : N + 8], 4, 0))
        left_ref[k] = jnp.where((sub >= 1) & (sub < 5), v_ref[a, 8:16], pltpu.roll(v_ref[c, 8:16], 4, 0))


def correct_kernel(
    v_in_ref, coarse_ref, far_left_ref, far_right_ref, from_left_ref, from_right_ref, v_ref, down_ref, up_ref, e_ref
):
    cross, n_cross = lax.axis_index("cross"), lax.axis_size("cross")
    has_left, has_right = cross > 0, cross < n_cross - 1
    sub = iota((8, LANES), 0)
    lane = iota((8, LANES), 1)
    even = (sub & 1) == 0

    def wide(row):
        return jnp.broadcast_to(row, (8, LANES))

    scale = [
        jnp.where((cross + d >= 0) & (cross + d < n_cross), F32(DAMPING / 6.0), F32(0.0)) for d in range(-2, 3)
    ]
    tiles = (far_left_ref, from_left_ref.at[16], coarse_ref, from_right_ref.at[16], far_right_ref)
    ids = [wide(t[4:5]) for t in tiles]
    masks = [wide(t[5:6]) for t in tiles]
    owner = jnp.where(sub < 2, ids[1], jnp.where(sub < 4, ids[2], ids[3]))
    strip = []
    for d in range(5):
        chosen = (ids[d] == owner) & (masks[d] > 0.5)
        for j in range(2):
            cells = jnp.where(even, wide(tiles[d][j : j + 1]), wide(tiles[d][2 + j : 3 + j]))
            strip.append(jnp.where(chosen, cells, 0.0))
    e = [scale[j // 2] * strip[j] for j in range(10)]
    for step in range(1, 4):
        new = list(e)
        for j in range(step, 10 - step):
            beside = e[j - 1] + e[j + 1]
            beside = beside + jnp.where(even, pltpu.roll(e[j], 7, 0), pltpu.roll(e[j], 1, 0))
            beside = beside + jnp.where(lane < CUBE, 0.0, pltpu.roll(e[j], CUBE, 1))
            beside = beside + jnp.where(lane >= LANES - CUBE, 0.0, pltpu.roll(e[j], LANES - CUBE, 1))
            new[j] = (1.0 - DAMPING) * e[j] + scale[j // 2] * (strip[j] + beside)
        e = new
    mask = jnp.where(
        sub < 2, jnp.where(has_left, masks[1], 0.0), jnp.where(sub < 4, masks[2], jnp.where(has_right, masks[3], 0.0))
    )
    for j in range(3, 7):
        e_ref[j - 3] = e[j] * mask

    in_left = (sub >= 3) & (sub < 7) & has_left
    in_right = (sub >= 1) & (sub < 5) & has_right
    for i in range(2):
        first, second = wide(e_ref[1, 2 + i : 3 + i]), wide(e_ref[2, 2 + i : 3 + i])
        own = jnp.concatenate([first, first, second, second], axis=0)
        beside = wide(e_ref[0, i : i + 1]), wide(e_ref[3, 4 + i : 5 + i])
        for k in range(CUBE):
            r = i * CUBE + k
            v_ref[r, 8 : 8 + N] = v_in_ref[r + REACH, 8 : 8 + N] + own
            left, right = from_left_ref[k], from_right_ref[k]
            if i == 1:
                left, right = pltpu.roll(left, 4, 0), pltpu.roll(right, 4, 0)
            left = jnp.where(in_left, left, jnp.where(sub == 7, v_in_ref[r + REACH, 0:8], 0.0))
            right = jnp.where(in_right, right, jnp.where(sub == 0, v_in_ref[r + REACH, 8 + N :], 0.0))
            v_ref[r, 0:8] = left + beside[0]
            v_ref[r, 8 + N :] = right + beside[1]
    for target, start in ((up_ref, 0), (down_ref, N - REACH)):
        for k in range(REACH):
            target[k, 0:N] = v_ref[start + k, 8 : 8 + N]
            target[k, N:] = jnp.where(sub < 4, v_ref[start + k, 8 + N :], v_ref[start + k, 0:8])


def second_kernel(
    b_ref, s_ref, v_in_ref, ww_ref, wwb_ref, above_ref, below_ref, pressure_ref, residual_ref, v_ref
):
    span = lax.axis_index("span")
    has_up, has_down = span > 0, span < lax.axis_size("span") - 1
    sub = iota((8, LANES), 0)
    for r in range(ROWS_V):
        if REACH <= r < REACH + N:
            v_ref[r] = v_in_ref[r - REACH]
        else:
            source, k, inside = (above_ref, r, has_up) if r < REACH else (below_ref, r - REACH - N, has_down)
            side = source[k, N:]
            v_ref[r, 0:8] = jnp.where((sub >= 4) & inside, side, 0.0)
            v_ref[r, 8 : 8 + N] = jnp.where(inside, source[k, 0:N], 0.0)
            v_ref[r, 8 + N :] = jnp.where((sub < 4) & inside, side, 0.0)
    sweeps(v_ref, ww_ref, wwb_ref, 1, ROWS_V - 1, 4)
    prev, cur = v_ref[REACH - 1], v_ref[REACH]
    for r in range(N):
        nxt = v_ref[r + REACH + 1]
        beside = neighbours(prev, cur, nxt)[8 : 8 + N]
        mine = cur[8 : 8 + N]
        pressure_ref[r] = mine
        residual_ref[r] = b_ref[r] - ((6.0 + s_ref[r]) * mine - beside)
        prev, cur = cur, nxt


def call(kernel, outs, args, scratch=(), spaces=None, ops=0, room=32):
    vmem = pl.BlockSpec(memory_space=pltpu.VMEM)
    size = 4 * sum(math.prod(s) for s in outs)
    return pl.pallas_call(
        kernel,
        out_shape=[jax.ShapeDtypeStruct(s, F32) for s in outs],
        in_specs=[spaces or vmem] * len(args),
        out_specs=[vmem] * len(outs),
        scratch_shapes=[pltpu.VMEM(s, F32) if isinstance(s, tuple) else s for s in scratch],
        compiler_params=pltpu.CompilerParams(vmem_limit_bytes=room * 1024 * 1024),
        cost_estimate=pl.CostEstimate(flops=ops, bytes_accessed=2 * size, transcendentals=0),
    )(*args)


def shifted(block, axis, step):
    count = lax.axis_size(axis)
    pairs = [(i, (i + step) % count) for i in range(count)]
    return lax.ppermute(block, axis, [p for p in pairs if axis == "span" or p[1] - p[0] == step])


def on_device(right_side, shift, tile_mask, owner_lists, owner_ids):
    block = (N, N, LANES)
    edge = (N, 8, LANES)
    right, left = call(
        edges_kernel,
        [edge, edge],
        [right_side, shift],
        scratch=[edge, edge, edge, edge, pltpu.SemaphoreType.DMA((4,))],
        spaces=pl.BlockSpec(memory_space=pltpu.HBM),
        room=62,
    )
    from_left = shifted(right, "cross", 1)
    from_right = shifted(left, "cross", -1)
    w, wb, info = call(coefficients_kernel, [block, block, (8, LANES)], [right_side, shift, tile_mask, owner_ids])
    rows = (2, HALO, N + 8, LANES)
    down, up = call(rows_kernel, [rows, rows], [w, wb, from_left, from_right])
    above = shifted(down, "span", 1)
    below = shifted(up, "span", -1)
    v, ww, wwb, right, left, coarse = call(
        first_kernel,
        [
            (ROWS_V, WIDE, LANES), (ROWS_W, WIDE, LANES), (ROWS_W, WIDE, LANES), (17, 8, LANES), (17, 8, LANES),
            (8, LANES),
        ],
        [right_side, shift, w, wb, from_left, from_right, above, below, info],
    )
    far_left = shifted(coarse, "cross", 2)
    far_right = shifted(coarse, "cross", -2)
    from_left = shifted(right, "cross", 1)
    from_right = shifted(left, "cross", -1)
    rows = (REACH, N + 8, LANES)
    v, down, up = call(
        correct_kernel,
        [(N, WIDE, LANES), rows, rows],
        [v, coarse, far_left, far_right, from_left, from_right],
        scratch=[(4, 8, LANES)],
    )
    above = shifted(down, "span", 1)
    below = shifted(up, "span", -1)
    pressure, residual = call(
        second_kernel,
        [block, block],
        [right_side, shift, v, ww, wwb, above, below],
        scratch=[(ROWS_V, WIDE, LANES)],
    )
    return (pressure, residual)


def solution(mesh):
    return jax.shard_map(
        on_device,
        mesh=mesh,
        in_specs=(
            P("span", "cross", None),
            P("span", "cross", None),
            P("span", "cross"),
            P("span", "cross", None),
            P("span", "cross"),
        ),
        out_specs=(P("span", "cross", None), P("span", "cross", None)),
        check_vma=False,
    )
```

time: 296 us -> 60.3 us (0.20)
  the two profiles are of different devices: /device:TPU:34 before, /device:TPU:31 now
where the time goes in v2:
time: 60.3 us; the launch traced here: 59.9 us
  starting transfers between devices  32.7 us (54%)
  waiting for transfers between devices  16.6 us (28%)
  Pallas kernels  8.59 us (14%)
  between operations  2.04 us (3%)
    ppermute x10, starting transfers between devices, shifted(): lax.ppermute(block, axis, [p for p in pairs if axis == 'span' or p[1] - p...  32.7 us
    ppermute x10, waiting for transfers between devices, shifted(): lax.ppermute(block, axis, [p for p in pairs if axis == 'span' or p[1] - p...  16.6 us
    pallas_call x6, Pallas kernels, call(): pl.pallas_call(kernel, out_shape=[jax.ShapeDtypeStruct(s, F32) for s in o...  8.59 us
  transfers between devices with their start and end apart: 10, of which 7 were waited for; matrix products, arithmetic and copies ran while one was open for 0% of the time, Pallas kernels for 0%

profile of v2, /device:TPU:31, one launch (start us, length us, event | category | flops | bytes accessed | tf_op | source)
XLA Modules:
  0.0 59.9 jit_solution(9852285020486742946)
XLA Ops:
  0.6 0.0 copy-start.1
  0.6 0.0 copy-start
  0.6 1.9 %shard_map.60 = (f32[32,8,128]{2,1,0:T(8,128)}, f32[32,8,128]{2,1,0:T(8,128)}) custom-call(f32[32,32,128]{2,1,0:T(8,128)} %b_ref.7, f32[32,32,128]{2,1,0:T(8,128)} %s_ref.7), custom_call_target="tpu_custom_call" | custom-call | bytes 524288 | tf_op jit(solution)/shard_map/pallas_call | solution.py:247
  2.6 4.0 %collective-permute-start = (f32[32,8,128]{2,1,0:T(8,128)}, f32[32,8,128]{2,1,0:T(8,128)S(1)}, u32[]{:S(2)}, u32[]{:S(2)}) collective-permute-start(f32[32,8,128]{2,1,0:T(8,128)} %get-tuple-element.20), channel_id=1, source_target_pairs={{0,1},{1,2},{2,3},{3,4},{4,5},{5,6},{6,7},{7,8},{8,9},{9,10},{10,1... | collective-permute-start | bytes 393224 | tf_op jit(solution)/shard_map/ppermute | solution.py:261
  6.6 8.9 %collective-permute-start.1 = (f32[32,8,128]{2,1,0:T(8,128)}, f32[32,8,128]{2,1,0:T(8,128)S(1)}, u32[]{:S(2)}, u32[]{:S(2)}) collective-permute-start(f32[32,8,128]{2,1,0:T(8,128)} %get-tuple-element.21), channel_id=1, source_target_pairs={{1,0},{2,1},{3,2},{4,3},{5,4},{6,5},{7,6},{8,7},{9,8},{10,9},{11,1... | collective-permute-start | bytes 393224 | tf_op jit(solution)/shard_map/ppermute | solution.py:261
  16.7 0.0 copy-done.1
  16.7 0.0 copy-done
  16.8 0.1 shard_map.59
  16.9 0.1 collective-permute-done.from_left_ref
  16.9 1.0 %collective-permute-done.1.from_right_ref = f32[32,8,128]{2,1,0:T(8,128)S(1)} collective-permute-done((f32[32,8,128]{2,1,0:T(8,128)}, f32[32,8,128]{2,1,0:T(8,128)S(1)}, u32[]{:S(2)}, u32[]{:S(2)}) %collective-permute-start.1) | collective-permute-done | bytes 131104 | tf_op jit(solution)/shard_map/ppermute | solution.py:261
  17.9 4.0 %collective-permute-start.2 = (f32[2,4,40,128]{3,2,1,0:T(8,128)S(1)}, f32[2,4,40,128]{3,2,1,0:T(8,128)S(1)}, u32[]{:S(2)}, u32[]{:S(2)}) collective-permute-start(f32[2,4,40,128]{3,2,1,0:T(8,128)S(1)} %get-tuple-element.22), channel_id=1, source_target_pairs={{0,32},{32,64},{64,96},{96,128},{128,160},{160,192},{192,224},{224... | collective-permute-start | bytes 491528 | tf_op jit(solution)/shard_map/ppermute | solution.py:261
  21.9 0.0 collective-permute-start.3
  21.9 2.3 %collective-permute-done.2.above_ref = f32[2,4,40,128]{3,2,1,0:T(8,128)S(1)} collective-permute-done((f32[2,4,40,128]{3,2,1,0:T(8,128)S(1)}, f32[2,4,40,128]{3,2,1,0:T(8,128)S(1)}, u32[]{:S(2)}, u32[]{:S(2)}) %collective-permute-start.2) | collective-permute-done | bytes 163872 | tf_op jit(solution)/shard_map/ppermute | solution.py:261
  24.1 3.7 %collective-permute-done.3.below_ref = f32[2,4,40,128]{3,2,1,0:T(8,128)S(1)} collective-permute-done((f32[2,4,40,128]{3,2,1,0:T(8,128)S(1)}, f32[2,4,40,128]{3,2,1,0:T(8,128)S(1)}, u32[]{:S(2)}, u32[]{:S(2)}) %collective-permute-start.3) | collective-permute-done | bytes 163872 | tf_op jit(solution)/shard_map/ppermute | solution.py:261
  27.8 2.6 %shard_map.62 = (f32[42,48,128]{2,1,0:T(8,128)S(1)}, f32[40,48,128]{2,1,0:T(8,128)S(1)}, f32[40,48,128]{2,1,0:T(8,128)S(1)}, f32[17,8,128]{2,1,0:T(8,128)S(1)}, ...) custom-call(f32[32,32,128]{2,1,0:T(8,128)S(1)} %copy-done, f32[32,32,128]{2,1,0:T(8,128)S(1)} %copy-done.1, ...), custom_call_target="tpu_custom_call" | custom-call | bytes 6283264 | tf_op jit(solution)/shard_map/pallas_call | solution.py:247
  30.5 1.9 %collective-permute-start.6 = (f32[17,8,128]{2,1,0:T(8,128)S(1)}, f32[17,8,128]{2,1,0:T(8,128)S(1)}, u32[]{:S(2)}, u32[]{:S(2)}) collective-permute-start(f32[17,8,128]{2,1,0:T(8,128)S(1)} %get-tuple-element.27), channel_id=1, source_target_pairs={{0,1},{1,2},{2,3},{3,4},{4,5},{5,6},{6,7},{7,8},{8,9},{9,10},{10,1... | collective-permute-start | bytes 208904 | tf_op jit(solution)/shard_map/ppermute | solution.py:261
  32.4 6.1 %collective-permute-start.7 = (f32[17,8,128]{2,1,0:T(8,128)S(1)}, f32[17,8,128]{2,1,0:T(8,128)S(1)}, u32[]{:S(2)}, u32[]{:S(2)}) collective-permute-start(f32[17,8,128]{2,1,0:T(8,128)S(1)} %get-tuple-element.28), channel_id=1, source_target_pairs={{1,0},{2,1},{3,2},{4,3},{5,4},{6,5},{7,6},{8,7},{9,8},{10,9},{11,1... | collective-permute-start | bytes 208904 | tf_op jit(solution)/shard_map/ppermute | solution.py:261
  38.5 3.1 %collective-permute-start.5 = (f32[8,128]{1,0:T(8,128)S(1)}, f32[8,128]{1,0:T(8,128)S(1)}, u32[]{:S(2)}, u32[]{:S(2)}) collective-permute-start(f32[8,128]{1,0:T(8,128)S(1)} %get-tuple-element.26.coarse_ref), channel_id=1, source_target_pairs={{2,0},{3,1},{4,2},{5,3},{6,4},{7,5},{8,6},{9,7},{10,8},{11,9},{12,... | collective-permute-start | bytes 12296 | tf_op jit(solution)/shard_map/ppermute | solution.py:261
  41.6 3.1 %collective-permute-start.4 = (f32[8,128]{1,0:T(8,128)S(1)}, f32[8,128]{1,0:T(8,128)S(1)}, u32[]{:S(2)}, u32[]{:S(2)}) collective-permute-start(f32[8,128]{1,0:T(8,128)S(1)} %get-tuple-element.26.coarse_ref), channel_id=1, source_target_pairs={{0,2},{1,3},{2,4},{3,5},{4,6},{5,7},{6,8},{7,9},{8,10},{9,11},{10,... | collective-permute-start | bytes 12296 | tf_op jit(solution)/shard_map/ppermute | solution.py:261
  44.7 0.0 collective-permute-done.5.far_right_ref
  44.7 4.3 %collective-permute-done.4.far_left_ref = f32[8,128]{1,0:T(8,128)S(1)} collective-permute-done((f32[8,128]{1,0:T(8,128)S(1)}, f32[8,128]{1,0:T(8,128)S(1)}, u32[]{:S(2)}, u32[]{:S(2)}) %collective-permute-start.4) | collective-permute-done | bytes 4128 | tf_op jit(solution)/shard_map/ppermute | solution.py:261
  49.0 0.0 collective-permute-done.6.from_left_ref
  49.0 0.0 collective-permute-done.7.from_right_ref
  49.0 0.3 shard_map.63
  49.3 1.7 %collective-permute-start.8 = (f32[5,40,128]{2,1,0:T(8,128)S(1)}, f32[5,40,128]{2,1,0:T(8,128)S(1)}, u32[]{:S(2)}, u32[]{:S(2)}) collective-permute-start(f32[5,40,128]{2,1,0:T(8,128)S(1)} %get-tuple-element.32), channel_id=1, source_target_pairs={{0,32},{32,64},{64,96},{96,128},{128,160},{160,192},{192,224},{224... | collective-permute-start | bytes 307208 | tf_op jit(solution)/shard_map/ppermute | solution.py:261
  51.0 0.0 collective-permute-start.9
  51.0 1.7 %collective-permute-done.8.above_ref = f32[5,40,128]{2,1,0:T(8,128)S(1)} collective-permute-done((f32[5,40,128]{2,1,0:T(8,128)S(1)}, f32[5,40,128]{2,1,0:T(8,128)S(1)}, u32[]{:S(2)}, u32[]{:S(2)}) %collective-permute-start.8) | collective-permute-done | bytes 102432 | tf_op jit(solution)/shard_map/ppermute | solution.py:261
  52.7 3.6 %collective-permute-done.9.below_ref = f32[5,40,128]{2,1,0:T(8,128)S(1)} collective-permute-done((f32[5,40,128]{2,1,0:T(8,128)S(1)}, f32[5,40,128]{2,1,0:T(8,128)S(1)}, u32[]{:S(2)}, u32[]{:S(2)}) %collective-permute-start.9) | collective-permute-done | bytes 102432 | tf_op jit(solution)/shard_map/ppermute | solution.py:261
  56.3 3.6 %shard_map.64 = (f32[32,32,128]{2,1,0:T(8,128)}, f32[32,32,128]{2,1,0:T(8,128)}) custom-call(f32[32,32,128]{2,1,0:T(8,128)S(1)} %copy-done, f32[32,32,128]{2,1,0:T(8,128)S(1)} %copy-done.1, f32[32,48,128]{2,1,0:T(8,128)S(1)} %get-tuple-element.29.v_in_ref, f32[40,48,128]{2,1,0:T(8,128)S(1)} %get-tuple-element.30.ww_ref, ...), custom_call_target="tpu_custom_call" | custom-call | bytes 2097152 | tf_op jit(solution)/shard_map/pallas_call | solution.py:247
  (1 shorter events, 0.0 us)
Async XLA Ops:
  0.6 16.1 %copy-start.1 = (f32[32,32,128]{2,1,0:T(8,128)S(1)}, f32[32,32,128]{2,1,0:T(8,128)}, u32[]{:S(2)}) copy-start(f32[32,32,128]{2,1,0:T(8,128)} %s_ref.7) | copy-start | bytes 1572868
  0.6 16.1 %copy-start = (f32[32,32,128]{2,1,0:T(8,128)S(1)}, f32[32,32,128]{2,1,0:T(8,128)}, u32[]{:S(2)}) copy-start(f32[32,32,128]{2,1,0:T(8,128)} %b_ref.7) | copy-start | bytes 1572868
  2.6 14.4 %collective-permute-start = (f32[32,8,128]{2,1,0:T(8,128)}, f32[32,8,128]{2,1,0:T(8,128)S(1)}, u32[]{:S(2)}, u32[]{:S(2)}) collective-permute-start(f32[32,8,128]{2,1,0:T(8,128)} %get-tuple-element.20), channel_id=1, source_target_pairs={{0,1},{1,2},{2,3},{3,4},{4,5},{5,6},{6,7},{7,8},{8,9},{9,10},{10,1... | collective-permute-start | bytes 393224 | tf_op jit(solution)/shard_map/ppermute | solution.py:261
  6.6 11.3 %collective-permute-start.1 = (f32[32,8,128]{2,1,0:T(8,128)}, f32[32,8,128]{2,1,0:T(8,128)S(1)}, u32[]{:S(2)}, u32[]{:S(2)}) collective-permute-start(f32[32,8,128]{2,1,0:T(8,128)} %get-tuple-element.21), channel_id=1, source_target_pairs={{1,0},{2,1},{3,2},{4,3},{5,4},{6,5},{7,6},{8,7},{9,8},{10,9},{11,1... | collective-permute-start | bytes 393224 | tf_op jit(solution)/shard_map/ppermute | solution.py:261
  17.9 6.2 %collective-permute-start.2 = (f32[2,4,40,128]{3,2,1,0:T(8,128)S(1)}, f32[2,4,40,128]{3,2,1,0:T(8,128)S(1)}, u32[]{:S(2)}, u32[]{:S(2)}) collective-permute-start(f32[2,4,40,128]{3,2,1,0:T(8,128)S(1)} %get-tuple-element.22), channel_id=1, source_target_pairs={{0,32},{32,64},{64,96},{96,128},{128,160},{160,192},{192,224},{224... | collective-permute-start | bytes 491528 | tf_op jit(solution)/shard_map/ppermute | solution.py:261
  21.9 6.0 %collective-permute-start.3 = (f32[2,4,40,128]{3,2,1,0:T(8,128)S(1)}, f32[2,4,40,128]{3,2,1,0:T(8,128)S(1)}, u32[]{:S(2)}, u32[]{:S(2)}) collective-permute-start(f32[2,4,40,128]{3,2,1,0:T(8,128)S(1)} %get-tuple-element.23), channel_id=1, source_target_pairs={{0,480},{32,0},{64,32},{96,64},{128,96},{160,128},{192,160},{224,1... | collective-permute-start | bytes 491528 | tf_op jit(solution)/shard_map/ppermute | solution.py:261
  30.5 18.5 %collective-permute-start.6 = (f32[17,8,128]{2,1,0:T(8,128)S(1)}, f32[17,8,128]{2,1,0:T(8,128)S(1)}, u32[]{:S(2)}, u32[]{:S(2)}) collective-permute-start(f32[17,8,128]{2,1,0:T(8,128)S(1)} %get-tuple-element.27), channel_id=1, source_target_pairs={{0,1},{1,2},{2,3},{3,4},{4,5},{5,6},{6,7},{7,8},{8,9},{9,10},{10,1... | collective-permute-start | bytes 208904 | tf_op jit(solution)/shard_map/ppermute | solution.py:261
  32.4 16.6 %collective-permute-start.7 = (f32[17,8,128]{2,1,0:T(8,128)S(1)}, f32[17,8,128]{2,1,0:T(8,128)S(1)}, u32[]{:S(2)}, u32[]{:S(2)}) collective-permute-start(f32[17,8,128]{2,1,0:T(8,128)S(1)} %get-tuple-element.28), channel_id=1, source_target_pairs={{1,0},{2,1},{3,2},{4,3},{5,4},{6,5},{7,6},{8,7},{9,8},{10,9},{11,1... | collective-permute-start | bytes 208904 | tf_op jit(solution)/shard_map/ppermute | solution.py:261
  38.5 6.2 %collective-permute-start.5 = (f32[8,128]{1,0:T(8,128)S(1)}, f32[8,128]{1,0:T(8,128)S(1)}, u32[]{:S(2)}, u32[]{:S(2)}) collective-permute-start(f32[8,128]{1,0:T(8,128)S(1)} %get-tuple-element.26.coarse_ref), channel_id=1, source_target_pairs={{2,0},{3,1},{4,2},{5,3},{6,4},{7,5},{8,6},{9,7},{10,8},{11,9},{12,... | collective-permute-start | bytes 12296 | tf_op jit(solution)/shard_map/ppermute | solution.py:261
  41.6 7.4 %collective-permute-start.4 = (f32[8,128]{1,0:T(8,128)S(1)}, f32[8,128]{1,0:T(8,128)S(1)}, u32[]{:S(2)}, u32[]{:S(2)}) collective-permute-start(f32[8,128]{1,0:T(8,128)S(1)} %get-tuple-element.26.coarse_ref), channel_id=1, source_target_pairs={{0,2},{1,3},{2,4},{3,5},{4,6},{5,7},{6,8},{7,9},{8,10},{9,11},{10,... | collective-permute-start | bytes 12296 | tf_op jit(solution)/shard_map/ppermute | solution.py:261
  49.3 3.4 %collective-permute-start.8 = (f32[5,40,128]{2,1,0:T(8,128)S(1)}, f32[5,40,128]{2,1,0:T(8,128)S(1)}, u32[]{:S(2)}, u32[]{:S(2)}) collective-permute-start(f32[5,40,128]{2,1,0:T(8,128)S(1)} %get-tuple-element.32), channel_id=1, source_target_pairs={{0,32},{32,64},{64,96},{96,128},{128,160},{160,192},{192,224},{224... | collective-permute-start | bytes 307208 | tf_op jit(solution)/shard_map/ppermute | solution.py:261
  51.0 5.3 %collective-permute-start.9 = (f32[5,40,128]{2,1,0:T(8,128)S(1)}, f32[5,40,128]{2,1,0:T(8,128)S(1)}, u32[]{:S(2)}, u32[]{:S(2)}) collective-permute-start(f32[5,40,128]{2,1,0:T(8,128)S(1)} %get-tuple-element.33), channel_id=1, source_target_pairs={{0,480},{32,0},{64,32},{96,64},{128,96},{160,128},{192,160},{224,1... | collective-permute-start | bytes 307208 | tf_op jit(solution)/shard_map/ppermute | solution.py:261

commit v3 on v2

v3 whole, which is shorter than its diff:
```python
import math

import jax
import jax.numpy as jnp
from jax import lax
from jax.experimental import pallas as pl
from jax.experimental.pallas import tpu as pltpu
from jax.sharding import PartitionSpec as P

DAMPING = 0.8
N = 32
LANES = 128
WIDE = N + 16
HALO = 4
REACH = 5
ROWS_W = N + 2 * HALO
ROWS_V = N + 2 * REACH
CUBE = 16
F32 = jnp.float32


def iota(shape, axis):
    return lax.broadcasted_iota(jnp.int32, shape, axis)


def neighbours(prev, cur, nxt):
    cells = cur.shape[0]
    lane = iota(cur.shape, 1)
    low = jnp.where(lane == 0, 0.0, pltpu.roll(cur, 1, 1))
    high = jnp.where(lane == LANES - 1, 0.0, pltpu.roll(cur, LANES - 1, 1))
    beside = pltpu.roll(cur, 1, 0) + pltpu.roll(cur, cells - 1, 0)
    return (prev + nxt) + beside + (low + high)


def swept(prev, cur, nxt, w, wb):
    return (1.0 - DAMPING) * cur + (wb + w * neighbours(prev, cur, nxt))


def inner_sweeps(v_ref, w_ref, wb_ref, saved_ref, count):
    def one(step, carry):
        prev, cur = v_ref[0], v_ref[1]
        for r in range(1, N - 1):
            nxt = v_ref[r + 1]
            v_ref[r] = swept(prev, cur, nxt, w_ref[r], wb_ref[r])
            prev, cur = cur, nxt
        for k in range(2):
            saved_ref[0, step, k] = v_ref[step + 1 + k]
            saved_ref[1, step, k] = v_ref[N - 3 - step + k]
        return carry

    lax.fori_loop(0, count, one, 0)


def outer_sweeps(rows, first, count, side, coefficients, saved_ref):
    for step in range(count):
        new = [swept(*rows[i : i + 3], *coefficients(first + 1 + i)) for i in range(len(rows) - 2)]
        saved = [saved_ref[side, step, k] for k in range(2)]
        rows, first = (new + saved, first + 1) if side == 0 else (saved + new, first - 1)
    return rows, first


def fine_residual(prev, cur, nxt, b, s):
    own = slice(8, 8 + N)
    return b - ((6.0 + s) * cur[own] - neighbours(prev, cur, nxt)[own])


def edges_kernel(b_ref, s_ref, right_ref, left_ref, b_left, b_right, s_left, s_right, sems):
    copies = [
        pltpu.make_async_copy(source.at[:, pl.ds(start, 8), :], target, sems.at[n])
        for n, (source, start, target) in enumerate(
            ((s_ref, N - 8, s_right), (b_ref, N - 8, b_right), (s_ref, 0, s_left), (b_ref, 0, b_left))
        )
    ]
    for copy in copies:
        copy.start()
    sub = iota((8, LANES), 0)
    copies[0].wait()
    copies[1].wait()
    for r in range(N):
        w = DAMPING / (6.0 + s_right[r])
        right_ref[r] = jnp.where(sub < 4, pltpu.roll(w, 4, 0), w * b_right[r])
    copies[2].wait()
    copies[3].wait()
    for r in range(N):
        w = DAMPING / (6.0 + s_left[r])
        left_ref[r] = jnp.where(sub < 4, w, pltpu.roll(w * b_left[r], 4, 0))


def coefficients_kernel(b_ref, s_ref, mask_ref, id_ref, w_ref, wb_ref, info_ref):
    for r in range(N):
        w = DAMPING / (6.0 + s_ref[r])
        w_ref[r] = w
        wb_ref[r] = w * b_ref[r]
    sub = iota((8, LANES), 0)
    number = jnp.broadcast_to(id_ref[...].astype(F32), (8, LANES))
    mask = jnp.broadcast_to(mask_ref[...].astype(F32), (8, LANES))
    info_ref[...] = jnp.where(sub == 4, number, jnp.where(sub == 5, mask, 0.0))


def beside_of(left_msg, right_msg):
    sub = iota((8, LANES), 0)
    w = jnp.where(sub < 4, right_msg, pltpu.roll(left_msg, 4, 0))
    wb = jnp.where(sub < 4, pltpu.roll(right_msg, 4, 0), left_msg)
    return w, wb


def rows_kernel(w_ref, wb_ref, from_left_ref, from_right_ref, down_ref, up_ref):
    for target, start in ((up_ref, 0), (down_ref, N - HALO)):
        for k in range(HALO):
            r = start + k
            sides = beside_of(from_left_ref[r], from_right_ref[r])
            for a, ref in enumerate((w_ref, wb_ref)):
                target[a, k, 0:N] = ref[r]
                target[a, k, N:] = sides[a]


def first_inner_kernel(
    b_ref, s_ref, w_ref, wb_ref, from_left_ref, from_right_ref, v_ref, ww_ref, wwb_ref, saved_ref, partial_ref
):
    cross = lax.axis_index("cross")
    sub = iota((8, LANES), 0)
    in_left, in_right = (sub >= 4) & (cross > 0), (sub < 4) & (cross < lax.axis_size("cross") - 1)
    for r in range(N):
        w_side, wb_side = beside_of(from_left_ref[r], from_right_ref[r])
        for ref, own, side in ((ww_ref, w_ref[r], w_side), (wwb_ref, wb_ref[r], wb_side)):
            ref[r, 0:8] = jnp.where(in_left, side, 0.0)
            ref[r, 8 : 8 + N] = own
            ref[r, 8 + N :] = jnp.where(in_right, side, 0.0)
        v_ref[r] = wwb_ref[r]
    inner_sweeps(v_ref, ww_ref, wwb_ref, saved_ref, 3)
    for part in range(2):
        total = jnp.zeros((N, LANES), F32)
        for r in range(4 + 12 * part, 16 + 12 * part):
            total = total + fine_residual(v_ref[r - 1], v_ref[r], v_ref[r + 1], b_ref[r], s_ref[r])
        partial_ref[part] = total


def first_outer_kernel(
    b_ref, s_ref, v_ref, ww_ref, wwb_ref, saved_ref, partial_ref, above_ref, below_ref, info_ref,
    ends_ref, halo_ref, right_ref, left_ref, coarse_ref,
):
    span, cross = lax.axis_index("span"), lax.axis_index("cross")
    sub = iota((8, LANES), 0)
    in_left, in_right = (sub >= 4) & (cross > 0), (sub < 4) & (cross < lax.axis_size("cross") - 1)
    inside = (span > 0, span < lax.axis_size("span") - 1)
    for side, source in enumerate((above_ref, below_ref)):
        for a in range(2):
            for k in range(HALO):
                beside = source[a, k, N:]
                halo_ref[side, a, k, 0:8] = jnp.where(in_left & inside[side], beside, 0.0)
                halo_ref[side, a, k, 8 : 8 + N] = jnp.where(inside[side], source[a, k, 0:N], 0.0)
                halo_ref[side, a, k, 8 + N :] = jnp.where(in_right & inside[side], beside, 0.0)

    def coefficients(r):
        if 0 <= r < N:
            return ww_ref[r], wwb_ref[r]
        side, k = (0, r + HALO) if r < 0 else (1, r - N)
        return halo_ref[side, 0, k], halo_ref[side, 1, k]

    tile = info_ref[...]
    for side in range(2):
        start = -HALO if side == 0 else N - 2
        rows, start = outer_sweeps(
            [coefficients(r)[1] for r in range(start, start + HALO + 2)], start, 3, side, coefficients, saved_ref
        )
        total = partial_ref[side]
        for i in range(1, 5):
            r = start + i
            total = total + fine_residual(*rows[i - 1 : i + 2], b_ref[r], s_ref[r])
        for half in range(2):
            row = jnp.sum(total[half * CUBE : (half + 1) * CUBE], axis=0, keepdims=True)
            tile = jnp.where(sub == 2 * side + half, row, tile)
        for k in range(3):
            ends_ref[side, k] = rows[k + 1 + side]
    lane = iota((8, LANES), 1)
    cells = tile
    for step in (1, 2, 4, 8):
        cells = cells + jnp.where((lane & step) == 0, pltpu.roll(cells, LANES - step, 1), pltpu.roll(cells, step, 1))
    tile = jnp.where(sub < 4, cells / float(CUBE), tile)
    coarse_ref[...] = tile
    right_ref[16] = tile
    left_ref[16] = tile

    def pressure(r):
        return ends_ref.at[0, r] if r < 3 else (v_ref.at[r] if r < N - 3 else ends_ref.at[1, r - N + 3])

    for k in range(16):
        a, c = pressure(k), pressure(16 + k)
        right_ref[k] = jnp.where((sub >= 3) & (sub < 7), a[N : N + 8], pltpu.roll(c[N : N + 8], 4, 0))
        left_ref[k] = jnp.where((sub >= 1) & (sub < 5), a[8:16], pltpu.roll(c[8:16], 4, 0))


def correct_kernel(
    inner_ref, ends_ref, coarse_ref, far_left_ref, far_right_ref, from_left_ref, from_right_ref, v_ref, down_ref, up_ref, e_ref
):
    cross, n_cross = lax.axis_index("cross"), lax.axis_size("cross")
    has_left, has_right = cross > 0, cross < n_cross - 1
    sub = iota((8, LANES), 0)
    lane = iota((8, LANES), 1)
    even = (sub & 1) == 0

    def wide(row):
        return jnp.broadcast_to(row, (8, LANES))

    scale = [
        jnp.where((cross + d >= 0) & (cross + d < n_cross), F32(DAMPING / 6.0), F32(0.0)) for d in range(-2, 3)
    ]
    tiles = (far_left_ref, from_left_ref.at[16], coarse_ref, from_right_ref.at[16], far_right_ref)
    ids = [wide(t[4:5]) for t in tiles]
    masks = [wide(t[5:6]) for t in tiles]
    owner = jnp.where(sub < 2, ids[1], jnp.where(sub < 4, ids[2], ids[3]))
    strip = []
    for d in range(5):
        chosen = (ids[d] == owner) & (masks[d] > 0.5)
        for j in range(2):
            cells = jnp.where(even, wide(tiles[d][j : j + 1]), wide(tiles[d][2 + j : 3 + j]))
            strip.append(jnp.where(chosen, cells, 0.0))
    e = [scale[j // 2] * strip[j] for j in range(10)]
    for step in range(1, 4):
        new = list(e)
        for j in range(step, 10 - step):
            beside = e[j - 1] + e[j + 1]
            beside = beside + jnp.where(even, pltpu.roll(e[j], 7, 0), pltpu.roll(e[j], 1, 0))
            beside = beside + jnp.where(lane < CUBE, 0.0, pltpu.roll(e[j], CUBE, 1))
            beside = beside + jnp.where(lane >= LANES - CUBE, 0.0, pltpu.roll(e[j], LANES - CUBE, 1))
            new[j] = (1.0 - DAMPING) * e[j] + scale[j // 2] * (strip[j] + beside)
        e = new
    mask = jnp.where(
        sub < 2, jnp.where(has_left, masks[1], 0.0), jnp.where(sub < 4, masks[2], jnp.where(has_right, masks[3], 0.0))
    )
    for j in range(3, 7):
        e_ref[j - 3] = e[j] * mask

    in_left = (sub >= 3) & (sub < 7) & has_left
    in_right = (sub >= 1) & (sub < 5) & has_right
    for i in range(2):
        first, second = wide(e_ref[1, 2 + i : 3 + i]), wide(e_ref[2, 2 + i : 3 + i])
        own = jnp.concatenate([first, first, second, second], axis=0)
        beside = wide(e_ref[0, i : i + 1]), wide(e_ref[3, 4 + i : 5 + i])
        for k in range(CUBE):
            r = i * CUBE + k
            source = ends_ref.at[0, r] if r < 3 else (inner_ref.at[r] if r < N - 3 else ends_ref.at[1, r - N + 3])
            v_ref[r, 8 : 8 + N] = source[8 : 8 + N] + own
            left, right = from_left_ref[k], from_right_ref[k]
            if i == 1:
                left, right = pltpu.roll(left, 4, 0), pltpu.roll(right, 4, 0)
            left = jnp.where(in_left, left, jnp.where(sub == 7, source[0:8], 0.0))
            right = jnp.where(in_right, right, jnp.where(sub == 0, source[8 + N :], 0.0))
            v_ref[r, 0:8] = left + beside[0]
            v_ref[r, 8 + N :] = right + beside[1]
    for target, start in ((up_ref, 0), (down_ref, N - REACH)):
        for k in range(REACH):
            target[k, 0:N] = v_ref[start + k, 8 : 8 + N]
            target[k, N:] = jnp.where(sub < 4, v_ref[start + k, 8 + N :], v_ref[start + k, 0:8])


def second_inner_kernel(
    b_ref, s_ref, v_in_ref, ww_ref, wwb_ref, saved_ref, pressure_hbm, residual_hbm, v_ref, residual_ref, sems
):
    for r in range(N):
        v_ref[r] = v_in_ref[r]
    inner_sweeps(v_ref, ww_ref, wwb_ref, saved_ref, 4)
    low, high = 4, N - 4
    first = pltpu.make_async_copy(
        v_ref.at[pl.ds(low, high - low), pl.ds(8, N), :], pressure_hbm.at[pl.ds(low, high - low)], sems.at[0]
    )
    first.start()
    low, high = 5, N - 5
    for r in range(low, high):
        residual_ref[r - low] = fine_residual(v_ref[r - 1], v_ref[r], v_ref[r + 1], b_ref[r], s_ref[r])
    second = pltpu.make_async_copy(residual_ref, residual_hbm.at[pl.ds(low, high - low)], sems.at[1])
    second.start()
    first.wait()
    second.wait()


def second_outer_kernel(
    b_ref, s_ref, v_ref, ww_ref, wwb_ref, halo_ref, saved_ref, above_ref, below_ref, pressure_in, residual_in,
    pressure_hbm, residual_hbm, pressure_ref, residual_ref, sems,
):
    span = lax.axis_index("span")
    inside = (span > 0, span < lax.axis_size("span") - 1)
    sub = iota((8, LANES), 0)

    def coefficients(r):
        if 0 <= r < N:
            return ww_ref[r], wwb_ref[r]
        side, k = (0, r + HALO) if r < 0 else (1, r - N)
        return halo_ref[side, 0, k], halo_ref[side, 1, k]

    copies = []
    for side, source in enumerate((above_ref, below_ref)):
        outside = []
        for k in range(REACH):
            beside = source[k, N:]
            left = jnp.where((sub >= 4) & inside[side], beside, 0.0)
            right = jnp.where((sub < 4) & inside[side], beside, 0.0)
            outside.append(jnp.concatenate([left, jnp.where(inside[side], source[k, 0:N], 0.0), right], axis=0))
        if side == 0:
            rows, start = outside + [v_ref[0], v_ref[1]], -REACH
        else:
            rows, start = [v_ref[N - 2], v_ref[N - 1]] + outside, N - 2
        rows, start = outer_sweeps(rows, start, 4, side, coefficients, saved_ref)
        for k in range(4):
            pressure_ref[side, k] = rows[k + 1 + side][8 : 8 + N]
        for i in range(1, 6):
            r = start + i
            residual_ref[side, i - 1] = fine_residual(*rows[i - 1 : i + 2], b_ref[r], s_ref[r])
        for ref, hbm, count in ((pressure_ref, pressure_hbm, 4), (residual_ref, residual_hbm, 5)):
            place = pl.ds(0 if side == 0 else N - count, count)
            copies.append(pltpu.make_async_copy(ref.at[side], hbm.at[place], sems.at[len(copies)]))
            copies[-1].start()
    for copy in copies:
        copy.wait()


VMEM = pl.BlockSpec(memory_space=pltpu.VMEM)
HBM = pl.BlockSpec(memory_space=pltpu.HBM)


def call(kernel, outs, args, scratch=(), ins=None, out_specs=None, ops=0, room=32, aliases=None):
    size = 4 * sum(math.prod(s) for s in outs)
    return pl.pallas_call(
        kernel,
        out_shape=[jax.ShapeDtypeStruct(s, F32) for s in outs],
        in_specs=ins or [VMEM] * len(args),
        out_specs=out_specs or [VMEM] * len(outs),
        scratch_shapes=[pltpu.VMEM(s, F32) if isinstance(s, tuple) else s for s in scratch],
        input_output_aliases=aliases or {},
        compiler_params=pltpu.CompilerParams(vmem_limit_bytes=room * 1024 * 1024),
        cost_estimate=pl.CostEstimate(flops=ops, bytes_accessed=2 * size, transcendentals=0),
    )(*args)


def shifted(block, axis, step):
    count = lax.axis_size(axis)
    pairs = [(i, (i + step) % count) for i in range(count)]
    return lax.ppermute(block, axis, [p for p in pairs if axis == "span" or p[1] - p[0] == step])


def on_device(right_side, shift, tile_mask, owner_lists, owner_ids):
    block, wide, edge = (N, N, LANES), (N, WIDE, LANES), (N, 8, LANES)
    sems = pltpu.SemaphoreType.DMA
    right, left = call(
        edges_kernel, [edge, edge], [right_side, shift], scratch=[edge, edge, edge, edge, sems((4,))],
        ins=[HBM] * 2, room=60,
    )
    b, s, right, left = lax.optimization_barrier((right_side, shift, right, left))
    from_left = shifted(right, "cross", 1)
    from_right = shifted(left, "cross", -1)
    w, wb, info = call(
        coefficients_kernel, [block, block, (8, LANES)], [b, s, tile_mask, owner_ids], ops=2**20
    )
    rows = (2, HALO, N + 8, LANES)
    down, up = call(rows_kernel, [rows, rows], [w, wb, from_left, from_right])
    above = shifted(down, "span", 1)
    below = shifted(up, "span", -1)
    v, ww, wwb, saved, partial = call(
        first_inner_kernel,
        [wide, wide, wide, (2, 3, 2, WIDE, LANES), (2, N, LANES)],
        [b, s, w, wb, from_left, from_right],
        ops=2**23,
    )
    ends, halo, right, left, coarse = call(
        first_outer_kernel,
        [(2, 3, WIDE, LANES), (2, 2, HALO, WIDE, LANES), (17, 8, LANES), (17, 8, LANES), (8, LANES)],
        [b, s, v, ww, wwb, saved, partial, above, below, info],
    )
    far_left = shifted(coarse, "cross", 2)
    far_right = shifted(coarse, "cross", -2)
    from_left = shifted(right, "cross", 1)
    from_right = shifted(left, "cross", -1)
    rows = (REACH, N + 8, LANES)
    v, down, up = call(
        correct_kernel,
        [wide, rows, rows],
        [v, ends, coarse, far_left, far_right, from_left, from_right],
        scratch=[(4, 8, LANES)],
    )
    above = shifted(down, "span", 1)
    below = shifted(up, "span", -1)
    saved, pressure, residual = call(
        second_inner_kernel,
        [(2, 4, 2, WIDE, LANES), block, block],
        [b, s, v, ww, wwb],
        scratch=[wide, (N - 10, N, LANES), sems((2,))],
        out_specs=[VMEM, HBM, HBM],
        ops=2**23,
    )
    return tuple(
        call(
            second_outer_kernel,
            [block, block],
            [b, s, v, ww, wwb, halo, saved, above, below, pressure, residual],
            scratch=[(2, 4, N, LANES), (2, 5, N, LANES), sems((4,))],
            ins=[VMEM] * 9 + [HBM] * 2,
            out_specs=[HBM, HBM],
            aliases={9: 0, 10: 1},
        )
    )


def solution(mesh):
    return jax.shard_map(
        on_device,
        mesh=mesh,
        in_specs=(
            P("span", "cross", None),
            P("span", "cross", None),
            P("span", "cross"),
            P("span", "cross", None),
            P("span", "cross"),
        ),
        out_specs=(P("span", "cross", None), P("span", "cross", None)),
        check_vma=False,
    )
```

time: 60.3 us -> 56.3 us (0.934)
  waiting for transfers between devices: 16.6 us -> 11.8 us
  Pallas kernels: 8.59 us -> 9.4 us
    ppermute x10, waiting for transfers between devices: 16.6 us -> 11.8 us  [shifted(): lax.ppermute(block, axis, [p for p in pairs if axis == 'span' or p[1] - p...]
    pallas_call x6 -> x8, Pallas kernels: 8.59 us -> 9.4 us  [call(): pl.pallas_call(kernel, out_shape=[jax.ShapeDtypeStruct(s, F32) for s in o...]
  transfers between devices with their start and end apart: 10 -> 10, of which waited for: 7 -> 6; matrix products, arithmetic and copies ran while one was open for 0% -> 0% of each run, Pallas kernels for 0% -> 9%
where the time goes in v3:
time: 56.3 us; the launch traced here: 56.1 us
  starting transfers between devices  32.7 us (58%)
  waiting for transfers between devices  11.8 us (21%)
  Pallas kernels  9.4 us (17%)
  between operations  2.06 us (4%)
    ppermute x10, starting transfers between devices, shifted(): lax.ppermute(block, axis, [p for p in pairs if axis == 'span' or p[1] - p...  32.7 us
    ppermute x10, waiting for transfers between devices, shifted(): lax.ppermute(block, axis, [p for p in pairs if axis == 'span' or p[1] - p...  11.8 us
    pallas_call x8, Pallas kernels, call(): pl.pallas_call(kernel, out_shape=[jax.ShapeDtypeStruct(s, F32) for s in o...  9.4 us
  transfers between devices with their start and end apart: 10, of which 6 were waited for; matrix products, arithmetic and copies ran while one was open for 0% of the time, Pallas kernels for 9%

profile of v3, /device:TPU:31, one launch (start us, length us, event | category | flops | bytes accessed | tf_op | source)
XLA Modules:
  0.0 56.1 jit_solution(267256731845303694)
XLA Ops:
  0.6 0.0 copy-start.1
  0.6 0.0 copy-start
  0.6 1.9 %shard_map.59 = (f32[32,8,128]{2,1,0:T(8,128)}, f32[32,8,128]{2,1,0:T(8,128)}) custom-call(f32[32,32,128]{2,1,0:T(8,128)} %b_ref.6, f32[32,32,128]{2,1,0:T(8,128)} %s_ref.6), custom_call_target="tpu_custom_call" | custom-call | bytes 524288 | tf_op jit(solution)/shard_map/pallas_call | solution.py:323
  2.6 4.0 %collective-permute-start = (f32[32,8,128]{2,1,0:T(8,128)}, f32[32,8,128]{2,1,0:T(8,128)S(1)}, u32[]{:S(2)}, u32[]{:S(2)}) collective-permute-start(f32[32,8,128]{2,1,0:T(8,128)} %get-tuple-element.35), channel_id=1, source_target_pairs={{0,1},{1,2},{2,3},{3,4},{4,5},{5,6},{6,7},{7,8},{8,9},{9,10},{10,1... | collective-permute-start | bytes 393224 | tf_op jit(solution)/shard_map/ppermute | solution.py:338
  6.6 8.9 %collective-permute-start.1 = (f32[32,8,128]{2,1,0:T(8,128)}, f32[32,8,128]{2,1,0:T(8,128)S(1)}, u32[]{:S(2)}, u32[]{:S(2)}) collective-permute-start(f32[32,8,128]{2,1,0:T(8,128)} %get-tuple-element.36), channel_id=1, source_target_pairs={{1,0},{2,1},{3,2},{4,3},{5,4},{6,5},{7,6},{8,7},{9,8},{10,9},{11,1... | collective-permute-start | bytes 393224 | tf_op jit(solution)/shard_map/ppermute | solution.py:338
  16.7 0.0 copy-done.1
  16.7 0.0 copy-done
  16.8 0.1 shard_map.60
  16.9 0.1 collective-permute-done.from_left_ref
  16.9 1.0 %collective-permute-done.1.from_right_ref = f32[32,8,128]{2,1,0:T(8,128)S(1)} collective-permute-done((f32[32,8,128]{2,1,0:T(8,128)}, f32[32,8,128]{2,1,0:T(8,128)S(1)}, u32[]{:S(2)}, u32[]{:S(2)}) %collective-permute-start.1) | collective-permute-done | bytes 131104 | tf_op jit(solution)/shard_map/ppermute | solution.py:338
  17.9 4.0 %collective-permute-start.2 = (f32[2,4,40,128]{3,2,1,0:T(8,128)S(1)}, f32[2,4,40,128]{3,2,1,0:T(8,128)S(1)}, u32[]{:S(2)}, u32[]{:S(2)}) collective-permute-start(f32[2,4,40,128]{3,2,1,0:T(8,128)S(1)} %get-tuple-element.42), channel_id=1, source_target_pairs={{0,32},{32,64},{64,96},{96,128},{128,160},{160,192},{192,224},{224... | collective-permute-start | bytes 491528 | tf_op jit(solution)/shard_map/ppermute | solution.py:338
  21.9 0.0 collective-permute-start.3
  21.9 1.8 %shard_map.61 = (f32[32,48,128]{2,1,0:T(8,128)S(1)}, f32[32,48,128]{2,1,0:T(8,128)S(1)}, f32[32,48,128]{2,1,0:T(8,128)S(1)}, f32[2,3,2,48,128]{4,3,2,1,0:T(8,128)S(1)}, f32[2,32,128]{2,1,0:T(8,128)S(1)}) custom-call(f32[32,32,128]{2,1,0:T(8,128)S(1)} %copy-done, f32[32,32,128]{2,1,0:T(8,128)S(1)} %copy-done.1, f32[32,32,128]{2,1,0:T(8,128)S(1)} %get-tuple-element.33.w_ref, ...), custom_call_target="tpu_custom_call" | custom-call | flops 8388608 | bytes 5373952 | tf_op jit(solution)/shard_map/pallas_call | solution.py:323
  23.7 0.5 collective-permute-done.2.above_ref
  24.1 3.7 %collective-permute-done.3.below_ref = f32[2,4,40,128]{3,2,1,0:T(8,128)S(1)} collective-permute-done((f32[2,4,40,128]{3,2,1,0:T(8,128)S(1)}, f32[2,4,40,128]{3,2,1,0:T(8,128)S(1)}, u32[]{:S(2)}, u32[]{:S(2)}) %collective-permute-start.3) | collective-permute-done | bytes 163872 | tf_op jit(solution)/shard_map/ppermute | solution.py:338
  27.8 0.8 %shard_map.63 = (f32[2,3,48,128]{3,2,1,0:T(8,128)S(1)}, f32[2,2,4,48,128]{4,3,2,1,0:T(8,128)S(1)}, f32[17,8,128]{2,1,0:T(8,128)S(1)}, f32[17,8,128]{2,1,0:T(8,128)S(1)}, f32[8,128]{1,0:T(8,128)S(1)}) custom-call(f32[32,32,128]{2,1,0:T(8,128)S(1)} %copy-done, f32[32,32,128]{2,1,0:T(8,128)S(1)} %copy-done.1, ...), custom_call_target="tpu_custom_call" | custom-call | bytes 1368064 | tf_op jit(solution)/shard_map/pallas_call | solution.py:323
  28.6 1.9 %collective-permute-start.6 = (f32[17,8,128]{2,1,0:T(8,128)S(1)}, f32[17,8,128]{2,1,0:T(8,128)S(1)}, u32[]{:S(2)}, u32[]{:S(2)}) collective-permute-start(f32[17,8,128]{2,1,0:T(8,128)S(1)} %get-tuple-element.47), channel_id=1, source_target_pairs={{0,1},{1,2},{2,3},{3,4},{4,5},{5,6},{6,7},{7,8},{8,9},{9,10},{10,1... | collective-permute-start | bytes 208904 | tf_op jit(solution)/shard_map/ppermute | solution.py:338
  30.5 6.1 %collective-permute-start.7 = (f32[17,8,128]{2,1,0:T(8,128)S(1)}, f32[17,8,128]{2,1,0:T(8,128)S(1)}, u32[]{:S(2)}, u32[]{:S(2)}) collective-permute-start(f32[17,8,128]{2,1,0:T(8,128)S(1)} %get-tuple-element.48), channel_id=1, source_target_pairs={{1,0},{2,1},{3,2},{4,3},{5,4},{6,5},{7,6},{8,7},{9,8},{10,9},{11,1... | collective-permute-start | bytes 208904 | tf_op jit(solution)/shard_map/ppermute | solution.py:338
  36.7 3.1 %collective-permute-start.5 = (f32[8,128]{1,0:T(8,128)S(1)}, f32[8,128]{1,0:T(8,128)S(1)}, u32[]{:S(2)}, u32[]{:S(2)}) collective-permute-start(f32[8,128]{1,0:T(8,128)S(1)} %get-tuple-element.46.coarse_ref), channel_id=1, source_target_pairs={{2,0},{3,1},{4,2},{5,3},{6,4},{7,5},{8,6},{9,7},{10,8},{11,9},{12,... | collective-permute-start | bytes 12296 | tf_op jit(solution)/shard_map/ppermute | solution.py:338
  39.8 3.1 %collective-permute-start.4 = (f32[8,128]{1,0:T(8,128)S(1)}, f32[8,128]{1,0:T(8,128)S(1)}, u32[]{:S(2)}, u32[]{:S(2)}) collective-permute-start(f32[8,128]{1,0:T(8,128)S(1)} %get-tuple-element.46.coarse_ref), channel_id=1, source_target_pairs={{0,2},{1,3},{2,4},{3,5},{4,6},{5,7},{6,8},{7,9},{8,10},{9,11},{10,... | collective-permute-start | bytes 12296 | tf_op jit(solution)/shard_map/ppermute | solution.py:338
  42.9 0.0 collective-permute-done.5.far_right_ref
  42.9 4.3 %collective-permute-done.4.far_left_ref = f32[8,128]{1,0:T(8,128)S(1)} collective-permute-done((f32[8,128]{1,0:T(8,128)S(1)}, f32[8,128]{1,0:T(8,128)S(1)}, u32[]{:S(2)}, u32[]{:S(2)}) %collective-permute-start.4) | collective-permute-done | bytes 4128 | tf_op jit(solution)/shard_map/ppermute | solution.py:338
  47.1 0.0 collective-permute-done.6.from_left_ref
  47.1 0.0 collective-permute-done.7.from_right_ref
  47.1 0.3 shard_map.64
  47.5 1.7 %collective-permute-start.8 = (f32[5,40,128]{2,1,0:T(8,128)S(1)}, f32[5,40,128]{2,1,0:T(8,128)S(1)}, u32[]{:S(2)}, u32[]{:S(2)}) collective-permute-start(f32[5,40,128]{2,1,0:T(8,128)S(1)} %get-tuple-element.52), channel_id=1, source_target_pairs={{0,32},{32,64},{64,96},{96,128},{128,160},{160,192},{192,224},{224... | collective-permute-start | bytes 307208 | tf_op jit(solution)/shard_map/ppermute | solution.py:338
  49.2 0.0 collective-permute-start.9
  49.2 2.9 %shard_map.65 = (f32[2,4,2,48,128]{4,3,2,1,0:T(8,128)S(1)}, f32[32,32,128]{2,1,0:T(8,128)}, f32[32,32,128]{2,1,0:T(8,128)}) custom-call(f32[32,32,128]{2,1,0:T(8,128)S(1)} %copy-done, f32[32,32,128]{2,1,0:T(8,128)S(1)} %copy-done.1, f32[32,48,128]{2,1,0:T(8,128)S(1)} %get-tuple-element.49.v_in_ref.v_ref, f32[32,48,128]{2,1,0:T(8,128)S(1)} %get-tuple-element.38.ww_ref, ...), custom_call_target="tpu_custom_call" | custom-call | flops 8388608 | bytes 2883584 | tf_op jit(solution)/shard_map/pallas_call | solution.py:323
  52.1 0.0 collective-permute-done.8.above_ref
  52.1 2.4 %collective-permute-done.9.below_ref = f32[5,40,128]{2,1,0:T(8,128)S(1)} collective-permute-done((f32[5,40,128]{2,1,0:T(8,128)S(1)}, f32[5,40,128]{2,1,0:T(8,128)S(1)}, u32[]{:S(2)}, u32[]{:S(2)}) %collective-permute-start.9) | collective-permute-done | bytes 102432 | tf_op jit(solution)/shard_map/ppermute | solution.py:338
  54.5 1.6 %shard_map.66 = (f32[32,32,128]{2,1,0:T(8,128)}, f32[32,32,128]{2,1,0:T(8,128)}) custom-call(f32[32,32,128]{2,1,0:T(8,128)S(1)} %copy-done, f32[32,32,128]{2,1,0:T(8,128)S(1)} %copy-done.1, f32[32,48,128]{2,1,0:T(8,128)S(1)} %get-tuple-element.49.v_in_ref.v_ref, ...), custom_call_target="tpu_custom_call", output_to_operand_aliasing={{0}: (9, {}), {1}: (10, {})} | custom-call | bytes 2097152 | tf_op jit(solution)/shard_map/pallas_call | solution.py:323
  (1 shorter events, 0.0 us)
Async XLA Ops:
  0.6 16.1 %copy-start.1 = (f32[32,32,128]{2,1,0:T(8,128)S(1)}, f32[32,32,128]{2,1,0:T(8,128)}, u32[]{:S(2)}) copy-start(f32[32,32,128]{2,1,0:T(8,128)} %s_ref.6) | copy-start | bytes 1572868
  0.6 16.1 %copy-start = (f32[32,32,128]{2,1,0:T(8,128)S(1)}, f32[32,32,128]{2,1,0:T(8,128)}, u32[]{:S(2)}) copy-start(f32[32,32,128]{2,1,0:T(8,128)} %b_ref.6) | copy-start | bytes 1572868
  2.6 14.4 %collective-permute-start = (f32[32,8,128]{2,1,0:T(8,128)}, f32[32,8,128]{2,1,0:T(8,128)S(1)}, u32[]{:S(2)}, u32[]{:S(2)}) collective-permute-start(f32[32,8,128]{2,1,0:T(8,128)} %get-tuple-element.35), channel_id=1, source_target_pairs={{0,1},{1,2},{2,3},{3,4},{4,5},{5,6},{6,7},{7,8},{8,9},{9,10},{10,1... | collective-permute-start | bytes 393224 | tf_op jit(solution)/shard_map/ppermute | solution.py:338
  6.6 11.3 %collective-permute-start.1 = (f32[32,8,128]{2,1,0:T(8,128)}, f32[32,8,128]{2,1,0:T(8,128)S(1)}, u32[]{:S(2)}, u32[]{:S(2)}) collective-permute-start(f32[32,8,128]{2,1,0:T(8,128)} %get-tuple-element.36), channel_id=1, source_target_pairs={{1,0},{2,1},{3,2},{4,3},{5,4},{6,5},{7,6},{8,7},{9,8},{10,9},{11,1... | collective-permute-start | bytes 393224 | tf_op jit(solution)/shard_map/ppermute | solution.py:338
  17.9 6.2 %collective-permute-start.2 = (f32[2,4,40,128]{3,2,1,0:T(8,128)S(1)}, f32[2,4,40,128]{3,2,1,0:T(8,128)S(1)}, u32[]{:S(2)}, u32[]{:S(2)}) collective-permute-start(f32[2,4,40,128]{3,2,1,0:T(8,128)S(1)} %get-tuple-element.42), channel_id=1, source_target_pairs={{0,32},{32,64},{64,96},{96,128},{128,160},{160,192},{192,224},{224... | collective-permute-start | bytes 491528 | tf_op jit(solution)/shard_map/ppermute | solution.py:338
  21.9 6.0 %collective-permute-start.3 = (f32[2,4,40,128]{3,2,1,0:T(8,128)S(1)}, f32[2,4,40,128]{3,2,1,0:T(8,128)S(1)}, u32[]{:S(2)}, u32[]{:S(2)}) collective-permute-start(f32[2,4,40,128]{3,2,1,0:T(8,128)S(1)} %get-tuple-element.43), channel_id=1, source_target_pairs={{0,480},{32,0},{64,32},{96,64},{128,96},{160,128},{192,160},{224,1... | collective-permute-start | bytes 491528 | tf_op jit(solution)/shard_map/ppermute | solution.py:338
  28.6 18.5 %collective-permute-start.6 = (f32[17,8,128]{2,1,0:T(8,128)S(1)}, f32[17,8,128]{2,1,0:T(8,128)S(1)}, u32[]{:S(2)}, u32[]{:S(2)}) collective-permute-start(f32[17,8,128]{2,1,0:T(8,128)S(1)} %get-tuple-element.47), channel_id=1, source_target_pairs={{0,1},{1,2},{2,3},{3,4},{4,5},{5,6},{6,7},{7,8},{8,9},{9,10},{10,1... | collective-permute-start | bytes 208904 | tf_op jit(solution)/shard_map/ppermute | solution.py:338
  30.5 16.6 %collective-permute-start.7 = (f32[17,8,128]{2,1,0:T(8,128)S(1)}, f32[17,8,128]{2,1,0:T(8,128)S(1)}, u32[]{:S(2)}, u32[]{:S(2)}) collective-permute-start(f32[17,8,128]{2,1,0:T(8,128)S(1)} %get-tuple-element.48), channel_id=1, source_target_pairs={{1,0},{2,1},{3,2},{4,3},{5,4},{6,5},{7,6},{8,7},{9,8},{10,9},{11,1... | collective-permute-start | bytes 208904 | tf_op jit(solution)/shard_map/ppermute | solution.py:338
  36.7 6.2 %collective-permute-start.5 = (f32[8,128]{1,0:T(8,128)S(1)}, f32[8,128]{1,0:T(8,128)S(1)}, u32[]{:S(2)}, u32[]{:S(2)}) collective-permute-start(f32[8,128]{1,0:T(8,128)S(1)} %get-tuple-element.46.coarse_ref), channel_id=1, source_target_pairs={{2,0},{3,1},{4,2},{5,3},{6,4},{7,5},{8,6},{9,7},{10,8},{11,9},{12,... | collective-permute-start | bytes 12296 | tf_op jit(solution)/shard_map/ppermute | solution.py:338
  39.8 7.4 %collective-permute-start.4 = (f32[8,128]{1,0:T(8,128)S(1)}, f32[8,128]{1,0:T(8,128)S(1)}, u32[]{:S(2)}, u32[]{:S(2)}) collective-permute-start(f32[8,128]{1,0:T(8,128)S(1)} %get-tuple-element.46.coarse_ref), channel_id=1, source_target_pairs={{0,2},{1,3},{2,4},{3,5},{4,6},{5,7},{6,8},{7,9},{8,10},{9,11},{10,... | collective-permute-start | bytes 12296 | tf_op jit(solution)/shard_map/ppermute | solution.py:338
  47.5 4.6 %collective-permute-start.8 = (f32[5,40,128]{2,1,0:T(8,128)S(1)}, f32[5,40,128]{2,1,0:T(8,128)S(1)}, u32[]{:S(2)}, u32[]{:S(2)}) collective-permute-start(f32[5,40,128]{2,1,0:T(8,128)S(1)} %get-tuple-element.52), channel_id=1, source_target_pairs={{0,32},{32,64},{64,96},{96,128},{128,160},{160,192},{192,224},{224... | collective-permute-start | bytes 307208 | tf_op jit(solution)/shard_map/ppermute | solution.py:338
  49.2 5.3 %collective-permute-start.9 = (f32[5,40,128]{2,1,0:T(8,128)S(1)}, f32[5,40,128]{2,1,0:T(8,128)S(1)}, u32[]{:S(2)}, u32[]{:S(2)}) collective-permute-start(f32[5,40,128]{2,1,0:T(8,128)S(1)} %get-tuple-element.53), channel_id=1, source_target_pairs={{0,480},{32,0},{64,32},{96,64},{128,96},{160,128},{192,160},{224,1... | collective-permute-start | bytes 307208 | tf_op jit(solution)/shard_map/ppermute | solution.py:338

commit v4 on v3

--- a/solution.py
+++ b/solution.py
@@ -136,7 +136,7 @@
 
 
 def first_outer_kernel(
-    b_ref, s_ref, v_ref, ww_ref, wwb_ref, saved_ref, partial_ref, above_ref, below_ref, info_ref,
+    b_ref, s_ref, v_ref, ww_ref, wwb_ref, saved_ref, partial_ref, below_ref, above_ref, info_ref,
     ends_ref, halo_ref, right_ref, left_ref, coarse_ref,
 ):
     span, cross = lax.axis_index("span"), lax.axis_index("cross")
@@ -191,7 +191,7 @@
 
 
 def correct_kernel(
-    inner_ref, ends_ref, coarse_ref, far_left_ref, far_right_ref, from_left_ref, from_right_ref, v_ref, down_ref, up_ref, e_ref
+    inner_ref, ends_ref, coarse_ref, far_right_ref, far_left_ref, from_left_ref, from_right_ref, v_ref, down_ref, up_ref, e_ref
 ):
     cross, n_cross = lax.axis_index("cross"), lax.axis_size("cross")
     has_left, has_right = cross > 0, cross < n_cross - 1
@@ -275,7 +275,7 @@
 
 
 def second_outer_kernel(
-    b_ref, s_ref, v_ref, ww_ref, wwb_ref, halo_ref, saved_ref, above_ref, below_ref, pressure_in, residual_in,
+    b_ref, s_ref, v_ref, ww_ref, wwb_ref, halo_ref, saved_ref, below_ref, above_ref, pressure_in, residual_in,
     pressure_hbm, residual_hbm, pressure_ref, residual_ref, sems,
 ):
     span = lax.axis_index("span")
@@ -364,7 +364,7 @@
     ends, halo, right, left, coarse = call(
         first_outer_kernel,
         [(2, 3, WIDE, LANES), (2, 2, HALO, WIDE, LANES), (17, 8, LANES), (17, 8, LANES), (8, LANES)],
-        [b, s, v, ww, wwb, saved, partial, above, below, info],
+        [b, s, v, ww, wwb, saved, partial, below, above, info],
     )
     far_left = shifted(coarse, "cross", 2)
     far_right = shifted(coarse, "cross", -2)
@@ -374,7 +374,7 @@
     v, down, up = call(
         correct_kernel,
         [wide, rows, rows],
-        [v, ends, coarse, far_left, far_right, from_left, from_right],
+        [v, ends, coarse, far_right, far_left, from_left, from_right],
         scratch=[(4, 8, LANES)],
     )
     above = shifted(down, "span", 1)
@@ -391,7 +391,7 @@
         call(
             second_outer_kernel,
             [block, block],
-            [b, s, v, ww, wwb, halo, saved, above, below, pressure, residual],
+            [b, s, v, ww, wwb, halo, saved, below, above, pressure, residual],
             scratch=[(2, 4, N, LANES), (2, 5, N, LANES), sems((4,))],
             ins=[VMEM] * 9 + [HBM] * 2,
             out_specs=[HBM, HBM],

time: 56.3 us -> 53.6 us (0.952)
  the two profiles are of different devices: /device:TPU:31 before, /device:TPU:6 now
where the time goes in v4:
time: 53.6 us; the launch traced here: 53.3 us
  starting transfers between devices  32.9 us (61%)
  Pallas kernels  9.39 us (18%)
  waiting for transfers between devices  8.99 us (17%)
  between operations  2.07 us (4%)
    ppermute x10, starting transfers between devices, shifted(): lax.ppermute(block, axis, [p for p in pairs if axis == 'span' or p[1] - p...  32.9 us
    pallas_call x8, Pallas kernels, call(): pl.pallas_call(kernel, out_shape=[jax.ShapeDtypeStruct(s, F32) for s in o...  9.39 us
    ppermute x10, waiting for transfers between devices, shifted(): lax.ppermute(block, axis, [p for p in pairs if axis == 'span' or p[1] - p...  8.99 us
  transfers between devices with their start and end apart: 10, of which 6 were waited for; matrix products, arithmetic and copies ran while one was open for 0% of the time, Pallas kernels for 9%

profile of v4, /device:TPU:6, one launch (start us, length us, event | category | flops | bytes accessed | tf_op | source)
XLA Modules:
  0.0 53.3 jit_solution(5660647614077078014)
XLA Ops:
  0.6 0.0 copy-start.1
  0.6 0.0 copy-start
  0.6 1.9 %shard_map.59 = (f32[32,8,128]{2,1,0:T(8,128)}, f32[32,8,128]{2,1,0:T(8,128)}) custom-call(f32[32,32,128]{2,1,0:T(8,128)} %b_ref.6, f32[32,32,128]{2,1,0:T(8,128)} %s_ref.6), custom_call_target="tpu_custom_call" | custom-call | bytes 524288 | tf_op jit(solution)/shard_map/pallas_call | solution.py:323
  2.6 4.3 %collective-permute-start = (f32[32,8,128]{2,1,0:T(8,128)}, f32[32,8,128]{2,1,0:T(8,128)S(1)}, u32[]{:S(2)}, u32[]{:S(2)}) collective-permute-start(f32[32,8,128]{2,1,0:T(8,128)} %get-tuple-element.35), channel_id=1, source_target_pairs={{0,1},{1,2},{2,3},{3,4},{4,5},{5,6},{6,7},{7,8},{8,9},{9,10},{10,1... | collective-permute-start | bytes 393224 | tf_op jit(solution)/shard_map/ppermute | solution.py:338
  6.9 8.9 %collective-permute-start.1 = (f32[32,8,128]{2,1,0:T(8,128)}, f32[32,8,128]{2,1,0:T(8,128)S(1)}, u32[]{:S(2)}, u32[]{:S(2)}) collective-permute-start(f32[32,8,128]{2,1,0:T(8,128)} %get-tuple-element.36), channel_id=1, source_target_pairs={{1,0},{2,1},{3,2},{4,3},{5,4},{6,5},{7,6},{8,7},{9,8},{10,9},{11,1... | collective-permute-start | bytes 393224 | tf_op jit(solution)/shard_map/ppermute | solution.py:338
  17.0 0.0 copy-done.1
  17.0 0.0 copy-done
  17.0 0.1 shard_map.60
  17.1 0.4 collective-permute-done.from_left_ref
  17.5 1.3 %collective-permute-done.1.from_right_ref = f32[32,8,128]{2,1,0:T(8,128)S(1)} collective-permute-done((f32[32,8,128]{2,1,0:T(8,128)}, f32[32,8,128]{2,1,0:T(8,128)S(1)}, u32[]{:S(2)}, u32[]{:S(2)}) %collective-permute-start.1) | collective-permute-done | bytes 131104 | tf_op jit(solution)/shard_map/ppermute | solution.py:338
  18.8 2.0 %collective-permute-start.2 = (f32[2,4,40,128]{3,2,1,0:T(8,128)S(1)}, f32[2,4,40,128]{3,2,1,0:T(8,128)S(1)}, u32[]{:S(2)}, u32[]{:S(2)}) collective-permute-start(f32[2,4,40,128]{3,2,1,0:T(8,128)S(1)} %get-tuple-element.42), channel_id=1, source_target_pairs={{0,480},{32,0},{64,32},{96,64},{128,96},{160,128},{192,160},{224,1... | collective-permute-start | bytes 491528 | tf_op jit(solution)/shard_map/ppermute | solution.py:338
  20.9 0.0 collective-permute-start.3
  20.9 1.8 %shard_map.61 = (f32[32,48,128]{2,1,0:T(8,128)S(1)}, f32[32,48,128]{2,1,0:T(8,128)S(1)}, f32[32,48,128]{2,1,0:T(8,128)S(1)}, f32[2,3,2,48,128]{4,3,2,1,0:T(8,128)S(1)}, f32[2,32,128]{2,1,0:T(8,128)S(1)}) custom-call(f32[32,32,128]{2,1,0:T(8,128)S(1)} %copy-done, f32[32,32,128]{2,1,0:T(8,128)S(1)} %copy-done.1, f32[32,32,128]{2,1,0:T(8,128)S(1)} %get-tuple-element.33.w_ref, ...), custom_call_target="tpu_custom_call" | custom-call | flops 8388608 | bytes 5373952 | tf_op jit(solution)/shard_map/pallas_call | solution.py:323
  22.7 1.0 %collective-permute-done.2.below_ref = f32[2,4,40,128]{3,2,1,0:T(8,128)S(1)} collective-permute-done((f32[2,4,40,128]{3,2,1,0:T(8,128)S(1)}, f32[2,4,40,128]{3,2,1,0:T(8,128)S(1)}, u32[]{:S(2)}, u32[]{:S(2)}) %collective-permute-start.2) | collective-permute-done | bytes 163872 | tf_op jit(solution)/shard_map/ppermute | solution.py:338
  23.7 3.1 %collective-permute-done.3.above_ref = f32[2,4,40,128]{3,2,1,0:T(8,128)S(1)} collective-permute-done((f32[2,4,40,128]{3,2,1,0:T(8,128)S(1)}, f32[2,4,40,128]{3,2,1,0:T(8,128)S(1)}, u32[]{:S(2)}, u32[]{:S(2)}) %collective-permute-start.3) | collective-permute-done | bytes 163872 | tf_op jit(solution)/shard_map/ppermute | solution.py:338
  26.8 0.8 %shard_map.63 = (f32[2,3,48,128]{3,2,1,0:T(8,128)S(1)}, f32[2,2,4,48,128]{4,3,2,1,0:T(8,128)S(1)}, f32[17,8,128]{2,1,0:T(8,128)S(1)}, f32[17,8,128]{2,1,0:T(8,128)S(1)}, f32[8,128]{1,0:T(8,128)S(1)}) custom-call(f32[32,32,128]{2,1,0:T(8,128)S(1)} %copy-done, f32[32,32,128]{2,1,0:T(8,128)S(1)} %copy-done.1, ...), custom_call_target="tpu_custom_call" | custom-call | bytes 1368064 | tf_op jit(solution)/shard_map/pallas_call | solution.py:323
  27.6 1.9 %collective-permute-start.6 = (f32[17,8,128]{2,1,0:T(8,128)S(1)}, f32[17,8,128]{2,1,0:T(8,128)S(1)}, u32[]{:S(2)}, u32[]{:S(2)}) collective-permute-start(f32[17,8,128]{2,1,0:T(8,128)S(1)} %get-tuple-element.47), channel_id=1, source_target_pairs={{0,1},{1,2},{2,3},{3,4},{4,5},{5,6},{6,7},{7,8},{8,9},{9,10},{10,1... | collective-permute-start | bytes 208904 | tf_op jit(solution)/shard_map/ppermute | solution.py:338
  29.5 6.4 %collective-permute-start.7 = (f32[17,8,128]{2,1,0:T(8,128)S(1)}, f32[17,8,128]{2,1,0:T(8,128)S(1)}, u32[]{:S(2)}, u32[]{:S(2)}) collective-permute-start(f32[17,8,128]{2,1,0:T(8,128)S(1)} %get-tuple-element.48), channel_id=1, source_target_pairs={{1,0},{2,1},{3,2},{4,3},{5,4},{6,5},{7,6},{8,7},{9,8},{10,9},{11,1... | collective-permute-start | bytes 208904 | tf_op jit(solution)/shard_map/ppermute | solution.py:338
  35.9 1.9 %collective-permute-start.5 = (f32[8,128]{1,0:T(8,128)S(1)}, f32[8,128]{1,0:T(8,128)S(1)}, u32[]{:S(2)}, u32[]{:S(2)}) collective-permute-start(f32[8,128]{1,0:T(8,128)S(1)} %get-tuple-element.46.coarse_ref), channel_id=1, source_target_pairs={{0,2},{1,3},{2,4},{3,5},{4,6},{5,7},{6,8},{7,9},{8,10},{9,11},{10,... | collective-permute-start | bytes 12296 | tf_op jit(solution)/shard_map/ppermute | solution.py:338
  37.8 6.9 %collective-permute-start.4 = (f32[8,128]{1,0:T(8,128)S(1)}, f32[8,128]{1,0:T(8,128)S(1)}, u32[]{:S(2)}, u32[]{:S(2)}) collective-permute-start(f32[8,128]{1,0:T(8,128)S(1)} %get-tuple-element.46.coarse_ref), channel_id=1, source_target_pairs={{2,0},{3,1},{4,2},{5,3},{6,4},{7,5},{8,6},{9,7},{10,8},{11,9},{12,... | collective-permute-start | bytes 12296 | tf_op jit(solution)/shard_map/ppermute | solution.py:338
  44.8 0.0 collective-permute-done.5.far_left_ref
  44.8 1.3 %collective-permute-done.4.far_right_ref = f32[8,128]{1,0:T(8,128)S(1)} collective-permute-done((f32[8,128]{1,0:T(8,128)S(1)}, f32[8,128]{1,0:T(8,128)S(1)}, u32[]{:S(2)}, u32[]{:S(2)}) %collective-permute-start.4) | collective-permute-done | bytes 4128 | tf_op jit(solution)/shard_map/ppermute | solution.py:338
  46.1 0.0 collective-permute-done.6.from_left_ref
  46.1 0.0 collective-permute-done.7.from_right_ref
  46.1 0.3 shard_map.64
  46.4 0.0 collective-permute-start.8
  46.5 0.5 collective-permute-start.9
  46.9 2.9 %shard_map.65 = (f32[2,4,2,48,128]{4,3,2,1,0:T(8,128)S(1)}, f32[32,32,128]{2,1,0:T(8,128)}, f32[32,32,128]{2,1,0:T(8,128)}) custom-call(f32[32,32,128]{2,1,0:T(8,128)S(1)} %copy-done, f32[32,32,128]{2,1,0:T(8,128)S(1)} %copy-done.1, f32[32,48,128]{2,1,0:T(8,128)S(1)} %get-tuple-element.49.v_in_ref.v_ref, f32[32,48,128]{2,1,0:T(8,128)S(1)} %get-tuple-element.38.ww_ref, ...), custom_call_target="tpu_custom_call" | custom-call | flops 8388608 | bytes 2883584 | tf_op jit(solution)/shard_map/pallas_call | solution.py:323
  49.8 0.0 collective-permute-done.8.below_ref
  49.9 1.9 %collective-permute-done.9.above_ref = f32[5,40,128]{2,1,0:T(8,128)S(1)} collective-permute-done((f32[5,40,128]{2,1,0:T(8,128)S(1)}, f32[5,40,128]{2,1,0:T(8,128)S(1)}, u32[]{:S(2)}, u32[]{:S(2)}) %collective-permute-start.9) | collective-permute-done | bytes 102432 | tf_op jit(solution)/shard_map/ppermute | solution.py:338
  51.8 1.6 %shard_map.66 = (f32[32,32,128]{2,1,0:T(8,128)}, f32[32,32,128]{2,1,0:T(8,128)}) custom-call(f32[32,32,128]{2,1,0:T(8,128)S(1)} %copy-done, f32[32,32,128]{2,1,0:T(8,128)S(1)} %copy-done.1, f32[32,48,128]{2,1,0:T(8,128)S(1)} %get-tuple-element.49.v_in_ref.v_ref, ...), custom_call_target="tpu_custom_call", output_to_operand_aliasing={{0}: (9, {}), {1}: (10, {})} | custom-call | bytes 2097152 | tf_op jit(solution)/shard_map/pallas_call | solution.py:323
  (1 shorter events, 0.0 us)
Async XLA Ops:
  0.6 16.4 %copy-start.1 = (f32[32,32,128]{2,1,0:T(8,128)S(1)}, f32[32,32,128]{2,1,0:T(8,128)}, u32[]{:S(2)}) copy-start(f32[32,32,128]{2,1,0:T(8,128)} %s_ref.6) | copy-start | bytes 1572868
  0.6 16.4 %copy-start = (f32[32,32,128]{2,1,0:T(8,128)S(1)}, f32[32,32,128]{2,1,0:T(8,128)}, u32[]{:S(2)}) copy-start(f32[32,32,128]{2,1,0:T(8,128)} %b_ref.6) | copy-start | bytes 1572868
  2.6 14.9 %collective-permute-start = (f32[32,8,128]{2,1,0:T(8,128)}, f32[32,8,128]{2,1,0:T(8,128)S(1)}, u32[]{:S(2)}, u32[]{:S(2)}) collective-permute-start(f32[32,8,128]{2,1,0:T(8,128)} %get-tuple-element.35), channel_id=1, source_target_pairs={{0,1},{1,2},{2,3},{3,4},{4,5},{5,6},{6,7},{7,8},{8,9},{9,10},{10,1... | collective-permute-start | bytes 393224 | tf_op jit(solution)/shard_map/ppermute | solution.py:338
  6.9 11.9 %collective-permute-start.1 = (f32[32,8,128]{2,1,0:T(8,128)}, f32[32,8,128]{2,1,0:T(8,128)S(1)}, u32[]{:S(2)}, u32[]{:S(2)}) collective-permute-start(f32[32,8,128]{2,1,0:T(8,128)} %get-tuple-element.36), channel_id=1, source_target_pairs={{1,0},{2,1},{3,2},{4,3},{5,4},{6,5},{7,6},{8,7},{9,8},{10,9},{11,1... | collective-permute-start | bytes 393224 | tf_op jit(solution)/shard_map/ppermute | solution.py:338
  18.8 4.9 %collective-permute-start.2 = (f32[2,4,40,128]{3,2,1,0:T(8,128)S(1)}, f32[2,4,40,128]{3,2,1,0:T(8,128)S(1)}, u32[]{:S(2)}, u32[]{:S(2)}) collective-permute-start(f32[2,4,40,128]{3,2,1,0:T(8,128)S(1)} %get-tuple-element.42), channel_id=1, source_target_pairs={{0,480},{32,0},{64,32},{96,64},{128,96},{160,128},{192,160},{224,1... | collective-permute-start | bytes 491528 | tf_op jit(solution)/shard_map/ppermute | solution.py:338
  20.9 6.0 %collective-permute-start.3 = (f32[2,4,40,128]{3,2,1,0:T(8,128)S(1)}, f32[2,4,40,128]{3,2,1,0:T(8,128)S(1)}, u32[]{:S(2)}, u32[]{:S(2)}) collective-permute-start(f32[2,4,40,128]{3,2,1,0:T(8,128)S(1)} %get-tuple-element.43), channel_id=1, source_target_pairs={{0,32},{32,64},{64,96},{96,128},{128,160},{160,192},{192,224},{224... | collective-permute-start | bytes 491528 | tf_op jit(solution)/shard_map/ppermute | solution.py:338
  27.6 18.5 %collective-permute-start.6 = (f32[17,8,128]{2,1,0:T(8,128)S(1)}, f32[17,8,128]{2,1,0:T(8,128)S(1)}, u32[]{:S(2)}, u32[]{:S(2)}) collective-permute-start(f32[17,8,128]{2,1,0:T(8,128)S(1)} %get-tuple-element.47), channel_id=1, source_target_pairs={{0,1},{1,2},{2,3},{3,4},{4,5},{5,6},{6,7},{7,8},{8,9},{9,10},{10,1... | collective-permute-start | bytes 208904 | tf_op jit(solution)/shard_map/ppermute | solution.py:338
  29.5 16.6 %collective-permute-start.7 = (f32[17,8,128]{2,1,0:T(8,128)S(1)}, f32[17,8,128]{2,1,0:T(8,128)S(1)}, u32[]{:S(2)}, u32[]{:S(2)}) collective-permute-start(f32[17,8,128]{2,1,0:T(8,128)S(1)} %get-tuple-element.48), channel_id=1, source_target_pairs={{1,0},{2,1},{3,2},{4,3},{5,4},{6,5},{7,6},{8,7},{9,8},{10,9},{11,1... | collective-permute-start | bytes 208904 | tf_op jit(solution)/shard_map/ppermute | solution.py:338
  35.9 8.9 %collective-permute-start.5 = (f32[8,128]{1,0:T(8,128)S(1)}, f32[8,128]{1,0:T(8,128)S(1)}, u32[]{:S(2)}, u32[]{:S(2)}) collective-permute-start(f32[8,128]{1,0:T(8,128)S(1)} %get-tuple-element.46.coarse_ref), channel_id=1, source_target_pairs={{0,2},{1,3},{2,4},{3,5},{4,6},{5,7},{6,8},{7,9},{8,10},{9,11},{10,... | collective-permute-start | bytes 12296 | tf_op jit(solution)/shard_map/ppermute | solution.py:338
  37.8 8.2 %collective-permute-start.4 = (f32[8,128]{1,0:T(8,128)S(1)}, f32[8,128]{1,0:T(8,128)S(1)}, u32[]{:S(2)}, u32[]{:S(2)}) collective-permute-start(f32[8,128]{1,0:T(8,128)S(1)} %get-tuple-element.46.coarse_ref), channel_id=1, source_target_pairs={{2,0},{3,1},{4,2},{5,3},{6,4},{7,5},{8,6},{9,7},{10,8},{11,9},{12,... | collective-permute-start | bytes 12296 | tf_op jit(solution)/shard_map/ppermute | solution.py:338
  46.4 3.4 %collective-permute-start.8 = (f32[5,40,128]{2,1,0:T(8,128)S(1)}, f32[5,40,128]{2,1,0:T(8,128)S(1)}, u32[]{:S(2)}, u32[]{:S(2)}) collective-permute-start(f32[5,40,128]{2,1,0:T(8,128)S(1)} %get-tuple-element.52), channel_id=1, source_target_pairs={{0,480},{32,0},{64,32},{96,64},{128,96},{160,128},{192,160},{224,1... | collective-permute-start | bytes 307208 | tf_op jit(solution)/shard_map/ppermute | solution.py:338
  46.5 5.3 %collective-permute-start.9 = (f32[5,40,128]{2,1,0:T(8,128)S(1)}, f32[5,40,128]{2,1,0:T(8,128)S(1)}, u32[]{:S(2)}, u32[]{:S(2)}) collective-permute-start(f32[5,40,128]{2,1,0:T(8,128)S(1)} %get-tuple-element.53), channel_id=1, source_target_pairs={{0,32},{32,64},{64,96},{96,128},{128,160},{160,192},{192,224},{224... | collective-permute-start | bytes 307208 | tf_op jit(solution)/shard_map/ppermute | solution.py:338

commit v5 on v4

--- a/solution.py
+++ b/solution.py
@@ -51,12 +51,15 @@
     lax.fori_loop(0, count, one, 0)
 
 
-def outer_sweeps(rows, first, count, side, coefficients, saved_ref):
+def outer_sweeps(ends, count, coefficients, saved_ref):
     for step in range(count):
-        new = [swept(*rows[i : i + 3], *coefficients(first + 1 + i)) for i in range(len(rows) - 2)]
-        saved = [saved_ref[side, step, k] for k in range(2)]
-        rows, first = (new + saved, first + 1) if side == 0 else (saved + new, first - 1)
-    return rows, first
+        later = []
+        for side, (rows, first) in enumerate(ends):
+            new = [swept(*rows[i : i + 3], *coefficients(first + 1 + i)) for i in range(len(rows) - 2)]
+            saved = [saved_ref[side, step, k] for k in range(2)]
+            later.append((new + saved, first + 1) if side == 0 else (saved + new, first - 1))
+        ends = later
+    return ends
 
 
 def fine_residual(prev, cur, nxt, b, s):
@@ -66,9 +69,9 @@
 
 def edges_kernel(b_ref, s_ref, right_ref, left_ref, b_left, b_right, s_left, s_right, sems):
     copies = [
-        pltpu.make_async_copy(source.at[:, pl.ds(start, 8), :], target, sems.at[n])
+        pltpu.make_async_copy(source.at[:, pl.ds(start, 4), :], target.at[:, pl.ds(start % 8, 4), :], sems.at[n])
         for n, (source, start, target) in enumerate(
-            ((s_ref, N - 8, s_right), (b_ref, N - 8, b_right), (s_ref, 0, s_left), (b_ref, 0, b_left))
+            ((s_ref, N - 4, s_right), (b_ref, N - 4, b_right), (s_ref, 0, s_left), (b_ref, 0, b_left))
         )
     ]
     for copy in copies:
@@ -158,11 +161,13 @@
         return halo_ref[side, 0, k], halo_ref[side, 1, k]
 
     tile = info_ref[...]
-    for side in range(2):
-        start = -HALO if side == 0 else N - 2
-        rows, start = outer_sweeps(
-            [coefficients(r)[1] for r in range(start, start + HALO + 2)], start, 3, side, coefficients, saved_ref
-        )
+    ends = outer_sweeps(
+        [([coefficients(r)[1] for r in range(start, start + HALO + 2)], start) for start in (-HALO, N - 2)],
+        3,
+        coefficients,
+        saved_ref,
+    )
+    for side, (rows, start) in enumerate(ends):
         total = partial_ref[side]
         for i in range(1, 5):
             r = start + i
@@ -265,13 +270,19 @@
         v_ref.at[pl.ds(low, high - low), pl.ds(8, N), :], pressure_hbm.at[pl.ds(low, high - low)], sems.at[0]
     )
     first.start()
-    low, high = 5, N - 5
-    for r in range(low, high):
-        residual_ref[r - low] = fine_residual(v_ref[r - 1], v_ref[r], v_ref[r + 1], b_ref[r], s_ref[r])
-    second = pltpu.make_async_copy(residual_ref, residual_hbm.at[pl.ds(low, high - low)], sems.at[1])
-    second.start()
-    first.wait()
-    second.wait()
+    low = 5
+    copies = [first]
+    for place, count in ((5, 14), (19, 8)):
+        for r in range(place, place + count):
+            residual_ref[r - low] = fine_residual(v_ref[r - 1], v_ref[r], v_ref[r + 1], b_ref[r], s_ref[r])
+        copies.append(
+            pltpu.make_async_copy(
+                residual_ref.at[pl.ds(place - low, count)], residual_hbm.at[pl.ds(place, count)], sems.at[len(copies)]
+            )
+        )
+        copies[-1].start()
+    for copy in copies:
+        copy.wait()
 
 
 def second_outer_kernel(
@@ -288,7 +299,7 @@
         side, k = (0, r + HALO) if r < 0 else (1, r - N)
         return halo_ref[side, 0, k], halo_ref[side, 1, k]
 
-    copies = []
+    copies, ends = [], []
     for side, source in enumerate((above_ref, below_ref)):
         outside = []
         for k in range(REACH):
@@ -296,16 +307,16 @@
             left = jnp.where((sub >= 4) & inside[side], beside, 0.0)
             right = jnp.where((sub < 4) & inside[side], beside, 0.0)
             outside.append(jnp.concatenate([left, jnp.where(inside[side], source[k, 0:N], 0.0), right], axis=0))
-        if side == 0:
-            rows, start = outside + [v_ref[0], v_ref[1]], -REACH
-        else:
-            rows, start = [v_ref[N - 2], v_ref[N - 1]] + outside, N - 2
-        rows, start = outer_sweeps(rows, start, 4, side, coefficients, saved_ref)
+        ends.append((outside + [v_ref[0], v_ref[1]], -REACH) if side == 0 else ([v_ref[N - 2], v_ref[N - 1]] + outside, N - 2))
+    ends = outer_sweeps(ends, 4, coefficients, saved_ref)
+    for side, (rows, start) in enumerate(ends):
         for k in range(4):
             pressure_ref[side, k] = rows[k + 1 + side][8 : 8 + N]
+    for side, (rows, start) in enumerate(ends):
         for i in range(1, 6):
             r = start + i
             residual_ref[side, i - 1] = fine_residual(*rows[i - 1 : i + 2], b_ref[r], s_ref[r])
+    for side in range(2):
         for ref, hbm, count in ((pressure_ref, pressure_hbm, 4), (residual_ref, residual_hbm, 5)):
             place = pl.ds(0 if side == 0 else N - count, count)
             copies.append(pltpu.make_async_copy(ref.at[side], hbm.at[place], sems.at[len(copies)]))
@@ -383,7 +394,7 @@
         second_inner_kernel,
         [(2, 4, 2, WIDE, LANES), block, block],
         [b, s, v, ww, wwb],
-        scratch=[wide, (N - 10, N, LANES), sems((2,))],
+        scratch=[wide, (N - 10, N, LANES), sems((3,))],
         out_specs=[VMEM, HBM, HBM],
         ops=2**23,
     )

time: 53.6 us -> 53.3 us (level)
  no operation moved by 1% of the time
where the time goes in v5:
time: 53.3 us; the launch traced here: 53 us
  starting transfers between devices  32.9 us (62%)
  waiting for transfers between devices  9.06 us (17%)
  Pallas kernels  9 us (17%)
  between operations  2.07 us (4%)
    ppermute x10, starting transfers between devices, shifted(): lax.ppermute(block, axis, [p for p in pairs if axis == 'span' or p[1] - p...  32.9 us
    ppermute x10, waiting for transfers between devices, shifted(): lax.ppermute(block, axis, [p for p in pairs if axis == 'span' or p[1] - p...  9.06 us
    pallas_call x8, Pallas kernels, call(): pl.pallas_call(kernel, out_shape=[jax.ShapeDtypeStruct(s, F32) for s in o...  9 us
  transfers between devices with their start and end apart: 10, of which 6 were waited for; matrix products, arithmetic and copies ran while one was open for 0% of the time, Pallas kernels for 9%

profile of v5, /device:TPU:6, one launch (start us, length us, event | category | flops | bytes accessed | tf_op | source)
XLA Modules:
  0.0 53.0 jit_solution(16821179320972444170)
XLA Ops:
  0.6 0.0 copy-start.1
  0.6 0.0 copy-start
  0.6 1.8 %shard_map.59 = (f32[32,8,128]{2,1,0:T(8,128)}, f32[32,8,128]{2,1,0:T(8,128)}) custom-call(f32[32,32,128]{2,1,0:T(8,128)} %b_ref.6, f32[32,32,128]{2,1,0:T(8,128)} %s_ref.6), custom_call_target="tpu_custom_call" | custom-call | bytes 524288 | tf_op jit(solution)/shard_map/pallas_call | solution.py:334
  2.4 4.3 %collective-permute-start = (f32[32,8,128]{2,1,0:T(8,128)}, f32[32,8,128]{2,1,0:T(8,128)S(1)}, u32[]{:S(2)}, u32[]{:S(2)}) collective-permute-start(f32[32,8,128]{2,1,0:T(8,128)} %get-tuple-element.35), channel_id=1, source_target_pairs={{0,1},{1,2},{2,3},{3,4},{4,5},{5,6},{6,7},{7,8},{8,9},{9,10},{10,1... | collective-permute-start | bytes 393224 | tf_op jit(solution)/shard_map/ppermute | solution.py:349
  6.7 8.9 %collective-permute-start.1 = (f32[32,8,128]{2,1,0:T(8,128)}, f32[32,8,128]{2,1,0:T(8,128)S(1)}, u32[]{:S(2)}, u32[]{:S(2)}) collective-permute-start(f32[32,8,128]{2,1,0:T(8,128)} %get-tuple-element.36), channel_id=1, source_target_pairs={{1,0},{2,1},{3,2},{4,3},{5,4},{6,5},{7,6},{8,7},{9,8},{10,9},{11,1... | collective-permute-start | bytes 393224 | tf_op jit(solution)/shard_map/ppermute | solution.py:349
  16.9 0.0 copy-done.1
  16.9 0.0 copy-done
  16.9 0.1 shard_map.60
  17.0 0.4 collective-permute-done.from_left_ref
  17.3 1.3 %collective-permute-done.1.from_right_ref = f32[32,8,128]{2,1,0:T(8,128)S(1)} collective-permute-done((f32[32,8,128]{2,1,0:T(8,128)}, f32[32,8,128]{2,1,0:T(8,128)S(1)}, u32[]{:S(2)}, u32[]{:S(2)}) %collective-permute-start.1) | collective-permute-done | bytes 131104 | tf_op jit(solution)/shard_map/ppermute | solution.py:349
  18.6 2.0 %collective-permute-start.2 = (f32[2,4,40,128]{3,2,1,0:T(8,128)S(1)}, f32[2,4,40,128]{3,2,1,0:T(8,128)S(1)}, u32[]{:S(2)}, u32[]{:S(2)}) collective-permute-start(f32[2,4,40,128]{3,2,1,0:T(8,128)S(1)} %get-tuple-element.42), channel_id=1, source_target_pairs={{0,480},{32,0},{64,32},{96,64},{128,96},{160,128},{192,160},{224,1... | collective-permute-start | bytes 491528 | tf_op jit(solution)/shard_map/ppermute | solution.py:349
  20.7 0.0 collective-permute-start.3
  20.7 1.8 %shard_map.61 = (f32[32,48,128]{2,1,0:T(8,128)S(1)}, f32[32,48,128]{2,1,0:T(8,128)S(1)}, f32[32,48,128]{2,1,0:T(8,128)S(1)}, f32[2,3,2,48,128]{4,3,2,1,0:T(8,128)S(1)}, f32[2,32,128]{2,1,0:T(8,128)S(1)}) custom-call(f32[32,32,128]{2,1,0:T(8,128)S(1)} %copy-done, f32[32,32,128]{2,1,0:T(8,128)S(1)} %copy-done.1, f32[32,32,128]{2,1,0:T(8,128)S(1)} %get-tuple-element.33.w_ref, ...), custom_call_target="tpu_custom_call" | custom-call | flops 8388608 | bytes 5373952 | tf_op jit(solution)/shard_map/pallas_call | solution.py:334
  22.5 1.0 %collective-permute-done.2.below_ref = f32[2,4,40,128]{3,2,1,0:T(8,128)S(1)} collective-permute-done((f32[2,4,40,128]{3,2,1,0:T(8,128)S(1)}, f32[2,4,40,128]{3,2,1,0:T(8,128)S(1)}, u32[]{:S(2)}, u32[]{:S(2)}) %collective-permute-start.2) | collective-permute-done | bytes 163872 | tf_op jit(solution)/shard_map/ppermute | solution.py:349
  23.5 3.1 %collective-permute-done.3.above_ref = f32[2,4,40,128]{3,2,1,0:T(8,128)S(1)} collective-permute-done((f32[2,4,40,128]{3,2,1,0:T(8,128)S(1)}, f32[2,4,40,128]{3,2,1,0:T(8,128)S(1)}, u32[]{:S(2)}, u32[]{:S(2)}) %collective-permute-start.3) | collective-permute-done | bytes 163872 | tf_op jit(solution)/shard_map/ppermute | solution.py:349
  26.6 0.8 %shard_map.63 = (f32[2,3,48,128]{3,2,1,0:T(8,128)S(1)}, f32[2,2,4,48,128]{4,3,2,1,0:T(8,128)S(1)}, f32[17,8,128]{2,1,0:T(8,128)S(1)}, f32[17,8,128]{2,1,0:T(8,128)S(1)}, f32[8,128]{1,0:T(8,128)S(1)}) custom-call(f32[32,32,128]{2,1,0:T(8,128)S(1)} %copy-done, f32[32,32,128]{2,1,0:T(8,128)S(1)} %copy-done.1, ...), custom_call_target="tpu_custom_call" | custom-call | bytes 1368064 | tf_op jit(solution)/shard_map/pallas_call | solution.py:334
  27.4 1.9 %collective-permute-start.6 = (f32[17,8,128]{2,1,0:T(8,128)S(1)}, f32[17,8,128]{2,1,0:T(8,128)S(1)}, u32[]{:S(2)}, u32[]{:S(2)}) collective-permute-start(f32[17,8,128]{2,1,0:T(8,128)S(1)} %get-tuple-element.47), channel_id=1, source_target_pairs={{0,1},{1,2},{2,3},{3,4},{4,5},{5,6},{6,7},{7,8},{8,9},{9,10},{10,1... | collective-permute-start | bytes 208904 | tf_op jit(solution)/shard_map/ppermute | solution.py:349
  29.4 6.4 %collective-permute-start.7 = (f32[17,8,128]{2,1,0:T(8,128)S(1)}, f32[17,8,128]{2,1,0:T(8,128)S(1)}, u32[]{:S(2)}, u32[]{:S(2)}) collective-permute-start(f32[17,8,128]{2,1,0:T(8,128)S(1)} %get-tuple-element.48), channel_id=1, source_target_pairs={{1,0},{2,1},{3,2},{4,3},{5,4},{6,5},{7,6},{8,7},{9,8},{10,9},{11,1... | collective-permute-start | bytes 208904 | tf_op jit(solution)/shard_map/ppermute | solution.py:349
  35.8 1.9 %collective-permute-start.5 = (f32[8,128]{1,0:T(8,128)S(1)}, f32[8,128]{1,0:T(8,128)S(1)}, u32[]{:S(2)}, u32[]{:S(2)}) collective-permute-start(f32[8,128]{1,0:T(8,128)S(1)} %get-tuple-element.46.coarse_ref), channel_id=1, source_target_pairs={{0,2},{1,3},{2,4},{3,5},{4,6},{5,7},{6,8},{7,9},{8,10},{9,11},{10,... | collective-permute-start | bytes 12296 | tf_op jit(solution)/shard_map/ppermute | solution.py:349
  37.7 6.9 %collective-permute-start.4 = (f32[8,128]{1,0:T(8,128)S(1)}, f32[8,128]{1,0:T(8,128)S(1)}, u32[]{:S(2)}, u32[]{:S(2)}) collective-permute-start(f32[8,128]{1,0:T(8,128)S(1)} %get-tuple-element.46.coarse_ref), channel_id=1, source_target_pairs={{2,0},{3,1},{4,2},{5,3},{6,4},{7,5},{8,6},{9,7},{10,8},{11,9},{12,... | collective-permute-start | bytes 12296 | tf_op jit(solution)/shard_map/ppermute | solution.py:349
  44.6 0.0 collective-permute-done.5.far_left_ref
  44.6 1.3 %collective-permute-done.4.far_right_ref = f32[8,128]{1,0:T(8,128)S(1)} collective-permute-done((f32[8,128]{1,0:T(8,128)S(1)}, f32[8,128]{1,0:T(8,128)S(1)}, u32[]{:S(2)}, u32[]{:S(2)}) %collective-permute-start.4) | collective-permute-done | bytes 4128 | tf_op jit(solution)/shard_map/ppermute | solution.py:349
  45.9 0.0 collective-permute-done.6.from_left_ref
  45.9 0.0 collective-permute-done.7.from_right_ref
  45.9 0.3 shard_map.64
  46.3 0.0 collective-permute-start.8
  46.3 0.5 collective-permute-start.9
  46.8 2.8 %shard_map.65 = (f32[2,4,2,48,128]{4,3,2,1,0:T(8,128)S(1)}, f32[32,32,128]{2,1,0:T(8,128)}, f32[32,32,128]{2,1,0:T(8,128)}) custom-call(f32[32,32,128]{2,1,0:T(8,128)S(1)} %copy-done, f32[32,32,128]{2,1,0:T(8,128)S(1)} %copy-done.1, f32[32,48,128]{2,1,0:T(8,128)S(1)} %get-tuple-element.49.v_in_ref.v_ref, f32[32,48,128]{2,1,0:T(8,128)S(1)} %get-tuple-element.38.ww_ref, ...), custom_call_target="tpu_custom_call" | custom-call | flops 8388608 | bytes 2883584 | tf_op jit(solution)/shard_map/pallas_call | solution.py:334
  49.6 0.0 collective-permute-done.8.below_ref
  49.6 2.0 %collective-permute-done.9.above_ref = f32[5,40,128]{2,1,0:T(8,128)S(1)} collective-permute-done((f32[5,40,128]{2,1,0:T(8,128)S(1)}, f32[5,40,128]{2,1,0:T(8,128)S(1)}, u32[]{:S(2)}, u32[]{:S(2)}) %collective-permute-start.9) | collective-permute-done | bytes 102432 | tf_op jit(solution)/shard_map/ppermute | solution.py:349
  51.6 1.4 %shard_map.66 = (f32[32,32,128]{2,1,0:T(8,128)}, f32[32,32,128]{2,1,0:T(8,128)}) custom-call(f32[32,32,128]{2,1,0:T(8,128)S(1)} %copy-done, f32[32,32,128]{2,1,0:T(8,128)S(1)} %copy-done.1, f32[32,48,128]{2,1,0:T(8,128)S(1)} %get-tuple-element.49.v_in_ref.v_ref, ...), custom_call_target="tpu_custom_call", output_to_operand_aliasing={{0}: (9, {}), {1}: (10, {})} | custom-call | bytes 2097152 | tf_op jit(solution)/shard_map/pallas_call | solution.py:334
  (1 shorter events, 0.0 us)
Async XLA Ops:
  0.6 16.2 %copy-start.1 = (f32[32,32,128]{2,1,0:T(8,128)S(1)}, f32[32,32,128]{2,1,0:T(8,128)}, u32[]{:S(2)}) copy-start(f32[32,32,128]{2,1,0:T(8,128)} %s_ref.6) | copy-start | bytes 1572868
  0.6 16.2 %copy-start = (f32[32,32,128]{2,1,0:T(8,128)S(1)}, f32[32,32,128]{2,1,0:T(8,128)}, u32[]{:S(2)}) copy-start(f32[32,32,128]{2,1,0:T(8,128)} %b_ref.6) | copy-start | bytes 1572868
  2.4 14.9 %collective-permute-start = (f32[32,8,128]{2,1,0:T(8,128)}, f32[32,8,128]{2,1,0:T(8,128)S(1)}, u32[]{:S(2)}, u32[]{:S(2)}) collective-permute-start(f32[32,8,128]{2,1,0:T(8,128)} %get-tuple-element.35), channel_id=1, source_target_pairs={{0,1},{1,2},{2,3},{3,4},{4,5},{5,6},{6,7},{7,8},{8,9},{9,10},{10,1... | collective-permute-start | bytes 393224 | tf_op jit(solution)/shard_map/ppermute | solution.py:349
  6.7 11.9 %collective-permute-start.1 = (f32[32,8,128]{2,1,0:T(8,128)}, f32[32,8,128]{2,1,0:T(8,128)S(1)}, u32[]{:S(2)}, u32[]{:S(2)}) collective-permute-start(f32[32,8,128]{2,1,0:T(8,128)} %get-tuple-element.36), channel_id=1, source_target_pairs={{1,0},{2,1},{3,2},{4,3},{5,4},{6,5},{7,6},{8,7},{9,8},{10,9},{11,1... | collective-permute-start | bytes 393224 | tf_op jit(solution)/shard_map/ppermute | solution.py:349
  18.6 4.9 %collective-permute-start.2 = (f32[2,4,40,128]{3,2,1,0:T(8,128)S(1)}, f32[2,4,40,128]{3,2,1,0:T(8,128)S(1)}, u32[]{:S(2)}, u32[]{:S(2)}) collective-permute-start(f32[2,4,40,128]{3,2,1,0:T(8,128)S(1)} %get-tuple-element.42), channel_id=1, source_target_pairs={{0,480},{32,0},{64,32},{96,64},{128,96},{160,128},{192,160},{224,1... | collective-permute-start | bytes 491528 | tf_op jit(solution)/shard_map/ppermute | solution.py:349
  20.7 6.0 %collective-permute-start.3 = (f32[2,4,40,128]{3,2,1,0:T(8,128)S(1)}, f32[2,4,40,128]{3,2,1,0:T(8,128)S(1)}, u32[]{:S(2)}, u32[]{:S(2)}) collective-permute-start(f32[2,4,40,128]{3,2,1,0:T(8,128)S(1)} %get-tuple-element.43), channel_id=1, source_target_pairs={{0,32},{32,64},{64,96},{96,128},{128,160},{160,192},{192,224},{224... | collective-permute-start | bytes 491528 | tf_op jit(solution)/shard_map/ppermute | solution.py:349
  27.4 18.5 %collective-permute-start.6 = (f32[17,8,128]{2,1,0:T(8,128)S(1)}, f32[17,8,128]{2,1,0:T(8,128)S(1)}, u32[]{:S(2)}, u32[]{:S(2)}) collective-permute-start(f32[17,8,128]{2,1,0:T(8,128)S(1)} %get-tuple-element.47), channel_id=1, source_target_pairs={{0,1},{1,2},{2,3},{3,4},{4,5},{5,6},{6,7},{7,8},{8,9},{9,10},{10,1... | collective-permute-start | bytes 208904 | tf_op jit(solution)/shard_map/ppermute | solution.py:349
  29.4 16.6 %collective-permute-start.7 = (f32[17,8,128]{2,1,0:T(8,128)S(1)}, f32[17,8,128]{2,1,0:T(8,128)S(1)}, u32[]{:S(2)}, u32[]{:S(2)}) collective-permute-start(f32[17,8,128]{2,1,0:T(8,128)S(1)} %get-tuple-element.48), channel_id=1, source_target_pairs={{1,0},{2,1},{3,2},{4,3},{5,4},{6,5},{7,6},{8,7},{9,8},{10,9},{11,1... | collective-permute-start | bytes 208904 | tf_op jit(solution)/shard_map/ppermute | solution.py:349
  35.8 8.9 %collective-permute-start.5 = (f32[8,128]{1,0:T(8,128)S(1)}, f32[8,128]{1,0:T(8,128)S(1)}, u32[]{:S(2)}, u32[]{:S(2)}) collective-permute-start(f32[8,128]{1,0:T(8,128)S(1)} %get-tuple-element.46.coarse_ref), channel_id=1, source_target_pairs={{0,2},{1,3},{2,4},{3,5},{4,6},{5,7},{6,8},{7,9},{8,10},{9,11},{10,... | collective-permute-start | bytes 12296 | tf_op jit(solution)/shard_map/ppermute | solution.py:349
  37.7 8.2 %collective-permute-start.4 = (f32[8,128]{1,0:T(8,128)S(1)}, f32[8,128]{1,0:T(8,128)S(1)}, u32[]{:S(2)}, u32[]{:S(2)}) collective-permute-start(f32[8,128]{1,0:T(8,128)S(1)} %get-tuple-element.46.coarse_ref), channel_id=1, source_target_pairs={{2,0},{3,1},{4,2},{5,3},{6,4},{7,5},{8,6},{9,7},{10,8},{11,9},{12,... | collective-permute-start | bytes 12296 | tf_op jit(solution)/shard_map/ppermute | solution.py:349
  46.3 3.4 %collective-permute-start.8 = (f32[5,40,128]{2,1,0:T(8,128)S(1)}, f32[5,40,128]{2,1,0:T(8,128)S(1)}, u32[]{:S(2)}, u32[]{:S(2)}) collective-permute-start(f32[5,40,128]{2,1,0:T(8,128)S(1)} %get-tuple-element.52), channel_id=1, source_target_pairs={{0,480},{32,0},{64,32},{96,64},{128,96},{160,128},{192,160},{224,1... | collective-permute-start | bytes 307208 | tf_op jit(solution)/shard_map/ppermute | solution.py:349
  46.3 5.3 %collective-permute-start.9 = (f32[5,40,128]{2,1,0:T(8,128)S(1)}, f32[5,40,128]{2,1,0:T(8,128)S(1)}, u32[]{:S(2)}, u32[]{:S(2)}) collective-permute-start(f32[5,40,128]{2,1,0:T(8,128)S(1)} %get-tuple-element.53), channel_id=1, source_target_pairs={{0,32},{32,64},{64,96},{96,128},{128,160},{160,192},{192,224},{224... | collective-permute-start | bytes 307208 | tf_op jit(solution)/shard_map/ppermute | solution.py:349

commit v6 on v5

--- a/solution.py
+++ b/solution.py
@@ -309,18 +309,21 @@
             outside.append(jnp.concatenate([left, jnp.where(inside[side], source[k, 0:N], 0.0), right], axis=0))
         ends.append((outside + [v_ref[0], v_ref[1]], -REACH) if side == 0 else ([v_ref[N - 2], v_ref[N - 1]] + outside, N - 2))
     ends = outer_sweeps(ends, 4, coefficients, saved_ref)
+    def send(ref, hbm, count):
+        for side in range(2):
+            place = pl.ds(0 if side == 0 else N - count, count)
+            copies.append(pltpu.make_async_copy(ref.at[side], hbm.at[place], sems.at[len(copies)]))
+            copies[-1].start()
+
     for side, (rows, start) in enumerate(ends):
         for k in range(4):
             pressure_ref[side, k] = rows[k + 1 + side][8 : 8 + N]
+    send(pressure_ref, pressure_hbm, 4)
     for side, (rows, start) in enumerate(ends):
         for i in range(1, 6):
             r = start + i
             residual_ref[side, i - 1] = fine_residual(*rows[i - 1 : i + 2], b_ref[r], s_ref[r])
-    for side in range(2):
-        for ref, hbm, count in ((pressure_ref, pressure_hbm, 4), (residual_ref, residual_hbm, 5)):
-            place = pl.ds(0 if side == 0 else N - count, count)
-            copies.append(pltpu.make_async_copy(ref.at[side], hbm.at[place], sems.at[len(copies)]))
-            copies[-1].start()
+    send(residual_ref, residual_hbm, 5)
     for copy in copies:
         copy.wait()
 

time: 53.3 us -> 53.3 us (level)
  no operation moved by 1% of the time
where the time goes in v6:
time: 53.3 us; the launch traced here: 53 us
  starting transfers between devices  32.9 us (62%)
  waiting for transfers between devices  9.06 us (17%)
  Pallas kernels  8.98 us (17%)
  between operations  2.07 us (4%)
    ppermute x10, starting transfers between devices, shifted(): lax.ppermute(block, axis, [p for p in pairs if axis == 'span' or p[1] - p...  32.9 us
    ppermute x10, waiting for transfers between devices, shifted(): lax.ppermute(block, axis, [p for p in pairs if axis == 'span' or p[1] - p...  9.06 us
    pallas_call x8, Pallas kernels, call(): pl.pallas_call(kernel, out_shape=[jax.ShapeDtypeStruct(s, F32) for s in o...  8.98 us
  transfers between devices with their start and end apart: 10, of which 6 were waited for; matrix products, arithmetic and copies ran while one was open for 0% of the time, Pallas kernels for 9%

profile of v6, /device:TPU:6, one launch (start us, length us, event | category | flops | bytes accessed | tf_op | source)
XLA Modules:
  0.0 53.0 jit_solution(8330933980264380924)
XLA Ops:
  0.6 0.0 copy-start.1
  0.6 0.0 copy-start
  0.6 1.8 %shard_map.59 = (f32[32,8,128]{2,1,0:T(8,128)}, f32[32,8,128]{2,1,0:T(8,128)}) custom-call(f32[32,32,128]{2,1,0:T(8,128)} %b_ref.6, f32[32,32,128]{2,1,0:T(8,128)} %s_ref.6), custom_call_target="tpu_custom_call" | custom-call | bytes 524288 | tf_op jit(solution)/shard_map/pallas_call | solution.py:337
  2.4 4.3 %collective-permute-start = (f32[32,8,128]{2,1,0:T(8,128)}, f32[32,8,128]{2,1,0:T(8,128)S(1)}, u32[]{:S(2)}, u32[]{:S(2)}) collective-permute-start(f32[32,8,128]{2,1,0:T(8,128)} %get-tuple-element.35), channel_id=1, source_target_pairs={{0,1},{1,2},{2,3},{3,4},{4,5},{5,6},{6,7},{7,8},{8,9},{9,10},{10,1... | collective-permute-start | bytes 393224 | tf_op jit(solution)/shard_map/ppermute | solution.py:352
  6.7 8.9 %collective-permute-start.1 = (f32[32,8,128]{2,1,0:T(8,128)}, f32[32,8,128]{2,1,0:T(8,128)S(1)}, u32[]{:S(2)}, u32[]{:S(2)}) collective-permute-start(f32[32,8,128]{2,1,0:T(8,128)} %get-tuple-element.36), channel_id=1, source_target_pairs={{1,0},{2,1},{3,2},{4,3},{5,4},{6,5},{7,6},{8,7},{9,8},{10,9},{11,1... | collective-permute-start | bytes 393224 | tf_op jit(solution)/shard_map/ppermute | solution.py:352
  16.9 0.0 copy-done.1
  16.9 0.0 copy-done
  16.9 0.1 shard_map.60
  17.0 0.4 collective-permute-done.from_left_ref
  17.3 1.3 %collective-permute-done.1.from_right_ref = f32[32,8,128]{2,1,0:T(8,128)S(1)} collective-permute-done((f32[32,8,128]{2,1,0:T(8,128)}, f32[32,8,128]{2,1,0:T(8,128)S(1)}, u32[]{:S(2)}, u32[]{:S(2)}) %collective-permute-start.1) | collective-permute-done | bytes 131104 | tf_op jit(solution)/shard_map/ppermute | solution.py:352
  18.6 2.0 %collective-permute-start.2 = (f32[2,4,40,128]{3,2,1,0:T(8,128)S(1)}, f32[2,4,40,128]{3,2,1,0:T(8,128)S(1)}, u32[]{:S(2)}, u32[]{:S(2)}) collective-permute-start(f32[2,4,40,128]{3,2,1,0:T(8,128)S(1)} %get-tuple-element.42), channel_id=1, source_target_pairs={{0,480},{32,0},{64,32},{96,64},{128,96},{160,128},{192,160},{224,1... | collective-permute-start | bytes 491528 | tf_op jit(solution)/shard_map/ppermute | solution.py:352
  20.7 0.0 collective-permute-start.3
  20.7 1.8 %shard_map.61 = (f32[32,48,128]{2,1,0:T(8,128)S(1)}, f32[32,48,128]{2,1,0:T(8,128)S(1)}, f32[32,48,128]{2,1,0:T(8,128)S(1)}, f32[2,3,2,48,128]{4,3,2,1,0:T(8,128)S(1)}, f32[2,32,128]{2,1,0:T(8,128)S(1)}) custom-call(f32[32,32,128]{2,1,0:T(8,128)S(1)} %copy-done, f32[32,32,128]{2,1,0:T(8,128)S(1)} %copy-done.1, f32[32,32,128]{2,1,0:T(8,128)S(1)} %get-tuple-element.33.w_ref, ...), custom_call_target="tpu_custom_call" | custom-call | flops 8388608 | bytes 5373952 | tf_op jit(solution)/shard_map/pallas_call | solution.py:337
  22.5 1.0 %collective-permute-done.2.below_ref = f32[2,4,40,128]{3,2,1,0:T(8,128)S(1)} collective-permute-done((f32[2,4,40,128]{3,2,1,0:T(8,128)S(1)}, f32[2,4,40,128]{3,2,1,0:T(8,128)S(1)}, u32[]{:S(2)}, u32[]{:S(2)}) %collective-permute-start.2) | collective-permute-done | bytes 163872 | tf_op jit(solution)/shard_map/ppermute | solution.py:352
  23.5 3.1 %collective-permute-done.3.above_ref = f32[2,4,40,128]{3,2,1,0:T(8,128)S(1)} collective-permute-done((f32[2,4,40,128]{3,2,1,0:T(8,128)S(1)}, f32[2,4,40,128]{3,2,1,0:T(8,128)S(1)}, u32[]{:S(2)}, u32[]{:S(2)}) %collective-permute-start.3) | collective-permute-done | bytes 163872 | tf_op jit(solution)/shard_map/ppermute | solution.py:352
  26.6 0.8 %shard_map.63 = (f32[2,3,48,128]{3,2,1,0:T(8,128)S(1)}, f32[2,2,4,48,128]{4,3,2,1,0:T(8,128)S(1)}, f32[17,8,128]{2,1,0:T(8,128)S(1)}, f32[17,8,128]{2,1,0:T(8,128)S(1)}, f32[8,128]{1,0:T(8,128)S(1)}) custom-call(f32[32,32,128]{2,1,0:T(8,128)S(1)} %copy-done, f32[32,32,128]{2,1,0:T(8,128)S(1)} %copy-done.1, ...), custom_call_target="tpu_custom_call" | custom-call | bytes 1368064 | tf_op jit(solution)/shard_map/pallas_call | solution.py:337
  27.4 1.9 %collective-permute-start.6 = (f32[17,8,128]{2,1,0:T(8,128)S(1)}, f32[17,8,128]{2,1,0:T(8,128)S(1)}, u32[]{:S(2)}, u32[]{:S(2)}) collective-permute-start(f32[17,8,128]{2,1,0:T(8,128)S(1)} %get-tuple-element.47), channel_id=1, source_target_pairs={{0,1},{1,2},{2,3},{3,4},{4,5},{5,6},{6,7},{7,8},{8,9},{9,10},{10,1... | collective-permute-start | bytes 208904 | tf_op jit(solution)/shard_map/ppermute | solution.py:352
  29.4 6.4 %collective-permute-start.7 = (f32[17,8,128]{2,1,0:T(8,128)S(1)}, f32[17,8,128]{2,1,0:T(8,128)S(1)}, u32[]{:S(2)}, u32[]{:S(2)}) collective-permute-start(f32[17,8,128]{2,1,0:T(8,128)S(1)} %get-tuple-element.48), channel_id=1, source_target_pairs={{1,0},{2,1},{3,2},{4,3},{5,4},{6,5},{7,6},{8,7},{9,8},{10,9},{11,1... | collective-permute-start | bytes 208904 | tf_op jit(solution)/shard_map/ppermute | solution.py:352
  35.8 1.9 %collective-permute-start.5 = (f32[8,128]{1,0:T(8,128)S(1)}, f32[8,128]{1,0:T(8,128)S(1)}, u32[]{:S(2)}, u32[]{:S(2)}) collective-permute-start(f32[8,128]{1,0:T(8,128)S(1)} %get-tuple-element.46.coarse_ref), channel_id=1, source_target_pairs={{0,2},{1,3},{2,4},{3,5},{4,6},{5,7},{6,8},{7,9},{8,10},{9,11},{10,... | collective-permute-start | bytes 12296 | tf_op jit(solution)/shard_map/ppermute | solution.py:352
  37.7 6.9 %collective-permute-start.4 = (f32[8,128]{1,0:T(8,128)S(1)}, f32[8,128]{1,0:T(8,128)S(1)}, u32[]{:S(2)}, u32[]{:S(2)}) collective-permute-start(f32[8,128]{1,0:T(8,128)S(1)} %get-tuple-element.46.coarse_ref), channel_id=1, source_target_pairs={{2,0},{3,1},{4,2},{5,3},{6,4},{7,5},{8,6},{9,7},{10,8},{11,9},{12,... | collective-permute-start | bytes 12296 | tf_op jit(solution)/shard_map/ppermute | solution.py:352
  44.6 0.0 collective-permute-done.5.far_left_ref
  44.6 1.3 %collective-permute-done.4.far_right_ref = f32[8,128]{1,0:T(8,128)S(1)} collective-permute-done((f32[8,128]{1,0:T(8,128)S(1)}, f32[8,128]{1,0:T(8,128)S(1)}, u32[]{:S(2)}, u32[]{:S(2)}) %collective-permute-start.4) | collective-permute-done | bytes 4128 | tf_op jit(solution)/shard_map/ppermute | solution.py:352
  45.9 0.0 collective-permute-done.6.from_left_ref
  45.9 0.0 collective-permute-done.7.from_right_ref
  45.9 0.3 shard_map.64
  46.3 0.0 collective-permute-start.8
  46.3 0.5 collective-permute-start.9
  46.8 2.8 %shard_map.65 = (f32[2,4,2,48,128]{4,3,2,1,0:T(8,128)S(1)}, f32[32,32,128]{2,1,0:T(8,128)}, f32[32,32,128]{2,1,0:T(8,128)}) custom-call(f32[32,32,128]{2,1,0:T(8,128)S(1)} %copy-done, f32[32,32,128]{2,1,0:T(8,128)S(1)} %copy-done.1, f32[32,48,128]{2,1,0:T(8,128)S(1)} %get-tuple-element.49.v_in_ref.v_ref, f32[32,48,128]{2,1,0:T(8,128)S(1)} %get-tuple-element.38.ww_ref, ...), custom_call_target="tpu_custom_call" | custom-call | flops 8388608 | bytes 2883584 | tf_op jit(solution)/shard_map/pallas_call | solution.py:337
  49.6 0.0 collective-permute-done.8.below_ref
  49.6 2.0 %collective-permute-done.9.above_ref = f32[5,40,128]{2,1,0:T(8,128)S(1)} collective-permute-done((f32[5,40,128]{2,1,0:T(8,128)S(1)}, f32[5,40,128]{2,1,0:T(8,128)S(1)}, u32[]{:S(2)}, u32[]{:S(2)}) %collective-permute-start.9) | collective-permute-done | bytes 102432 | tf_op jit(solution)/shard_map/ppermute | solution.py:352
  51.6 1.4 %shard_map.66 = (f32[32,32,128]{2,1,0:T(8,128)}, f32[32,32,128]{2,1,0:T(8,128)}) custom-call(f32[32,32,128]{2,1,0:T(8,128)S(1)} %copy-done, f32[32,32,128]{2,1,0:T(8,128)S(1)} %copy-done.1, f32[32,48,128]{2,1,0:T(8,128)S(1)} %get-tuple-element.49.v_in_ref.v_ref, ...), custom_call_target="tpu_custom_call", output_to_operand_aliasing={{0}: (9, {}), {1}: (10, {})} | custom-call | bytes 2097152 | tf_op jit(solution)/shard_map/pallas_call | solution.py:337
  (1 shorter events, 0.0 us)
Async XLA Ops:
  0.6 16.2 %copy-start.1 = (f32[32,32,128]{2,1,0:T(8,128)S(1)}, f32[32,32,128]{2,1,0:T(8,128)}, u32[]{:S(2)}) copy-start(f32[32,32,128]{2,1,0:T(8,128)} %s_ref.6) | copy-start | bytes 1572868
  0.6 16.2 %copy-start = (f32[32,32,128]{2,1,0:T(8,128)S(1)}, f32[32,32,128]{2,1,0:T(8,128)}, u32[]{:S(2)}) copy-start(f32[32,32,128]{2,1,0:T(8,128)} %b_ref.6) | copy-start | bytes 1572868
  2.4 14.9 %collective-permute-start = (f32[32,8,128]{2,1,0:T(8,128)}, f32[32,8,128]{2,1,0:T(8,128)S(1)}, u32[]{:S(2)}, u32[]{:S(2)}) collective-permute-start(f32[32,8,128]{2,1,0:T(8,128)} %get-tuple-element.35), channel_id=1, source_target_pairs={{0,1},{1,2},{2,3},{3,4},{4,5},{5,6},{6,7},{7,8},{8,9},{9,10},{10,1... | collective-permute-start | bytes 393224 | tf_op jit(solution)/shard_map/ppermute | solution.py:352
  6.7 11.9 %collective-permute-start.1 = (f32[32,8,128]{2,1,0:T(8,128)}, f32[32,8,128]{2,1,0:T(8,128)S(1)}, u32[]{:S(2)}, u32[]{:S(2)}) collective-permute-start(f32[32,8,128]{2,1,0:T(8,128)} %get-tuple-element.36), channel_id=1, source_target_pairs={{1,0},{2,1},{3,2},{4,3},{5,4},{6,5},{7,6},{8,7},{9,8},{10,9},{11,1... | collective-permute-start | bytes 393224 | tf_op jit(solution)/shard_map/ppermute | solution.py:352
  18.6 4.9 %collective-permute-start.2 = (f32[2,4,40,128]{3,2,1,0:T(8,128)S(1)}, f32[2,4,40,128]{3,2,1,0:T(8,128)S(1)}, u32[]{:S(2)}, u32[]{:S(2)}) collective-permute-start(f32[2,4,40,128]{3,2,1,0:T(8,128)S(1)} %get-tuple-element.42), channel_id=1, source_target_pairs={{0,480},{32,0},{64,32},{96,64},{128,96},{160,128},{192,160},{224,1... | collective-permute-start | bytes 491528 | tf_op jit(solution)/shard_map/ppermute | solution.py:352
  20.7 6.0 %collective-permute-start.3 = (f32[2,4,40,128]{3,2,1,0:T(8,128)S(1)}, f32[2,4,40,128]{3,2,1,0:T(8,128)S(1)}, u32[]{:S(2)}, u32[]{:S(2)}) collective-permute-start(f32[2,4,40,128]{3,2,1,0:T(8,128)S(1)} %get-tuple-element.43), channel_id=1, source_target_pairs={{0,32},{32,64},{64,96},{96,128},{128,160},{160,192},{192,224},{224... | collective-permute-start | bytes 491528 | tf_op jit(solution)/shard_map/ppermute | solution.py:352
  27.4 18.5 %collective-permute-start.6 = (f32[17,8,128]{2,1,0:T(8,128)S(1)}, f32[17,8,128]{2,1,0:T(8,128)S(1)}, u32[]{:S(2)}, u32[]{:S(2)}) collective-permute-start(f32[17,8,128]{2,1,0:T(8,128)S(1)} %get-tuple-element.47), channel_id=1, source_target_pairs={{0,1},{1,2},{2,3},{3,4},{4,5},{5,6},{6,7},{7,8},{8,9},{9,10},{10,1... | collective-permute-start | bytes 208904 | tf_op jit(solution)/shard_map/ppermute | solution.py:352
  29.4 16.6 %collective-permute-start.7 = (f32[17,8,128]{2,1,0:T(8,128)S(1)}, f32[17,8,128]{2,1,0:T(8,128)S(1)}, u32[]{:S(2)}, u32[]{:S(2)}) collective-permute-start(f32[17,8,128]{2,1,0:T(8,128)S(1)} %get-tuple-element.48), channel_id=1, source_target_pairs={{1,0},{2,1},{3,2},{4,3},{5,4},{6,5},{7,6},{8,7},{9,8},{10,9},{11,1... | collective-permute-start | bytes 208904 | tf_op jit(solution)/shard_map/ppermute | solution.py:352
  35.8 8.9 %collective-permute-start.5 = (f32[8,128]{1,0:T(8,128)S(1)}, f32[8,128]{1,0:T(8,128)S(1)}, u32[]{:S(2)}, u32[]{:S(2)}) collective-permute-start(f32[8,128]{1,0:T(8,128)S(1)} %get-tuple-element.46.coarse_ref), channel_id=1, source_target_pairs={{0,2},{1,3},{2,4},{3,5},{4,6},{5,7},{6,8},{7,9},{8,10},{9,11},{10,... | collective-permute-start | bytes 12296 | tf_op jit(solution)/shard_map/ppermute | solution.py:352
  37.7 8.2 %collective-permute-start.4 = (f32[8,128]{1,0:T(8,128)S(1)}, f32[8,128]{1,0:T(8,128)S(1)}, u32[]{:S(2)}, u32[]{:S(2)}) collective-permute-start(f32[8,128]{1,0:T(8,128)S(1)} %get-tuple-element.46.coarse_ref), channel_id=1, source_target_pairs={{2,0},{3,1},{4,2},{5,3},{6,4},{7,5},{8,6},{9,7},{10,8},{11,9},{12,... | collective-permute-start | bytes 12296 | tf_op jit(solution)/shard_map/ppermute | solution.py:352
  46.3 3.4 %collective-permute-start.8 = (f32[5,40,128]{2,1,0:T(8,128)S(1)}, f32[5,40,128]{2,1,0:T(8,128)S(1)}, u32[]{:S(2)}, u32[]{:S(2)}) collective-permute-start(f32[5,40,128]{2,1,0:T(8,128)S(1)} %get-tuple-element.52), channel_id=1, source_target_pairs={{0,480},{32,0},{64,32},{96,64},{128,96},{160,128},{192,160},{224,1... | collective-permute-start | bytes 307208 | tf_op jit(solution)/shard_map/ppermute | solution.py:352
  46.3 5.3 %collective-permute-start.9 = (f32[5,40,128]{2,1,0:T(8,128)S(1)}, f32[5,40,128]{2,1,0:T(8,128)S(1)}, u32[]{:S(2)}, u32[]{:S(2)}) collective-permute-start(f32[5,40,128]{2,1,0:T(8,128)S(1)} %get-tuple-element.53), channel_id=1, source_target_pairs={{0,32},{32,64},{64,96},{96,128},{128,160},{160,192},{192,224},{224... | collective-permute-start | bytes 307208 | tf_op jit(solution)/shard_map/ppermute | solution.py:352

commit v7 on v6

--- a/solution.py
+++ b/solution.py
@@ -272,7 +272,7 @@
     first.start()
     low = 5
     copies = [first]
-    for place, count in ((5, 14), (19, 8)):
+    for place, count in ((5, 17), (22, 5)):
         for r in range(place, place + count):
             residual_ref[r - low] = fine_residual(v_ref[r - 1], v_ref[r], v_ref[r + 1], b_ref[r], s_ref[r])
         copies.append(

time: 53.3 us -> 53.3 us (level)
  no operation moved by 1% of the time
where the time goes in v7:
time: 53.3 us; the launch traced here: 53 us
  starting transfers between devices  32.9 us (62%)
  waiting for transfers between devices  9.04 us (17%)
  Pallas kernels  9 us (17%)
  between operations  2.07 us (4%)
    ppermute x10, starting transfers between devices, shifted(): lax.ppermute(block, axis, [p for p in pairs if axis == 'span' or p[1] - p...  32.9 us
    ppermute x10, waiting for transfers between devices, shifted(): lax.ppermute(block, axis, [p for p in pairs if axis == 'span' or p[1] - p...  9.04 us
    pallas_call x8, Pallas kernels, call(): pl.pallas_call(kernel, out_shape=[jax.ShapeDtypeStruct(s, F32) for s in o...  9 us
  transfers between devices with their start and end apart: 10, of which 6 were waited for; matrix products, arithmetic and copies ran while one was open for 0% of the time, Pallas kernels for 9%

profile of v7, /device:TPU:6, one launch (start us, length us, event | category | flops | bytes accessed | tf_op | source)
XLA Modules:
  0.0 53.0 jit_solution(12105221629694193108)
XLA Ops:
  0.6 0.0 copy-start.1
  0.6 0.0 copy-start
  0.6 1.8 %shard_map.59 = (f32[32,8,128]{2,1,0:T(8,128)}, f32[32,8,128]{2,1,0:T(8,128)}) custom-call(f32[32,32,128]{2,1,0:T(8,128)} %b_ref.6, f32[32,32,128]{2,1,0:T(8,128)} %s_ref.6), custom_call_target="tpu_custom_call" | custom-call | bytes 524288 | tf_op jit(solution)/shard_map/pallas_call | solution.py:337
  2.4 4.3 %collective-permute-start = (f32[32,8,128]{2,1,0:T(8,128)}, f32[32,8,128]{2,1,0:T(8,128)S(1)}, u32[]{:S(2)}, u32[]{:S(2)}) collective-permute-start(f32[32,8,128]{2,1,0:T(8,128)} %get-tuple-element.35), channel_id=1, source_target_pairs={{0,1},{1,2},{2,3},{3,4},{4,5},{5,6},{6,7},{7,8},{8,9},{9,10},{10,1... | collective-permute-start | bytes 393224 | tf_op jit(solution)/shard_map/ppermute | solution.py:352
  6.7 8.9 %collective-permute-start.1 = (f32[32,8,128]{2,1,0:T(8,128)}, f32[32,8,128]{2,1,0:T(8,128)S(1)}, u32[]{:S(2)}, u32[]{:S(2)}) collective-permute-start(f32[32,8,128]{2,1,0:T(8,128)} %get-tuple-element.36), channel_id=1, source_target_pairs={{1,0},{2,1},{3,2},{4,3},{5,4},{6,5},{7,6},{8,7},{9,8},{10,9},{11,1... | collective-permute-start | bytes 393224 | tf_op jit(solution)/shard_map/ppermute | solution.py:352
  16.9 0.0 copy-done.1
  16.9 0.0 copy-done
  16.9 0.1 shard_map.60
  17.0 0.4 collective-permute-done.from_left_ref
  17.3 1.3 %collective-permute-done.1.from_right_ref = f32[32,8,128]{2,1,0:T(8,128)S(1)} collective-permute-done((f32[32,8,128]{2,1,0:T(8,128)}, f32[32,8,128]{2,1,0:T(8,128)S(1)}, u32[]{:S(2)}, u32[]{:S(2)}) %collective-permute-start.1) | collective-permute-done | bytes 131104 | tf_op jit(solution)/shard_map/ppermute | solution.py:352
  18.6 2.0 %collective-permute-start.2 = (f32[2,4,40,128]{3,2,1,0:T(8,128)S(1)}, f32[2,4,40,128]{3,2,1,0:T(8,128)S(1)}, u32[]{:S(2)}, u32[]{:S(2)}) collective-permute-start(f32[2,4,40,128]{3,2,1,0:T(8,128)S(1)} %get-tuple-element.42), channel_id=1, source_target_pairs={{0,480},{32,0},{64,32},{96,64},{128,96},{160,128},{192,160},{224,1... | collective-permute-start | bytes 491528 | tf_op jit(solution)/shard_map/ppermute | solution.py:352
  20.7 0.0 collective-permute-start.3
  20.7 1.8 %shard_map.61 = (f32[32,48,128]{2,1,0:T(8,128)S(1)}, f32[32,48,128]{2,1,0:T(8,128)S(1)}, f32[32,48,128]{2,1,0:T(8,128)S(1)}, f32[2,3,2,48,128]{4,3,2,1,0:T(8,128)S(1)}, f32[2,32,128]{2,1,0:T(8,128)S(1)}) custom-call(f32[32,32,128]{2,1,0:T(8,128)S(1)} %copy-done, f32[32,32,128]{2,1,0:T(8,128)S(1)} %copy-done.1, f32[32,32,128]{2,1,0:T(8,128)S(1)} %get-tuple-element.33.w_ref, ...), custom_call_target="tpu_custom_call" | custom-call | flops 8388608 | bytes 5373952 | tf_op jit(solution)/shard_map/pallas_call | solution.py:337
  22.5 1.0 %collective-permute-done.2.below_ref = f32[2,4,40,128]{3,2,1,0:T(8,128)S(1)} collective-permute-done((f32[2,4,40,128]{3,2,1,0:T(8,128)S(1)}, f32[2,4,40,128]{3,2,1,0:T(8,128)S(1)}, u32[]{:S(2)}, u32[]{:S(2)}) %collective-permute-start.2) | collective-permute-done | bytes 163872 | tf_op jit(solution)/shard_map/ppermute | solution.py:352
  23.5 3.1 %collective-permute-done.3.above_ref = f32[2,4,40,128]{3,2,1,0:T(8,128)S(1)} collective-permute-done((f32[2,4,40,128]{3,2,1,0:T(8,128)S(1)}, f32[2,4,40,128]{3,2,1,0:T(8,128)S(1)}, u32[]{:S(2)}, u32[]{:S(2)}) %collective-permute-start.3) | collective-permute-done | bytes 163872 | tf_op jit(solution)/shard_map/ppermute | solution.py:352
  26.6 0.8 %shard_map.63 = (f32[2,3,48,128]{3,2,1,0:T(8,128)S(1)}, f32[2,2,4,48,128]{4,3,2,1,0:T(8,128)S(1)}, f32[17,8,128]{2,1,0:T(8,128)S(1)}, f32[17,8,128]{2,1,0:T(8,128)S(1)}, f32[8,128]{1,0:T(8,128)S(1)}) custom-call(f32[32,32,128]{2,1,0:T(8,128)S(1)} %copy-done, f32[32,32,128]{2,1,0:T(8,128)S(1)} %copy-done.1, ...), custom_call_target="tpu_custom_call" | custom-call | bytes 1368064 | tf_op jit(solution)/shard_map/pallas_call | solution.py:337
  27.4 1.9 %collective-permute-start.6 = (f32[17,8,128]{2,1,0:T(8,128)S(1)}, f32[17,8,128]{2,1,0:T(8,128)S(1)}, u32[]{:S(2)}, u32[]{:S(2)}) collective-permute-start(f32[17,8,128]{2,1,0:T(8,128)S(1)} %get-tuple-element.47), channel_id=1, source_target_pairs={{0,1},{1,2},{2,3},{3,4},{4,5},{5,6},{6,7},{7,8},{8,9},{9,10},{10,1... | collective-permute-start | bytes 208904 | tf_op jit(solution)/shard_map/ppermute | solution.py:352
  29.4 6.4 %collective-permute-start.7 = (f32[17,8,128]{2,1,0:T(8,128)S(1)}, f32[17,8,128]{2,1,0:T(8,128)S(1)}, u32[]{:S(2)}, u32[]{:S(2)}) collective-permute-start(f32[17,8,128]{2,1,0:T(8,128)S(1)} %get-tuple-element.48), channel_id=1, source_target_pairs={{1,0},{2,1},{3,2},{4,3},{5,4},{6,5},{7,6},{8,7},{9,8},{10,9},{11,1... | collective-permute-start | bytes 208904 | tf_op jit(solution)/shard_map/ppermute | solution.py:352
  35.8 1.9 %collective-permute-start.5 = (f32[8,128]{1,0:T(8,128)S(1)}, f32[8,128]{1,0:T(8,128)S(1)}, u32[]{:S(2)}, u32[]{:S(2)}) collective-permute-start(f32[8,128]{1,0:T(8,128)S(1)} %get-tuple-element.46.coarse_ref), channel_id=1, source_target_pairs={{0,2},{1,3},{2,4},{3,5},{4,6},{5,7},{6,8},{7,9},{8,10},{9,11},{10,... | collective-permute-start | bytes 12296 | tf_op jit(solution)/shard_map/ppermute | solution.py:352
  37.7 6.9 %collective-permute-start.4 = (f32[8,128]{1,0:T(8,128)S(1)}, f32[8,128]{1,0:T(8,128)S(1)}, u32[]{:S(2)}, u32[]{:S(2)}) collective-permute-start(f32[8,128]{1,0:T(8,128)S(1)} %get-tuple-element.46.coarse_ref), channel_id=1, source_target_pairs={{2,0},{3,1},{4,2},{5,3},{6,4},{7,5},{8,6},{9,7},{10,8},{11,9},{12,... | collective-permute-start | bytes 12296 | tf_op jit(solution)/shard_map/ppermute | solution.py:352
  44.6 0.0 collective-permute-done.5.far_left_ref
  44.6 1.3 %collective-permute-done.4.far_right_ref = f32[8,128]{1,0:T(8,128)S(1)} collective-permute-done((f32[8,128]{1,0:T(8,128)S(1)}, f32[8,128]{1,0:T(8,128)S(1)}, u32[]{:S(2)}, u32[]{:S(2)}) %collective-permute-start.4) | collective-permute-done | bytes 4128 | tf_op jit(solution)/shard_map/ppermute | solution.py:352
  45.9 0.0 collective-permute-done.6.from_left_ref
  45.9 0.0 collective-permute-done.7.from_right_ref
  45.9 0.3 shard_map.64
  46.3 0.0 collective-permute-start.8
  46.3 0.5 collective-permute-start.9
  46.8 2.9 %shard_map.65 = (f32[2,4,2,48,128]{4,3,2,1,0:T(8,128)S(1)}, f32[32,32,128]{2,1,0:T(8,128)}, f32[32,32,128]{2,1,0:T(8,128)}) custom-call(f32[32,32,128]{2,1,0:T(8,128)S(1)} %copy-done, f32[32,32,128]{2,1,0:T(8,128)S(1)} %copy-done.1, f32[32,48,128]{2,1,0:T(8,128)S(1)} %get-tuple-element.49.v_in_ref.v_ref, f32[32,48,128]{2,1,0:T(8,128)S(1)} %get-tuple-element.38.ww_ref, ...), custom_call_target="tpu_custom_call" | custom-call | flops 8388608 | bytes 2883584 | tf_op jit(solution)/shard_map/pallas_call | solution.py:337
  49.6 0.0 collective-permute-done.8.below_ref
  49.7 1.9 %collective-permute-done.9.above_ref = f32[5,40,128]{2,1,0:T(8,128)S(1)} collective-permute-done((f32[5,40,128]{2,1,0:T(8,128)S(1)}, f32[5,40,128]{2,1,0:T(8,128)S(1)}, u32[]{:S(2)}, u32[]{:S(2)}) %collective-permute-start.9) | collective-permute-done | bytes 102432 | tf_op jit(solution)/shard_map/ppermute | solution.py:352
  51.6 1.4 %shard_map.66 = (f32[32,32,128]{2,1,0:T(8,128)}, f32[32,32,128]{2,1,0:T(8,128)}) custom-call(f32[32,32,128]{2,1,0:T(8,128)S(1)} %copy-done, f32[32,32,128]{2,1,0:T(8,128)S(1)} %copy-done.1, f32[32,48,128]{2,1,0:T(8,128)S(1)} %get-tuple-element.49.v_in_ref.v_ref, ...), custom_call_target="tpu_custom_call", output_to_operand_aliasing={{0}: (9, {}), {1}: (10, {})} | custom-call | bytes 2097152 | tf_op jit(solution)/shard_map/pallas_call | solution.py:337
  (1 shorter events, 0.0 us)
Async XLA Ops:
  0.6 16.2 %copy-start.1 = (f32[32,32,128]{2,1,0:T(8,128)S(1)}, f32[32,32,128]{2,1,0:T(8,128)}, u32[]{:S(2)}) copy-start(f32[32,32,128]{2,1,0:T(8,128)} %s_ref.6) | copy-start | bytes 1572868
  0.6 16.2 %copy-start = (f32[32,32,128]{2,1,0:T(8,128)S(1)}, f32[32,32,128]{2,1,0:T(8,128)}, u32[]{:S(2)}) copy-start(f32[32,32,128]{2,1,0:T(8,128)} %b_ref.6) | copy-start | bytes 1572868
  2.4 14.9 %collective-permute-start = (f32[32,8,128]{2,1,0:T(8,128)}, f32[32,8,128]{2,1,0:T(8,128)S(1)}, u32[]{:S(2)}, u32[]{:S(2)}) collective-permute-start(f32[32,8,128]{2,1,0:T(8,128)} %get-tuple-element.35), channel_id=1, source_target_pairs={{0,1},{1,2},{2,3},{3,4},{4,5},{5,6},{6,7},{7,8},{8,9},{9,10},{10,1... | collective-permute-start | bytes 393224 | tf_op jit(solution)/shard_map/ppermute | solution.py:352
  6.7 11.9 %collective-permute-start.1 = (f32[32,8,128]{2,1,0:T(8,128)}, f32[32,8,128]{2,1,0:T(8,128)S(1)}, u32[]{:S(2)}, u32[]{:S(2)}) collective-permute-start(f32[32,8,128]{2,1,0:T(8,128)} %get-tuple-element.36), channel_id=1, source_target_pairs={{1,0},{2,1},{3,2},{4,3},{5,4},{6,5},{7,6},{8,7},{9,8},{10,9},{11,1... | collective-permute-start | bytes 393224 | tf_op jit(solution)/shard_map/ppermute | solution.py:352
  18.6 4.9 %collective-permute-start.2 = (f32[2,4,40,128]{3,2,1,0:T(8,128)S(1)}, f32[2,4,40,128]{3,2,1,0:T(8,128)S(1)}, u32[]{:S(2)}, u32[]{:S(2)}) collective-permute-start(f32[2,4,40,128]{3,2,1,0:T(8,128)S(1)} %get-tuple-element.42), channel_id=1, source_target_pairs={{0,480},{32,0},{64,32},{96,64},{128,96},{160,128},{192,160},{224,1... | collective-permute-start | bytes 491528 | tf_op jit(solution)/shard_map/ppermute | solution.py:352
  20.7 6.0 %collective-permute-start.3 = (f32[2,4,40,128]{3,2,1,0:T(8,128)S(1)}, f32[2,4,40,128]{3,2,1,0:T(8,128)S(1)}, u32[]{:S(2)}, u32[]{:S(2)}) collective-permute-start(f32[2,4,40,128]{3,2,1,0:T(8,128)S(1)} %get-tuple-element.43), channel_id=1, source_target_pairs={{0,32},{32,64},{64,96},{96,128},{128,160},{160,192},{192,224},{224... | collective-permute-start | bytes 491528 | tf_op jit(solution)/shard_map/ppermute | solution.py:352
  27.4 18.5 %collective-permute-start.6 = (f32[17,8,128]{2,1,0:T(8,128)S(1)}, f32[17,8,128]{2,1,0:T(8,128)S(1)}, u32[]{:S(2)}, u32[]{:S(2)}) collective-permute-start(f32[17,8,128]{2,1,0:T(8,128)S(1)} %get-tuple-element.47), channel_id=1, source_target_pairs={{0,1},{1,2},{2,3},{3,4},{4,5},{5,6},{6,7},{7,8},{8,9},{9,10},{10,1... | collective-permute-start | bytes 208904 | tf_op jit(solution)/shard_map/ppermute | solution.py:352
  29.4 16.6 %collective-permute-start.7 = (f32[17,8,128]{2,1,0:T(8,128)S(1)}, f32[17,8,128]{2,1,0:T(8,128)S(1)}, u32[]{:S(2)}, u32[]{:S(2)}) collective-permute-start(f32[17,8,128]{2,1,0:T(8,128)S(1)} %get-tuple-element.48), channel_id=1, source_target_pairs={{1,0},{2,1},{3,2},{4,3},{5,4},{6,5},{7,6},{8,7},{9,8},{10,9},{11,1... | collective-permute-start | bytes 208904 | tf_op jit(solution)/shard_map/ppermute | solution.py:352
  35.8 8.9 %collective-permute-start.5 = (f32[8,128]{1,0:T(8,128)S(1)}, f32[8,128]{1,0:T(8,128)S(1)}, u32[]{:S(2)}, u32[]{:S(2)}) collective-permute-start(f32[8,128]{1,0:T(8,128)S(1)} %get-tuple-element.46.coarse_ref), channel_id=1, source_target_pairs={{0,2},{1,3},{2,4},{3,5},{4,6},{5,7},{6,8},{7,9},{8,10},{9,11},{10,... | collective-permute-start | bytes 12296 | tf_op jit(solution)/shard_map/ppermute | solution.py:352
  37.7 8.2 %collective-permute-start.4 = (f32[8,128]{1,0:T(8,128)S(1)}, f32[8,128]{1,0:T(8,128)S(1)}, u32[]{:S(2)}, u32[]{:S(2)}) collective-permute-start(f32[8,128]{1,0:T(8,128)S(1)} %get-tuple-element.46.coarse_ref), channel_id=1, source_target_pairs={{2,0},{3,1},{4,2},{5,3},{6,4},{7,5},{8,6},{9,7},{10,8},{11,9},{12,... | collective-permute-start | bytes 12296 | tf_op jit(solution)/shard_map/ppermute | solution.py:352
  46.3 3.4 %collective-permute-start.8 = (f32[5,40,128]{2,1,0:T(8,128)S(1)}, f32[5,40,128]{2,1,0:T(8,128)S(1)}, u32[]{:S(2)}, u32[]{:S(2)}) collective-permute-start(f32[5,40,128]{2,1,0:T(8,128)S(1)} %get-tuple-element.52), channel_id=1, source_target_pairs={{0,480},{32,0},{64,32},{96,64},{128,96},{160,128},{192,160},{224,1... | collective-permute-start | bytes 307208 | tf_op jit(solution)/shard_map/ppermute | solution.py:352
  46.3 5.3 %collective-permute-start.9 = (f32[5,40,128]{2,1,0:T(8,128)S(1)}, f32[5,40,128]{2,1,0:T(8,128)S(1)}, u32[]{:S(2)}, u32[]{:S(2)}) collective-permute-start(f32[5,40,128]{2,1,0:T(8,128)S(1)} %get-tuple-element.53), channel_id=1, source_target_pairs={{0,32},{32,64},{64,96},{96,128},{128,160},{160,192},{192,224},{224... | collective-permute-start | bytes 307208 | tf_op jit(solution)/shard_map/ppermute | solution.py:352
